TPU v7x, 256 devices: a whole 4x4x8 slice. The times are simulated.
256 devices in a mesh: tm: 4 (over x), space: 64 (over z, y, core).
Axes of the slice: x: 4, y: 4, z: 8, core: 2. Of those that a mesh axis runs over, the one named last changes fastest.
Arguments:
- c_points: float32 [4, 8192, 1024], P('tm', 'space'), may hold values from -3 to 3
- source: float32 [8192, 1024], P('space'), may hold values from -2 to 2
Outputs:
- c_new: float32 [4, 8192, 1024], P('tm', 'space')
- fine_end: float32 [4, 8192, 1024], P('tm', 'space')
All inputs are finite; a program needn't handle non-finite values.
Results may differ from a plain program's by a relative error of at most 0.00002.
Values sent between devices are 32-bit elements; how exact they have to be, the bound alone decides.
No kernel may reach another device: no remote copies, remote signals or barrier semaphores. Data moves between devices by JAX's collectives and lax.ppermute only.
A program may use at most 64 MiB of HBM per device.

v0:
```python
import jax
import jax.numpy as jnp
from jax import lax
from jax.sharding import PartitionSpec as P

STEPS_SLAB = 8


ADVECT = 0.02
DIFFUSE = 0.01
FORCE = 0.05


def with_halo(cells, sides, width):
    for axis, dim in sides:
        count = lax.axis_size(axis)
        ends = count - 1
        head = lax.slice_in_dim(cells, 0, width, axis=dim)
        tail = lax.slice_in_dim(cells, cells.shape[dim] - width, cells.shape[dim], axis=dim)
        cells = jnp.concatenate(
            [
                lax.ppermute(tail, axis, [(i, (i + 1) % count) for i in range(ends)]),
                cells,
                lax.ppermute(head, axis, [((i + 1) % count, i) for i in range(ends)]),
            ],
            axis=dim,
        )
    return cells


def from_behind(array, axis, by):
    size = lax.axis_size(axis)
    pairs = [(i, i + by) for i in range(size) if 0 <= i + by < size]
    return lax.ppermute(array, axis, pairs)


def advance(current, upper_row, lower_row, forcing, factor):
    left_col = jnp.roll(current, 1, axis=1)
    right_col = jnp.roll(current, -1, axis=1)
    transport = jnp.maximum(current, 0.0) * (
        current - upper_row + (current - left_col)
    ) + jnp.minimum(current, 0.0) * (lower_row - current + (right_col - current))
    laplace_term = upper_row + lower_row + left_col + right_col - 4.0 * current
    return (
        current
        - factor * ADVECT * transport
        + factor * DIFFUSE * laplace_term
        + factor * FORCE * forcing
    )


def local(c_points, source):
    first_field = c_points[0]
    coarse_factor = float(STEPS_SLAB)

    def coarse_strip(current):
        padded = with_halo(current, (("space", 0),), 1)
        return advance(current, padded[:-2], padded[2:], source, coarse_factor)

    def fine_slab(current):
        for _ in range(STEPS_SLAB):
            padded = with_halo(current, (("space", 0),), 1)
            current = advance(current, padded[:-2], padded[2:], source, 1.0)
        return current

    defect = fine_slab(first_field) - coarse_strip(first_field)
    my_slab = lax.axis_index("tm")
    is_first = my_slab == 0
    slabs = lax.axis_size("tm")

    def link_strip(turn, incoming):
        begin_field = jnp.where(is_first, first_field, incoming)
        return from_behind(coarse_strip(begin_field) + defect, "tm", 1)

    incoming = lax.fori_loop(0, slabs - 1, link_strip, jnp.zeros_like(first_field))
    begin_field = jnp.where(is_first, first_field, incoming)
    corrected = coarse_strip(begin_field) + defect
    fine_result = fine_slab(begin_field)
    return (corrected[None], fine_result[None])


def solution(mesh):
    return jax.shard_map(
        local,
        mesh=mesh,
        in_specs=(P("tm", "space", None), P("space", None)),
        out_specs=(P("tm", "space", None), P("tm", "space", None)),
        check_vma=False,
    )
```

profile of v0, /device:TPU:123, one launch (start us, length us, event | category | flops | bytes accessed | tf_op | source)
XLA Modules:
  0.0 258.0 jit_solution(2998533353988008832)
XLA Ops:
  1.4 5.0 %collective-permute-start.3 = (f32[1,1024]{1,0:T(1,128)S(1)}, f32[1,1024]{1,0:T(1,128)S(1)}, u32[]{:S(2)}, u32[]{:S(2)}) collective-permute-start(f32[1,1024]{1,0:T(1,128)S(1)} %get-tuple-element.149), channel_id=1, source_target_pairs={{0,1},{1,2},{2,3},{3,4},{4,5},{5,6},{6,7},{7,8},{8,9},{9,10},{10,1... | collective-permute-start | bytes 12296 | tf_op jit(solution)/shard_map/ppermute | solution.py:22
  10.0 4.6 %collective-permute-done.4 = f32[1,1024]{1,0:T(1,128)S(1)} collective-permute-done((f32[1,1024]{1,0:T(1,128)S(1)}, f32[1,1024]{1,0:T(1,128)S(1)}, u32[]{:S(2)}, u32[]{:S(2)}) %collective-permute-start.4) | collective-permute-done | bytes 4128 | tf_op jit(solution)/shard_map/ppermute | solution.py:24
  15.4 2.3 collective-permute-start.5
  17.7 2.0 collective-permute-start.6
  19.8 6.2 %collective-permute-done.6 = f32[1,1024]{1,0:T(1,128)S(1)} collective-permute-done((f32[1,1024]{1,0:T(1,128)S(1)}, f32[1,1024]{1,0:T(1,128)S(1)}, u32[]{:S(2)}, u32[]{:S(2)}) %collective-permute-start.6) | collective-permute-done | bytes 4128 | tf_op jit(solution)/shard_map/ppermute | solution.py:24
  26.8 1.9 collective-permute-start.7
  28.7 2.4 collective-permute-start.8
  31.2 5.8 %collective-permute-done.8 = f32[1,1024]{1,0:T(1,128)S(1)} collective-permute-done((f32[1,1024]{1,0:T(1,128)S(1)}, f32[1,1024]{1,0:T(1,128)S(1)}, u32[]{:S(2)}, u32[]{:S(2)}) %collective-permute-start.8) | collective-permute-done | bytes 4128 | tf_op jit(solution)/shard_map/ppermute | solution.py:24
  39.7 7.0 %collective-permute-start.9 = (f32[1,1024]{1,0:T(1,128)S(1)}, f32[1,1024]{1,0:T(1,128)S(1)}, u32[]{:S(2)}, u32[]{:S(2)}) collective-permute-start(f32[1,1024]{1,0:T(1,128)S(1)} %get-tuple-element.131), channel_id=1, source_target_pairs={{0,1},{1,2},{2,3},{3,4},{4,5},{5,6},{6,7},{7,8},{8,9},{9,10},{10,1... | collective-permute-start | bytes 12296 | tf_op jit(solution)/shard_map/ppermute | solution.py:22
  48.1 7.5 %collective-permute-start.11 = (f32[1,1024]{1,0:T(1,128)S(1)}, f32[1,1024]{1,0:T(1,128)S(1)}, u32[]{:S(2)}, u32[]{:S(2)}) collective-permute-start(f32[1,1024]{1,0:T(1,128)S(1)} %get-tuple-element.125), channel_id=1, source_target_pairs={{0,1},{1,2},{2,3},{3,4},{4,5},{5,6},{6,7},{7,8},{8,9},{9,10},{10,1... | collective-permute-start | bytes 12296 | tf_op jit(solution)/shard_map/ppermute | solution.py:22
  57.7 6.2 %collective-permute-done.12 = f32[1,1024]{1,0:T(1,128)S(1)} collective-permute-done((f32[1,1024]{1,0:T(1,128)S(1)}, f32[1,1024]{1,0:T(1,128)S(1)}, u32[]{:S(2)}, u32[]{:S(2)}) %collective-permute-start.12) | collective-permute-done | bytes 4128 | tf_op jit(solution)/shard_map/ppermute | solution.py:24
  64.7 1.9 collective-permute-start.13
  66.6 2.4 collective-permute-start.14
  69.1 5.8 %collective-permute-done.14 = f32[1,1024]{1,0:T(1,128)S(1)} collective-permute-done((f32[1,1024]{1,0:T(1,128)S(1)}, f32[1,1024]{1,0:T(1,128)S(1)}, u32[]{:S(2)}, u32[]{:S(2)}) %collective-permute-start.14) | collective-permute-done | bytes 4128 | tf_op jit(solution)/shard_map/ppermute | solution.py:24
  75.6 1.9 collective-permute-start.15
  77.6 2.4 collective-permute-start.16
  80.1 5.8 %collective-permute-done.16 = f32[1,1024]{1,0:T(1,128)S(1)} collective-permute-done((f32[1,1024]{1,0:T(1,128)S(1)}, f32[1,1024]{1,0:T(1,128)S(1)}, u32[]{:S(2)}, u32[]{:S(2)}) %collective-permute-start.16) | collective-permute-done | bytes 4128 | tf_op jit(solution)/shard_map/ppermute | solution.py:24
  86.6 1.9 collective-permute-start.17
  88.6 2.4 collective-permute-start.18
  91.0 5.8 %collective-permute-done.18 = f32[1,1024]{1,0:T(1,128)S(1)} collective-permute-done((f32[1,1024]{1,0:T(1,128)S(1)}, f32[1,1024]{1,0:T(1,128)S(1)}, u32[]{:S(2)}, u32[]{:S(2)}) %collective-permute-start.18) | collective-permute-done | bytes 4128 | tf_op jit(solution)/shard_map/ppermute | solution.py:24
  97.9 65.4 %while.10 = (s32[]{:T(128)}, f32[128,1024]{1,0:T(8,128)S(1)}, pred[]{:T(512)}, f32[128,1024]{1,0:T(8,128)S(1)}, f32[128,1024]{1,0:T(8,128)S(1)}, /*index=5*/f32[128,1024]{1,0:T(8,128)S(1)}, s32[]{:T(128)}) while((s32[]{:T(128)}, f32[128,1024]{1,0:T(8,128)S(1)}, pred[]{:T(512)}, f32[128,1024]{1,0:T(8,128)S(1)}, f32[128,1024]{1,0:T(8,128)S(1)}, ...), condition=%wide.region_1.2_spmd, body=%wide.region_0.1_spmd.sunk | while | flops 3670018 | bytes 8970438 | solution.py:75
  99.9 7.0 %collective-permute-start.1 = (f32[1,1024]{1,0:T(1,128)S(1)}, f32[1,1024]{1,0:T(1,128)S(1)}, u32[]{:S(2)}, u32[]{:S(2)}) collective-permute-start(f32[1,1024]{1,0:T(1,128)S(1)} %get-tuple-element.195), channel_id=1, source_target_pairs={{0,1},{1,2},{2,3},{3,4},{4,5},{5,6},{6,7},{7,8},{8,9},{9,10},{10,1... | collective-permute-start | bytes 12296 | tf_op jit(solution)/shard_map/while/body/eval_jaxpr/ppermute | solution.py:22
  108.2 3.1 %collective-permute-start.2 = (f32[128,1024]{1,0:T(8,128)S(1)}, f32[128,1024]{1,0:T(8,128)S(1)}, u32[]{:S(2)}, u32[]{:S(2)}) collective-permute-start(f32[128,1024]{1,0:T(8,128)S(1)} %fusion.322), channel_id=1, source_target_pairs={{0,64},{64,128},{128,192},{1,65},{65,129},{129,193},{2,66},{66,130... | collective-permute-start | bytes 1572872 | tf_op jit(solution)/shard_map/while/body/eval_jaxpr/ppermute | solution.py:34
  111.3 8.4 %collective-permute-done.2 = f32[128,1024]{1,0:T(8,128)S(1)} collective-permute-done((f32[128,1024]{1,0:T(8,128)S(1)}, f32[128,1024]{1,0:T(8,128)S(1)}, u32[]{:S(2)}, u32[]{:S(2)}) %collective-permute-start.2) | collective-permute-done | bytes 524320 | tf_op jit(solution)/shard_map/while/body/eval_jaxpr/ppermute | solution.py:34
  121.7 7.1 %collective-permute-start.1 = (f32[1,1024]{1,0:T(1,128)S(1)}, f32[1,1024]{1,0:T(1,128)S(1)}, u32[]{:S(2)}, u32[]{:S(2)}) collective-permute-start(f32[1,1024]{1,0:T(1,128)S(1)} %get-tuple-element.195), channel_id=1, source_target_pairs={{0,1},{1,2},{2,3},{3,4},{4,5},{5,6},{6,7},{7,8},{8,9},{9,10},{10,1... | collective-permute-start | bytes 12296 | tf_op jit(solution)/shard_map/while/body/eval_jaxpr/ppermute | solution.py:22
  130.1 3.1 %collective-permute-start.2 = (f32[128,1024]{1,0:T(8,128)S(1)}, f32[128,1024]{1,0:T(8,128)S(1)}, u32[]{:S(2)}, u32[]{:S(2)}) collective-permute-start(f32[128,1024]{1,0:T(8,128)S(1)} %fusion.322), channel_id=1, source_target_pairs={{0,64},{64,128},{128,192},{1,65},{65,129},{129,193},{2,66},{66,130... | collective-permute-start | bytes 1572872 | tf_op jit(solution)/shard_map/while/body/eval_jaxpr/ppermute | solution.py:34
  133.2 8.3 %collective-permute-done.2 = f32[128,1024]{1,0:T(8,128)S(1)} collective-permute-done((f32[128,1024]{1,0:T(8,128)S(1)}, f32[128,1024]{1,0:T(8,128)S(1)}, u32[]{:S(2)}, u32[]{:S(2)}) %collective-permute-start.2) | collective-permute-done | bytes 524320 | tf_op jit(solution)/shard_map/while/body/eval_jaxpr/ppermute | solution.py:34
  143.5 7.1 %collective-permute-start.1 = (f32[1,1024]{1,0:T(1,128)S(1)}, f32[1,1024]{1,0:T(1,128)S(1)}, u32[]{:S(2)}, u32[]{:S(2)}) collective-permute-start(f32[1,1024]{1,0:T(1,128)S(1)} %get-tuple-element.195), channel_id=1, source_target_pairs={{0,1},{1,2},{2,3},{3,4},{4,5},{5,6},{6,7},{7,8},{8,9},{9,10},{10,1... | collective-permute-start | bytes 12296 | tf_op jit(solution)/shard_map/while/body/eval_jaxpr/ppermute | solution.py:22
  152.0 3.1 %collective-permute-start.2 = (f32[128,1024]{1,0:T(8,128)S(1)}, f32[128,1024]{1,0:T(8,128)S(1)}, u32[]{:S(2)}, u32[]{:S(2)}) collective-permute-start(f32[128,1024]{1,0:T(8,128)S(1)} %fusion.322), channel_id=1, source_target_pairs={{0,64},{64,128},{128,192},{1,65},{65,129},{129,193},{2,66},{66,130... | collective-permute-start | bytes 1572872 | tf_op jit(solution)/shard_map/while/body/eval_jaxpr/ppermute | solution.py:34
  155.1 8.2 %collective-permute-done.2 = f32[128,1024]{1,0:T(8,128)S(1)} collective-permute-done((f32[128,1024]{1,0:T(8,128)S(1)}, f32[128,1024]{1,0:T(8,128)S(1)}, u32[]{:S(2)}, u32[]{:S(2)}) %collective-permute-start.2) | collective-permute-done | bytes 524320 | tf_op jit(solution)/shard_map/while/body/eval_jaxpr/ppermute | solution.py:34
  163.6 7.2 %collective-permute-start.19 = (f32[1,1024]{1,0:T(1,128)S(1)}, f32[1,1024]{1,0:T(1,128)S(1)}, u32[]{:S(2)}, u32[]{:S(2)}) collective-permute-start(f32[1,1024]{1,0:T(1,128)S(1)} %get-tuple-element.101), channel_id=1, source_target_pairs={{0,1},{1,2},{2,3},{3,4},{4,5},{5,6},{6,7},{7,8},{8,9},{9,10},{10,1... | collective-permute-start | bytes 12296 | tf_op jit(solution)/shard_map/ppermute | solution.py:22
  172.8 6.2 %collective-permute-done.20 = f32[1,1024]{1,0:T(1,128)S(1)} collective-permute-done((f32[1,1024]{1,0:T(1,128)S(1)}, f32[1,1024]{1,0:T(1,128)S(1)}, u32[]{:S(2)}, u32[]{:S(2)}) %collective-permute-start.20) | collective-permute-done | bytes 4128 | tf_op jit(solution)/shard_map/ppermute | solution.py:24
  180.8 1.9 collective-permute-start.21
  182.7 2.4 collective-permute-start.22
  185.2 5.8 %collective-permute-done.22 = f32[1,1024]{1,0:T(1,128)S(1)} collective-permute-done((f32[1,1024]{1,0:T(1,128)S(1)}, f32[1,1024]{1,0:T(1,128)S(1)}, u32[]{:S(2)}, u32[]{:S(2)}) %collective-permute-start.22) | collective-permute-done | bytes 4128 | tf_op jit(solution)/shard_map/ppermute | solution.py:24
  191.7 1.9 collective-permute-start.23
  193.7 2.4 collective-permute-start.24
  196.1 5.8 %collective-permute-done.24 = f32[1,1024]{1,0:T(1,128)S(1)} collective-permute-done((f32[1,1024]{1,0:T(1,128)S(1)}, f32[1,1024]{1,0:T(1,128)S(1)}, u32[]{:S(2)}, u32[]{:S(2)}) %collective-permute-start.24) | collective-permute-done | bytes 4128 | tf_op jit(solution)/shard_map/ppermute | solution.py:24
  204.6 2.6 collective-permute-start.26
  207.3 5.6 %collective-permute-done.26 = f32[1,1024]{1,0:T(1,128)S(1)} collective-permute-done((f32[1,1024]{1,0:T(1,128)S(1)}, f32[1,1024]{1,0:T(1,128)S(1)}, u32[]{:S(2)}, u32[]{:S(2)}) %collective-permute-start.26) | collective-permute-done | bytes 4128 | tf_op jit(solution)/shard_map/ppermute | solution.py:24
  215.6 2.4 collective-permute-start.28
  218.1 5.8 %collective-permute-done.28 = f32[1,1024]{1,0:T(1,128)S(1)} collective-permute-done((f32[1,1024]{1,0:T(1,128)S(1)}, f32[1,1024]{1,0:T(1,128)S(1)}, u32[]{:S(2)}, u32[]{:S(2)}) %collective-permute-start.28) | collective-permute-done | bytes 4128 | tf_op jit(solution)/shard_map/ppermute | solution.py:24
  226.5 2.4 collective-permute-start.30
  229.0 5.8 %collective-permute-done.30 = f32[1,1024]{1,0:T(1,128)S(1)} collective-permute-done((f32[1,1024]{1,0:T(1,128)S(1)}, f32[1,1024]{1,0:T(1,128)S(1)}, u32[]{:S(2)}, u32[]{:S(2)}) %collective-permute-start.30) | collective-permute-done | bytes 4128 | tf_op jit(solution)/shard_map/ppermute | solution.py:24
  237.5 2.4 collective-permute-start.32
  240.0 5.8 %collective-permute-done.32 = f32[1,1024]{1,0:T(1,128)S(1)} collective-permute-done((f32[1,1024]{1,0:T(1,128)S(1)}, f32[1,1024]{1,0:T(1,128)S(1)}, u32[]{:S(2)}, u32[]{:S(2)}) %collective-permute-start.32) | collective-permute-done | bytes 4128 | tf_op jit(solution)/shard_map/ppermute | solution.py:24
  248.5 2.4 collective-permute-start.34
  250.9 5.8 %collective-permute-done.34 = f32[1,1024]{1,0:T(1,128)S(1)} collective-permute-done((f32[1,1024]{1,0:T(1,128)S(1)}, f32[1,1024]{1,0:T(1,128)S(1)}, u32[]{:S(2)}, u32[]{:S(2)}) %collective-permute-start.34) | collective-permute-done | bytes 4128 | tf_op jit(solution)/shard_map/ppermute | solution.py:24
  (120 shorter events, 45.7 us)
Async XLA Ops:
  1.4 8.6 %collective-permute-start.3 = (f32[1,1024]{1,0:T(1,128)S(1)}, f32[1,1024]{1,0:T(1,128)S(1)}, u32[]{:S(2)}, u32[]{:S(2)}) collective-permute-start(f32[1,1024]{1,0:T(1,128)S(1)} %get-tuple-element.149), channel_id=1, source_target_pairs={{0,1},{1,2},{2,3},{3,4},{4,5},{5,6},{6,7},{7,8},{8,9},{9,10},{10,1... | collective-permute-start | bytes 12296 | tf_op jit(solution)/shard_map/ppermute | solution.py:22
  6.4 8.2 %collective-permute-start.4 = (f32[1,1024]{1,0:T(1,128)S(1)}, f32[1,1024]{1,0:T(1,128)S(1)}, u32[]{:S(2)}, u32[]{:S(2)}) collective-permute-start(f32[1,1024]{1,0:T(1,128)S(1)} %get-tuple-element.150), channel_id=1, source_target_pairs={{1,0},{2,1},{3,2},{4,3},{5,4},{6,5},{7,6},{8,7},{9,8},{10,9},{11,1... | collective-permute-start | bytes 12296 | tf_op jit(solution)/shard_map/ppermute | solution.py:24
  8.3 1.6 copy-start.1
  8.3 6.3 %copy-start = (f32[128,1024]{1,0:T(8,128)S(1)}, f32[128,1024]{1,0:T(8,128)}, u32[]{:S(2)}) copy-start(f32[128,1024]{1,0:T(8,128)} %param.5) | copy-start | bytes 1572868
  15.4 4.4 %collective-permute-start.5 = (f32[1,1024]{1,0:T(1,128)S(1)}, f32[1,1024]{1,0:T(1,128)S(1)}, u32[]{:S(2)}, u32[]{:S(2)}) collective-permute-start(f32[1,1024]{1,0:T(1,128)S(1)} %get-tuple-element.143), channel_id=1, source_target_pairs={{0,1},{1,2},{2,3},{3,4},{4,5},{5,6},{6,7},{7,8},{8,9},{9,10},{10,1... | collective-permute-start | bytes 12296 | tf_op jit(solution)/shard_map/ppermute | solution.py:22
  17.7 8.2 %collective-permute-start.6 = (f32[1,1024]{1,0:T(1,128)S(1)}, f32[1,1024]{1,0:T(1,128)S(1)}, u32[]{:S(2)}, u32[]{:S(2)}) collective-permute-start(f32[1,1024]{1,0:T(1,128)S(1)} %get-tuple-element.144), channel_id=1, source_target_pairs={{1,0},{2,1},{3,2},{4,3},{5,4},{6,5},{7,6},{8,7},{9,8},{10,9},{11,1... | collective-permute-start | bytes 12296 | tf_op jit(solution)/shard_map/ppermute | solution.py:24
  26.8 4.4 %collective-permute-start.7 = (f32[1,1024]{1,0:T(1,128)S(1)}, f32[1,1024]{1,0:T(1,128)S(1)}, u32[]{:S(2)}, u32[]{:S(2)}) collective-permute-start(f32[1,1024]{1,0:T(1,128)S(1)} %get-tuple-element.137), channel_id=1, source_target_pairs={{0,1},{1,2},{2,3},{3,4},{4,5},{5,6},{6,7},{7,8},{8,9},{9,10},{10,1... | collective-permute-start | bytes 12296 | tf_op jit(solution)/shard_map/ppermute | solution.py:22
  28.7 8.2 %collective-permute-start.8 = (f32[1,1024]{1,0:T(1,128)S(1)}, f32[1,1024]{1,0:T(1,128)S(1)}, u32[]{:S(2)}, u32[]{:S(2)}) collective-permute-start(f32[1,1024]{1,0:T(1,128)S(1)} %get-tuple-element.138), channel_id=1, source_target_pairs={{1,0},{2,1},{3,2},{4,3},{5,4},{6,5},{7,6},{8,7},{9,8},{10,9},{11,1... | collective-permute-start | bytes 12296 | tf_op jit(solution)/shard_map/ppermute | solution.py:24
  37.7 9.0 %collective-permute-start.10 = (f32[1,1024]{1,0:T(1,128)S(1)}, f32[1,1024]{1,0:T(1,128)S(1)}, u32[]{:S(2)}, u32[]{:S(2)}) collective-permute-start(f32[1,1024]{1,0:T(1,128)S(1)} %get-tuple-element.132), channel_id=1, source_target_pairs={{1,0},{2,1},{3,2},{4,3},{5,4},{6,5},{7,6},{8,7},{9,8},{10,9},{11,1... | collective-permute-start | bytes 12296 | tf_op jit(solution)/shard_map/ppermute | solution.py:24
  39.7 7.7 %collective-permute-start.9 = (f32[1,1024]{1,0:T(1,128)S(1)}, f32[1,1024]{1,0:T(1,128)S(1)}, u32[]{:S(2)}, u32[]{:S(2)}) collective-permute-start(f32[1,1024]{1,0:T(1,128)S(1)} %get-tuple-element.131), channel_id=1, source_target_pairs={{0,1},{1,2},{2,3},{3,4},{4,5},{5,6},{6,7},{7,8},{8,9},{9,10},{10,1... | collective-permute-start | bytes 12296 | tf_op jit(solution)/shard_map/ppermute | solution.py:22
  48.1 9.5 %collective-permute-start.11 = (f32[1,1024]{1,0:T(1,128)S(1)}, f32[1,1024]{1,0:T(1,128)S(1)}, u32[]{:S(2)}, u32[]{:S(2)}) collective-permute-start(f32[1,1024]{1,0:T(1,128)S(1)} %get-tuple-element.125), channel_id=1, source_target_pairs={{0,1},{1,2},{2,3},{3,4},{4,5},{5,6},{6,7},{7,8},{8,9},{9,10},{10,1... | collective-permute-start | bytes 12296 | tf_op jit(solution)/shard_map/ppermute | solution.py:22
  55.6 8.2 %collective-permute-start.12 = (f32[1,1024]{1,0:T(1,128)S(1)}, f32[1,1024]{1,0:T(1,128)S(1)}, u32[]{:S(2)}, u32[]{:S(2)}) collective-permute-start(f32[1,1024]{1,0:T(1,128)S(1)} %get-tuple-element.126), channel_id=1, source_target_pairs={{1,0},{2,1},{3,2},{4,3},{5,4},{6,5},{7,6},{8,7},{9,8},{10,9},{11,1... | collective-permute-start | bytes 12296 | tf_op jit(solution)/shard_map/ppermute | solution.py:24
  64.7 4.4 %collective-permute-start.13 = (f32[1,1024]{1,0:T(1,128)S(1)}, f32[1,1024]{1,0:T(1,128)S(1)}, u32[]{:S(2)}, u32[]{:S(2)}) collective-permute-start(f32[1,1024]{1,0:T(1,128)S(1)} %get-tuple-element.119), channel_id=1, source_target_pairs={{0,1},{1,2},{2,3},{3,4},{4,5},{5,6},{6,7},{7,8},{8,9},{9,10},{10,1... | collective-permute-start | bytes 12296 | tf_op jit(solution)/shard_map/ppermute | solution.py:22
  66.6 8.2 %collective-permute-start.14 = (f32[1,1024]{1,0:T(1,128)S(1)}, f32[1,1024]{1,0:T(1,128)S(1)}, u32[]{:S(2)}, u32[]{:S(2)}) collective-permute-start(f32[1,1024]{1,0:T(1,128)S(1)} %get-tuple-element.120), channel_id=1, source_target_pairs={{1,0},{2,1},{3,2},{4,3},{5,4},{6,5},{7,6},{8,7},{9,8},{10,9},{11,1... | collective-permute-start | bytes 12296 | tf_op jit(solution)/shard_map/ppermute | solution.py:24
  75.6 4.4 %collective-permute-start.15 = (f32[1,1024]{1,0:T(1,128)S(1)}, f32[1,1024]{1,0:T(1,128)S(1)}, u32[]{:S(2)}, u32[]{:S(2)}) collective-permute-start(f32[1,1024]{1,0:T(1,128)S(1)} %get-tuple-element.113), channel_id=1, source_target_pairs={{0,1},{1,2},{2,3},{3,4},{4,5},{5,6},{6,7},{7,8},{8,9},{9,10},{10,1... | collective-permute-start | bytes 12296 | tf_op jit(solution)/shard_map/ppermute | solution.py:22
  77.6 8.2 %collective-permute-start.16 = (f32[1,1024]{1,0:T(1,128)S(1)}, f32[1,1024]{1,0:T(1,128)S(1)}, u32[]{:S(2)}, u32[]{:S(2)}) collective-permute-start(f32[1,1024]{1,0:T(1,128)S(1)} %get-tuple-element.114), channel_id=1, source_target_pairs={{1,0},{2,1},{3,2},{4,3},{5,4},{6,5},{7,6},{8,7},{9,8},{10,9},{11,1... | collective-permute-start | bytes 12296 | tf_op jit(solution)/shard_map/ppermute | solution.py:24
  86.6 4.4 %collective-permute-start.17 = (f32[1,1024]{1,0:T(1,128)S(1)}, f32[1,1024]{1,0:T(1,128)S(1)}, u32[]{:S(2)}, u32[]{:S(2)}) collective-permute-start(f32[1,1024]{1,0:T(1,128)S(1)} %get-tuple-element.107), channel_id=1, source_target_pairs={{0,1},{1,2},{2,3},{3,4},{4,5},{5,6},{6,7},{7,8},{8,9},{9,10},{10,1... | collective-permute-start | bytes 12296 | tf_op jit(solution)/shard_map/ppermute | solution.py:22
  88.6 8.2 %collective-permute-start.18 = (f32[1,1024]{1,0:T(1,128)S(1)}, f32[1,1024]{1,0:T(1,128)S(1)}, u32[]{:S(2)}, u32[]{:S(2)}) collective-permute-start(f32[1,1024]{1,0:T(1,128)S(1)} %get-tuple-element.108), channel_id=1, source_target_pairs={{1,0},{2,1},{3,2},{4,3},{5,4},{6,5},{7,6},{8,7},{9,8},{10,9},{11,1... | collective-permute-start | bytes 12296 | tf_op jit(solution)/shard_map/ppermute | solution.py:24
  98.0 9.2 %collective-permute-start = (f32[1,1024]{1,0:T(1,128)S(1)}, f32[1,1024]{1,0:T(1,128)S(1)}, u32[]{:S(2)}, u32[]{:S(2)}) collective-permute-start(f32[1,1024]{1,0:T(1,128)S(1)} %get-tuple-element.194), channel_id=1, source_target_pairs={{1,0},{2,1},{3,2},{4,3},{5,4},{6,5},{7,6},{8,7},{9,8},{10,9},{11,1... | collective-permute-start | bytes 12296 | tf_op jit(solution)/shard_map/while/body/eval_jaxpr/ppermute | solution.py:24
  99.9 7.7 %collective-permute-start.1 = (f32[1,1024]{1,0:T(1,128)S(1)}, f32[1,1024]{1,0:T(1,128)S(1)}, u32[]{:S(2)}, u32[]{:S(2)}) collective-permute-start(f32[1,1024]{1,0:T(1,128)S(1)} %get-tuple-element.195), channel_id=1, source_target_pairs={{0,1},{1,2},{2,3},{3,4},{4,5},{5,6},{6,7},{7,8},{8,9},{9,10},{10,1... | collective-permute-start | bytes 12296 | tf_op jit(solution)/shard_map/while/body/eval_jaxpr/ppermute | solution.py:22
  108.2 11.5 %collective-permute-start.2 = (f32[128,1024]{1,0:T(8,128)S(1)}, f32[128,1024]{1,0:T(8,128)S(1)}, u32[]{:S(2)}, u32[]{:S(2)}) collective-permute-start(f32[128,1024]{1,0:T(8,128)S(1)} %fusion.322), channel_id=1, source_target_pairs={{0,64},{64,128},{128,192},{1,65},{65,129},{129,193},{2,66},{66,130... | collective-permute-start | bytes 1572872 | tf_op jit(solution)/shard_map/while/body/eval_jaxpr/ppermute | solution.py:34
  119.8 9.3 %collective-permute-start = (f32[1,1024]{1,0:T(1,128)S(1)}, f32[1,1024]{1,0:T(1,128)S(1)}, u32[]{:S(2)}, u32[]{:S(2)}) collective-permute-start(f32[1,1024]{1,0:T(1,128)S(1)} %get-tuple-element.194), channel_id=1, source_target_pairs={{1,0},{2,1},{3,2},{4,3},{5,4},{6,5},{7,6},{8,7},{9,8},{10,9},{11,1... | collective-permute-start | bytes 12296 | tf_op jit(solution)/shard_map/while/body/eval_jaxpr/ppermute | solution.py:24
  121.7 7.8 %collective-permute-start.1 = (f32[1,1024]{1,0:T(1,128)S(1)}, f32[1,1024]{1,0:T(1,128)S(1)}, u32[]{:S(2)}, u32[]{:S(2)}) collective-permute-start(f32[1,1024]{1,0:T(1,128)S(1)} %get-tuple-element.195), channel_id=1, source_target_pairs={{0,1},{1,2},{2,3},{3,4},{4,5},{5,6},{6,7},{7,8},{8,9},{9,10},{10,1... | collective-permute-start | bytes 12296 | tf_op jit(solution)/shard_map/while/body/eval_jaxpr/ppermute | solution.py:22
  130.1 11.4 %collective-permute-start.2 = (f32[128,1024]{1,0:T(8,128)S(1)}, f32[128,1024]{1,0:T(8,128)S(1)}, u32[]{:S(2)}, u32[]{:S(2)}) collective-permute-start(f32[128,1024]{1,0:T(8,128)S(1)} %fusion.322), channel_id=1, source_target_pairs={{0,64},{64,128},{128,192},{1,65},{65,129},{129,193},{2,66},{66,130... | collective-permute-start | bytes 1572872 | tf_op jit(solution)/shard_map/while/body/eval_jaxpr/ppermute | solution.py:34
  141.6 9.4 %collective-permute-start = (f32[1,1024]{1,0:T(1,128)S(1)}, f32[1,1024]{1,0:T(1,128)S(1)}, u32[]{:S(2)}, u32[]{:S(2)}) collective-permute-start(f32[1,1024]{1,0:T(1,128)S(1)} %get-tuple-element.194), channel_id=1, source_target_pairs={{1,0},{2,1},{3,2},{4,3},{5,4},{6,5},{7,6},{8,7},{9,8},{10,9},{11,1... | collective-permute-start | bytes 12296 | tf_op jit(solution)/shard_map/while/body/eval_jaxpr/ppermute | solution.py:24
  143.5 7.9 %collective-permute-start.1 = (f32[1,1024]{1,0:T(1,128)S(1)}, f32[1,1024]{1,0:T(1,128)S(1)}, u32[]{:S(2)}, u32[]{:S(2)}) collective-permute-start(f32[1,1024]{1,0:T(1,128)S(1)} %get-tuple-element.195), channel_id=1, source_target_pairs={{0,1},{1,2},{2,3},{3,4},{4,5},{5,6},{6,7},{7,8},{8,9},{9,10},{10,1... | collective-permute-start | bytes 12296 | tf_op jit(solution)/shard_map/while/body/eval_jaxpr/ppermute | solution.py:22
  152.0 11.3 %collective-permute-start.2 = (f32[128,1024]{1,0:T(8,128)S(1)}, f32[128,1024]{1,0:T(8,128)S(1)}, u32[]{:S(2)}, u32[]{:S(2)}) collective-permute-start(f32[128,1024]{1,0:T(8,128)S(1)} %fusion.322), channel_id=1, source_target_pairs={{0,64},{64,128},{128,192},{1,65},{65,129},{129,193},{2,66},{66,130... | collective-permute-start | bytes 1572872 | tf_op jit(solution)/shard_map/while/body/eval_jaxpr/ppermute | solution.py:34
  163.6 9.3 %collective-permute-start.19 = (f32[1,1024]{1,0:T(1,128)S(1)}, f32[1,1024]{1,0:T(1,128)S(1)}, u32[]{:S(2)}, u32[]{:S(2)}) collective-permute-start(f32[1,1024]{1,0:T(1,128)S(1)} %get-tuple-element.101), channel_id=1, source_target_pairs={{0,1},{1,2},{2,3},{3,4},{4,5},{5,6},{6,7},{7,8},{8,9},{9,10},{10,1... | collective-permute-start | bytes 12296 | tf_op jit(solution)/shard_map/ppermute | solution.py:22
  170.8 8.2 %collective-permute-start.20 = (f32[1,1024]{1,0:T(1,128)S(1)}, f32[1,1024]{1,0:T(1,128)S(1)}, u32[]{:S(2)}, u32[]{:S(2)}) collective-permute-start(f32[1,1024]{1,0:T(1,128)S(1)} %get-tuple-element.102), channel_id=1, source_target_pairs={{1,0},{2,1},{3,2},{4,3},{5,4},{6,5},{7,6},{8,7},{9,8},{10,9},{11,1... | collective-permute-start | bytes 12296 | tf_op jit(solution)/shard_map/ppermute | solution.py:24
  180.8 4.4 %collective-permute-start.21 = (f32[1,1024]{1,0:T(1,128)S(1)}, f32[1,1024]{1,0:T(1,128)S(1)}, u32[]{:S(2)}, u32[]{:S(2)}) collective-permute-start(f32[1,1024]{1,0:T(1,128)S(1)} %get-tuple-element.95), channel_id=1, source_target_pairs={{0,1},{1,2},{2,3},{3,4},{4,5},{5,6},{6,7},{7,8},{8,9},{9,10},{10,1... | collective-permute-start | bytes 12296 | tf_op jit(solution)/shard_map/ppermute | solution.py:22
  182.7 8.2 %collective-permute-start.22 = (f32[1,1024]{1,0:T(1,128)S(1)}, f32[1,1024]{1,0:T(1,128)S(1)}, u32[]{:S(2)}, u32[]{:S(2)}) collective-permute-start(f32[1,1024]{1,0:T(1,128)S(1)} %get-tuple-element.96), channel_id=1, source_target_pairs={{1,0},{2,1},{3,2},{4,3},{5,4},{6,5},{7,6},{8,7},{9,8},{10,9},{11,1... | collective-permute-start | bytes 12296 | tf_op jit(solution)/shard_map/ppermute | solution.py:24
  191.7 4.4 %collective-permute-start.23 = (f32[1,1024]{1,0:T(1,128)S(1)}, f32[1,1024]{1,0:T(1,128)S(1)}, u32[]{:S(2)}, u32[]{:S(2)}) collective-permute-start(f32[1,1024]{1,0:T(1,128)S(1)} %get-tuple-element.89), channel_id=1, source_target_pairs={{0,1},{1,2},{2,3},{3,4},{4,5},{5,6},{6,7},{7,8},{8,9},{9,10},{10,1... | collective-permute-start | bytes 12296 | tf_op jit(solution)/shard_map/ppermute | solution.py:22
  193.7 8.2 %collective-permute-start.24 = (f32[1,1024]{1,0:T(1,128)S(1)}, f32[1,1024]{1,0:T(1,128)S(1)}, u32[]{:S(2)}, u32[]{:S(2)}) collective-permute-start(f32[1,1024]{1,0:T(1,128)S(1)} %get-tuple-element.90), channel_id=1, source_target_pairs={{1,0},{2,1},{3,2},{4,3},{5,4},{6,5},{7,6},{8,7},{9,8},{10,9},{11,1... | collective-permute-start | bytes 12296 | tf_op jit(solution)/shard_map/ppermute | solution.py:24
  202.7 4.6 %collective-permute-start.25 = (f32[1,1024]{1,0:T(1,128)S(1)}, f32[1,1024]{1,0:T(1,128)S(1)}, u32[]{:S(2)}, u32[]{:S(2)}) collective-permute-start(f32[1,1024]{1,0:T(1,128)S(1)} %get-tuple-element.83), channel_id=1, source_target_pairs={{0,1},{1,2},{2,3},{3,4},{4,5},{5,6},{6,7},{7,8},{8,9},{9,10},{10,1... | collective-permute-start | bytes 12296 | tf_op jit(solution)/shard_map/ppermute | solution.py:22
  204.6 8.2 %collective-permute-start.26 = (f32[1,1024]{1,0:T(1,128)S(1)}, f32[1,1024]{1,0:T(1,128)S(1)}, u32[]{:S(2)}, u32[]{:S(2)}) collective-permute-start(f32[1,1024]{1,0:T(1,128)S(1)} %get-tuple-element.84), channel_id=1, source_target_pairs={{1,0},{2,1},{3,2},{4,3},{5,4},{6,5},{7,6},{8,7},{9,8},{10,9},{11,1... | collective-permute-start | bytes 12296 | tf_op jit(solution)/shard_map/ppermute | solution.py:24
  213.6 4.4 %collective-permute-start.27 = (f32[1,1024]{1,0:T(1,128)S(1)}, f32[1,1024]{1,0:T(1,128)S(1)}, u32[]{:S(2)}, u32[]{:S(2)}) collective-permute-start(f32[1,1024]{1,0:T(1,128)S(1)} %get-tuple-element.77), channel_id=1, source_target_pairs={{0,1},{1,2},{2,3},{3,4},{4,5},{5,6},{6,7},{7,8},{8,9},{9,10},{10,1... | collective-permute-start | bytes 12296 | tf_op jit(solution)/shard_map/ppermute | solution.py:22
  215.6 8.2 %collective-permute-start.28 = (f32[1,1024]{1,0:T(1,128)S(1)}, f32[1,1024]{1,0:T(1,128)S(1)}, u32[]{:S(2)}, u32[]{:S(2)}) collective-permute-start(f32[1,1024]{1,0:T(1,128)S(1)} %get-tuple-element.78), channel_id=1, source_target_pairs={{1,0},{2,1},{3,2},{4,3},{5,4},{6,5},{7,6},{8,7},{9,8},{10,9},{11,1... | collective-permute-start | bytes 12296 | tf_op jit(solution)/shard_map/ppermute | solution.py:24
  224.6 4.4 %collective-permute-start.29 = (f32[1,1024]{1,0:T(1,128)S(1)}, f32[1,1024]{1,0:T(1,128)S(1)}, u32[]{:S(2)}, u32[]{:S(2)}) collective-permute-start(f32[1,1024]{1,0:T(1,128)S(1)} %get-tuple-element.71), channel_id=1, source_target_pairs={{0,1},{1,2},{2,3},{3,4},{4,5},{5,6},{6,7},{7,8},{8,9},{9,10},{10,1... | collective-permute-start | bytes 12296 | tf_op jit(solution)/shard_map/ppermute | solution.py:22
  226.5 8.2 %collective-permute-start.30 = (f32[1,1024]{1,0:T(1,128)S(1)}, f32[1,1024]{1,0:T(1,128)S(1)}, u32[]{:S(2)}, u32[]{:S(2)}) collective-permute-start(f32[1,1024]{1,0:T(1,128)S(1)} %get-tuple-element.72), channel_id=1, source_target_pairs={{1,0},{2,1},{3,2},{4,3},{5,4},{6,5},{7,6},{8,7},{9,8},{10,9},{11,1... | collective-permute-start | bytes 12296 | tf_op jit(solution)/shard_map/ppermute | solution.py:24
  235.5 4.4 %collective-permute-start.31 = (f32[1,1024]{1,0:T(1,128)S(1)}, f32[1,1024]{1,0:T(1,128)S(1)}, u32[]{:S(2)}, u32[]{:S(2)}) collective-permute-start(f32[1,1024]{1,0:T(1,128)S(1)} %get-tuple-element.65), channel_id=1, source_target_pairs={{0,1},{1,2},{2,3},{3,4},{4,5},{5,6},{6,7},{7,8},{8,9},{9,10},{10,1... | collective-permute-start | bytes 12296 | tf_op jit(solution)/shard_map/ppermute | solution.py:22
  237.5 8.2 %collective-permute-start.32 = (f32[1,1024]{1,0:T(1,128)S(1)}, f32[1,1024]{1,0:T(1,128)S(1)}, u32[]{:S(2)}, u32[]{:S(2)}) collective-permute-start(f32[1,1024]{1,0:T(1,128)S(1)} %get-tuple-element.66), channel_id=1, source_target_pairs={{1,0},{2,1},{3,2},{4,3},{5,4},{6,5},{7,6},{8,7},{9,8},{10,9},{11,1... | collective-permute-start | bytes 12296 | tf_op jit(solution)/shard_map/ppermute | solution.py:24
  246.5 4.4 %collective-permute-start.33 = (f32[1,1024]{1,0:T(1,128)S(1)}, f32[1,1024]{1,0:T(1,128)S(1)}, u32[]{:S(2)}, u32[]{:S(2)}) collective-permute-start(f32[1,1024]{1,0:T(1,128)S(1)} %get-tuple-element.59), channel_id=1, source_target_pairs={{0,1},{1,2},{2,3},{3,4},{4,5},{5,6},{6,7},{7,8},{8,9},{9,10},{10,1... | collective-permute-start | bytes 12296 | tf_op jit(solution)/shard_map/ppermute | solution.py:22
  248.5 8.2 %collective-permute-start.34 = (f32[1,1024]{1,0:T(1,128)S(1)}, f32[1,1024]{1,0:T(1,128)S(1)}, u32[]{:S(2)}, u32[]{:S(2)}) collective-permute-start(f32[1,1024]{1,0:T(1,128)S(1)} %get-tuple-element.60), channel_id=1, source_target_pairs={{1,0},{2,1},{3,2},{4,3},{5,4},{6,5},{7,6},{8,7},{9,8},{10,9},{11,1... | collective-permute-start | bytes 12296 | tf_op jit(solution)/shard_map/ppermute | solution.py:24
where the time goes:
time: 259 us; the launch traced here: 258 us
  starting transfers between devices  123 us (47%)
  waiting for transfers between devices  114 us (44%)
  other arithmetic  12.7 us (5%)
  local copies, waits for them, and re-layouts  7.76 us (3%)
    ppermute x19, waiting for transfers between devices, with_halo(): lax.ppermute(head, axis, [((i + 1) % count, i) for i in range(ends)])  86.6 us
    ppermute x19, starting transfers between devices, with_halo(): lax.ppermute(tail, axis, [(i, (i + 1) % count) for i in range(ends)])  71.6 us
    ppermute x19, starting transfers between devices, with_halo(): lax.ppermute(head, axis, [((i + 1) % count, i) for i in range(ends)])  41.7 us
    ppermute x3, waiting for transfers between devices, from_behind(): return lax.ppermute(array, axis, pairs)  24.9 us
    ppermute x3, starting transfers between devices, from_behind(): return lax.ppermute(array, axis, pairs)  9.36 us
    add x14, other arithmetic, advance(): current - factor * ADVECT * transport + factor * DIFFUSE * laplace_term  8.44 us
    slice x38, local copies, waits for them, and re-layouts, advance(): left_col = jnp.roll(current, 1, axis=1)  6.78 us
  transfers between devices with their start and end apart: 41, of which 22 were waited for; matrix products, arithmetic and copies ran while one was open for 1% of the time, Pallas kernels for 0%

commit v1 on v0

v1 whole, which is shorter than its diff:
```python
import functools

import jax
import jax.numpy as jnp
from jax import lax
from jax.experimental import pallas as pl
from jax.experimental.pallas import tpu as pltpu
from jax.sharding import PartitionSpec as P

ADVECT = 0.02
DIFFUSE = 0.01
FORCE = 0.05
STEPS = 8
SLABS = 4
ROWS = 128
COLS = 1024
LANE = 128
TILES = COLS // LANE
HALO = 24
PAD = 8
REACH = STEPS
PART = (ROWS + 2 * REACH) // SLABS
BLOCK = PART + 4
FAR = REACH + 2


def increment(now, above, below, left, right, force):
    twice = now + now
    rear = above + left - twice
    ahead = below + right - twice
    gain = jnp.maximum(now, 0.0) + DIFFUSE
    return force + gain * rear + (gain - now) * ahead


def row_tile(state, start, lane_ids):
    now = [state[g, pl.ds(start, 8), :] for g in range(TILES)]
    above = [state[g, pl.ds(start - 1, 8), :] for g in range(TILES)]
    below = [state[g, pl.ds(start + 1, 8), :] for g in range(TILES)]
    fore = [pltpu.roll(x, 1, 1) for x in now]
    back = [pltpu.roll(x, LANE - 1, 1) for x in now]
    for g in range(TILES):
        left = jnp.where(lane_ids == 0, fore[g - 1], fore[g])
        right = jnp.where(lane_ids == LANE - 1, back[(g + 1) % TILES], back[g])
        yield g, now[g], above[g], below[g], left, right


def lanes():
    return lax.broadcasted_iota(jnp.int32, (8, LANE), 1)


def place():
    slab = lax.axis_index("tm")
    strip = lax.axis_index("space")
    up_mask = jnp.where(strip == 0, 0.0, 1.0)
    down_mask = jnp.where(strip == lax.axis_size("space") - 1, 0.0, 1.0)
    return slab, strip % 2, up_mask, down_mask


def defect_kernel(c_ref, s_ref, intra_ref, inter_ref, defect_ref, mine_ref, one_ref, two_ref, three_ref, force_ref, one, two, force, coarse):
    slab, odd, up_mask, down_mask = place()
    lane_ids = lanes()
    base = PAD + HALO

    def fill(target, scale, top, main, bottom, offset):
        for g in range(TILES):
            cut = pl.ds(g * LANE, LANE)
            for i in range(HALO // 8):
                rows = pl.ds(offset + 8 * i, 8)
                target[g, pl.ds(PAD + 8 * i, 8), :] = top[rows, cut] * (scale * up_mask)
                target[g, pl.ds(base + ROWS + 8 * i, 8), :] = bottom[rows, cut] * (scale * down_mask)
            if main is not None:
                for i in range(ROWS // 8):
                    target[g, pl.ds(base + 8 * i, 8), :] = main[pl.ds(8 * i, 8), cut] * scale

    c_scale, s_scale = ADVECT, ADVECT * FORCE

    @pl.when(odd == 1)
    def _():
        fill(one, c_scale, intra_ref, c_ref, inter_ref, 0)
        fill(force, s_scale, intra_ref, s_ref, inter_ref, HALO)

    @pl.when(odd == 0)
    def _():
        fill(one, c_scale, inter_ref, c_ref, intra_ref, 0)
        fill(force, s_scale, inter_ref, s_ref, intra_ref, HALO)

    count = (ROWS + 2 * HALO) // 8
    edge = HALO // 8

    def sweep(source, target, first, last, keep):
        for i in range(first, last):
            at = PAD + 8 * i
            for g, now, above, below, left, right in row_tile(source, at, lane_ids):
                inc = increment(now, above, below, left, right, force[g, pl.ds(at, 8), :])
                new = now + inc
                if keep:
                    coarse[g, pl.ds(at, 8), :] = now + 8.0 * inc
                if i < edge:
                    new = new * up_mask
                if i >= count - edge:
                    new = new * down_mask
                target[g, pl.ds(at, 8), :] = new

    sweep(one, two, 0, count, True)
    sweep(two, one, 1, count - 1, False)

    def pair(_, carry):
        sweep(one, two, 1, count - 1, False)
        sweep(two, one, 1, count - 1, False)
        return carry

    lax.fori_loop(0, STEPS // 2 - 1, pair, 0)
    first = jnp.where(slab == 0, 0.0, 1.0)
    for i in range(1, count - 1):
        rows = pl.ds(PAD + 8 * i, 8)
        for g in range(TILES):
            fine = one[g, rows, :]
            rough = coarse[g, rows, :]
            if i < edge:
                rough = rough * up_mask
            if i >= count - edge:
                rough = rough * down_mask
            two[g, rows, :] = fine - first * rough
            if edge <= i < count - edge:
                defect_ref[pl.ds(8 * (i - edge), 8), pl.ds(g * LANE, LANE)] = fine - rough

    for k, out in enumerate((mine_ref, one_ref, two_ref, three_ref)):
        start = base - FAR + PART * (slab ^ k)
        for i in range(BLOCK // 8):
            for g in range(TILES):
                cut = pl.ds(g * LANE, LANE)
                rows = pl.ds(start + 8 * i, 8)
                out[pl.ds(8 * i, 8), cut] = two[g, rows, :]
                if k == 0:
                    force_ref[g, pl.ds(8 * i, 8), :] = force[g, rows, :]


def chain_kernel(mine_ref, one_ref, two_ref, three_ref, force_ref, out0_ref, out1_ref, out2_ref, out3_ref, start1, start2, start3):
    slab, odd, up_mask, down_mask = place()
    lane_ids = lanes()
    boxes = (mine_ref, one_ref, two_ref, three_ref)
    outs = (out0_ref, out1_ref, out2_ref, out3_ref)
    origin = PART * slab - FAR
    row_ids = lax.broadcasted_iota(jnp.int32, (8, LANE), 0)

    def sweep(source, target, defect):
        for i in range(BLOCK // 8):
            at = PAD + 8 * i
            row = row_ids + (origin + 8 * i)
            mask = jnp.where(row < 0, up_mask, jnp.where(row >= ROWS, down_mask, 1.0))
            for g, now, above, below, left, right in row_tile(source, at, lane_ids):
                inc = increment(now, above, below, left, right, force_ref[g, pl.ds(8 * i, 8), :])
                new = now + 8.0 * inc + defect[pl.ds(8 * i, 8), pl.ds(g * LANE, LANE)]
                target[g, pl.ds(at, 8), :] = new * mask

    for t in range(SLABS):
        @pl.when(slab == t)
        def _(t=t):
            for i in range(BLOCK // 8):
                for g in range(TILES):
                    start1[g, pl.ds(PAD + 8 * i, 8), :] = boxes[t][pl.ds(8 * i, 8), pl.ds(g * LANE, LANE)]
            sweep(start1, start2, boxes[t ^ 1])
            sweep(start2, start3, boxes[t ^ 2])
            starts = (None, start1, start2, start3)
            for k in range(SLABS):
                begin = starts[max(t ^ k, 1)]
                for i in range(BLOCK // 8):
                    size = min(8, PART - 8 * i)
                    for g in range(TILES):
                        outs[k][pl.ds(8 * i, size), pl.ds(g * LANE, LANE)] = begin[g, pl.ds(PAD + 2 + 8 * i, size), :]


def fine_kernel(c_ref, s_ref, intra_ref, inter_ref, defect_ref, mine_ref, one_ref, two_ref, three_ref, new_ref, end_ref, one, two, force):
    slab, odd, up_mask, down_mask = place()
    lane_ids = lanes()
    base = PAD + REACH
    boxes = (mine_ref, one_ref, two_ref, three_ref)
    c_scale, s_scale = ADVECT, ADVECT * FORCE

    def fill(target, scale, top, main, bottom, offset):
        for g in range(TILES):
            cut = pl.ds(g * LANE, LANE)
            target[g, pl.ds(PAD, 8), :] = top[pl.ds(offset + HALO - 8, 8), cut] * (scale * up_mask)
            target[g, pl.ds(base + ROWS, 8), :] = bottom[pl.ds(offset, 8), cut] * (scale * down_mask)
            for i in range(ROWS // 8):
                target[g, pl.ds(base + 8 * i, 8), :] = main[pl.ds(8 * i, 8), cut] * scale

    @pl.when(odd == 1)
    def _():
        fill(force, s_scale, intra_ref, s_ref, inter_ref, HALO)

    @pl.when(odd == 0)
    def _():
        fill(force, s_scale, inter_ref, s_ref, intra_ref, HALO)

    @pl.when((slab == 0) & (odd == 1))
    def _():
        fill(one, c_scale, intra_ref, c_ref, inter_ref, 0)

    @pl.when((slab == 0) & (odd == 0))
    def _():
        fill(one, c_scale, inter_ref, c_ref, intra_ref, 0)

    for t in range(1, SLABS):
        @pl.when(slab == t)
        def _(t=t):
            for w in range(SLABS):
                for i in range(BLOCK // 8):
                    size = min(8, PART - 8 * i)
                    for g in range(TILES):
                        one[g, pl.ds(PAD + PART * w + 8 * i, size), :] = boxes[t ^ w][pl.ds(8 * i, size), pl.ds(g * LANE, LANE)]

    count = (ROWS + 2 * REACH) // 8

    def sweep(source, target, first):
        for i in range(count):
            at = PAD + 8 * i
            for g, now, above, below, left, right in row_tile(source, at, lane_ids):
                inc = increment(now, above, below, left, right, force[g, pl.ds(at, 8), :])
                new = now + inc
                if i == 0:
                    new = new * up_mask
                elif i == count - 1:
                    new = new * down_mask
                elif first:
                    cut = (pl.ds(8 * i - 8, 8), pl.ds(g * LANE, LANE))
                    new_ref[cut] = (now + 8.0 * inc + defect_ref[cut]) * (1.0 / ADVECT)
                target[g, pl.ds(at, 8), :] = new

    sweep(one, two, True)

    def pair(_, carry):
        sweep(two, one, False)
        sweep(one, two, False)
        return carry

    lax.fori_loop(0, STEPS // 2 - 1, pair, 0)
    for i in range(1, count - 1):
        at = PAD + 8 * i
        for g, now, above, below, left, right in row_tile(two, at, lane_ids):
            inc = increment(now, above, below, left, right, force[g, pl.ds(at, 8), :])
            end_ref[pl.ds(8 * i - 8, 8), pl.ds(g * LANE, LANE)] = (now + inc) * (1.0 / ADVECT)


def swap(array, axis, by):
    size = lax.axis_size(axis)
    return lax.ppermute(array, axis, [(i, i ^ by) for i in range(size)])


def call(kernel, outs, scratch):
    spec = pl.BlockSpec(memory_space=pltpu.VMEM)
    return pl.pallas_call(
        kernel,
        out_shape=[jax.ShapeDtypeStruct(shape, jnp.float32) for shape in outs],
        out_specs=[spec] * len(outs),
        scratch_shapes=[pltpu.VMEM(shape, jnp.float32) for shape in scratch],
        compiler_params=pltpu.CompilerParams(vmem_limit_bytes=32 * 1024 * 1024),
    )


def local(c_points, source):
    field = c_points[0]
    odd = lax.axis_index("space") % 2 == 1
    count = lax.axis_size("space")
    top = jnp.concatenate([field[:HALO], source[:HALO]])
    bottom = jnp.concatenate([field[-HALO:], source[-HALO:]])
    intra = swap(jnp.where(odd, top, bottom), "space", 1)
    across = [(i, (i + 1) % count) for i in range(1, count, 2)]
    inter = lax.ppermute(jnp.where(odd, bottom, top), "space", across + [(b, a) for a, b in across])

    wide = (TILES, ROWS + 2 * HALO + 2 * PAD, LANE)
    block = (BLOCK, COLS)
    defect, *boxes, force = call(
        defect_kernel,
        [(ROWS, COLS)] + [block] * 4 + [(TILES, BLOCK, LANE)],
        [wide] * 4,
    )(field, source, intra, inter)
    boxes = [boxes[0]] + [swap(boxes[k], "tm", k) for k in (1, 3, 2)]
    boxes = [boxes[0], boxes[1], boxes[3], boxes[2]]
    starts = call(
        chain_kernel, [(PART, COLS)] * 4, [(TILES, BLOCK + 2 * PAD, LANE)] * 3
    )(*boxes, force)
    starts = [starts[0]] + [swap(starts[k], "tm", k) for k in (1, 3, 2)]
    starts = [starts[0], starts[1], starts[3], starts[2]]
    middle = (TILES, ROWS + 2 * REACH + 2 * PAD, LANE)
    corrected, fine = call(
        fine_kernel, [(ROWS, COLS)] * 2, [middle] * 3
    )(field, source, intra, inter, defect, *starts)
    return corrected[None], fine[None]


def solution(mesh):
    return jax.shard_map(
        local,
        mesh=mesh,
        in_specs=(P("tm", "space", None), P("space", None)),
        out_specs=(P("tm", "space", None), P("tm", "space", None)),
        check_vma=False,
    )
```

time: 259 us -> 44.2 us (0.17)
  the two profiles are of different devices: /device:TPU:123 before, /device:TPU:158 now
where the time goes in v1:
time: 44.2 us; the launch traced here: 44.1 us
  waiting for transfers between devices  22.7 us (51%)
  starting transfers between devices  10.4 us (24%)
  Pallas kernels  8.22 us (19%)
  local copies, waits for them, and re-layouts  2.01 us (5%)
  between operations  0.7 us (2%)
    ppermute x7, waiting for transfers between devices, swap(): return lax.ppermute(array, axis, [(i, i ^ by) for i in range(size)])  18.4 us
    ppermute x7, starting transfers between devices, swap(): return lax.ppermute(array, axis, [(i, i ^ by) for i in range(size)])  10.2 us
    ppermute x1, waiting for transfers between devices, local(): lax.ppermute(jnp.where(odd, bottom, top), 'space', across + [(b, a) for a...  4.3 us
    pallas_call x1, Pallas kernels, local(): call(fine_kernel, [(ROWS, COLS)] * 2, [middle] * 3)  4.13 us
    pallas_call x1, Pallas kernels, local(): call(defect_kernel, [(ROWS, COLS)] + [block] * 4 + [(TILES, BLOCK, LANE)]...  3.76 us
    slice x2, local copies, waits for them, and re-layouts, local(): top = jnp.concatenate([field[:HALO], source[:HALO]])  2 us
  transfers between devices with their start and end apart: 8, of which 7 were waited for; matrix products, arithmetic and copies ran while one was open for 0% of the time, Pallas kernels for 0%

profile of v1, /device:TPU:158, one launch (start us, length us, event | category | flops | bytes accessed | tf_op | source)
XLA Modules:
  0.0 44.1 jit_solution(4894591866512103329)
XLA Ops:
  0.6 1.0 %slice_bitcast_fusion.1 = (f32[24,1024]{1,0:T(8,128)S(1)}, f32[24,1024]{1,0:T(8,128)S(1)}) fusion(f32[1,128,1024]{2,1,0:T(8,128)} %param.2), kind=kLoop, calls=%fused_computation.5 | loop fusion | bytes 393216 | tf_op jit(solution)/shard_map/slice | solution.py:265
  1.6 0.0 copy-start
  1.6 0.0 copy-start.1
  1.6 1.0 %fusion.2 = (f32[24,1024]{1,0:T(8,128)S(1)}, f32[24,1024]{1,0:T(8,128)S(1)}) fusion(f32[128,1024]{1,0:T(8,128)} %s_ref.3), kind=kLoop, calls=%fused_computation.6 | loop fusion | bytes 393216 | tf_op jit(solution)/shard_map/slice | solution.py:265
  2.7 0.3 collective-permute-start.1
  3.0 0.6 %collective-permute-start = (f32[48,1024]{1,0:T(8,128)S(1)}, f32[48,1024]{1,0:T(8,128)S(1)}, u32[]{:S(2)}, u32[]{:S(2)}) collective-permute-start(f32[48,1024]{1,0:T(8,128)S(1)} %get-tuple-element.31), channel_id=1, source_target_pairs={{0,1},{1,0},{2,3},{3,2},{4,5},{5,4},{6,7},{7,6},{8,9},{9,8},{10,11... | collective-permute-start | bytes 589832 | tf_op jit(solution)/shard_map/ppermute | solution.py:247
  3.6 4.3 %collective-permute-done.1.inter_ref = f32[48,1024]{1,0:T(8,128)S(1)} collective-permute-done((f32[48,1024]{1,0:T(8,128)S(1)}, f32[48,1024]{1,0:T(8,128)S(1)}, u32[]{:S(2)}, u32[]{:S(2)}) %collective-permute-start.1) | collective-permute-done | bytes 196640 | tf_op jit(solution)/shard_map/ppermute | solution.py:269
  7.9 0.0 collective-permute-done.intra_ref
  7.9 0.0 copy-done
  7.9 0.0 copy-done.1
  7.9 3.8 %shard_map.41 = (f32[128,1024]{1,0:T(8,128)S(1)}, f32[40,1024]{1,0:T(8,128)S(1)}, f32[40,1024]{1,0:T(8,128)S(1)}, f32[40,1024]{1,0:T(8,128)S(1)}, f32[40,1024]{1,0:T(8,128)S(1)}, /*index=5*/f32[8,40,128]{2,1,0:T(8,128)S(1)}) custom-call(f32[128,1024]{1,0:T(8,128)S(1)} %bitcast.7, f32[128,1024]{1,0:T(8,128)S(1)} %copy-done.1, ...), custom_call_target="tpu_custom_call" | custom-call | tf_op jit(solution)/shard_map/pallas_call | solution.py:273
  11.7 0.9 %collective-permute-start.2 = (f32[40,1024]{1,0:T(8,128)S(1)}, f32[40,1024]{1,0:T(8,128)S(1)}, u32[]{:S(2)}, u32[]{:S(2)}) collective-permute-start(f32[40,1024]{1,0:T(8,128)S(1)} %get-tuple-element.16), channel_id=1, source_target_pairs={{0,64},{64,0},{128,192},{192,128},{1,65},{65,1},{129,193},{193,129... | collective-permute-start | bytes 491528 | tf_op jit(solution)/shard_map/ppermute | solution.py:247
  12.6 1.1 %collective-permute-start.3 = (f32[40,1024]{1,0:T(8,128)S(1)}, f32[40,1024]{1,0:T(8,128)S(1)}, u32[]{:S(2)}, u32[]{:S(2)}) collective-permute-start(f32[40,1024]{1,0:T(8,128)S(1)} %get-tuple-element.17), channel_id=1, source_target_pairs={{0,128},{64,192},{128,0},{192,64},{1,129},{65,193},{129,1},{193,65... | collective-permute-start | bytes 491528 | tf_op jit(solution)/shard_map/ppermute | solution.py:247
  13.7 2.8 %collective-permute-start.4 = (f32[40,1024]{1,0:T(8,128)S(1)}, f32[40,1024]{1,0:T(8,128)S(1)}, u32[]{:S(2)}, u32[]{:S(2)}) collective-permute-start(f32[40,1024]{1,0:T(8,128)S(1)} %get-tuple-element.18), channel_id=1, source_target_pairs={{0,192},{64,128},{128,64},{192,0},{1,193},{65,129},{129,65},{193,1... | collective-permute-start | bytes 491528 | tf_op jit(solution)/shard_map/ppermute | solution.py:247
  16.5 1.4 %collective-permute-done.2.one_ref = f32[40,1024]{1,0:T(8,128)S(1)} collective-permute-done((f32[40,1024]{1,0:T(8,128)S(1)}, f32[40,1024]{1,0:T(8,128)S(1)}, u32[]{:S(2)}, u32[]{:S(2)}) %collective-permute-start.2) | collective-permute-done | bytes 163872 | tf_op jit(solution)/shard_map/ppermute | solution.py:247
  17.9 3.5 %collective-permute-done.3.two_ref = f32[40,1024]{1,0:T(8,128)S(1)} collective-permute-done((f32[40,1024]{1,0:T(8,128)S(1)}, f32[40,1024]{1,0:T(8,128)S(1)}, u32[]{:S(2)}, u32[]{:S(2)}) %collective-permute-start.3) | collective-permute-done | bytes 163872 | tf_op jit(solution)/shard_map/ppermute | solution.py:247
  21.4 3.6 %collective-permute-done.4.three_ref = f32[40,1024]{1,0:T(8,128)S(1)} collective-permute-done((f32[40,1024]{1,0:T(8,128)S(1)}, f32[40,1024]{1,0:T(8,128)S(1)}, u32[]{:S(2)}, u32[]{:S(2)}) %collective-permute-start.4) | collective-permute-done | bytes 163872 | tf_op jit(solution)/shard_map/ppermute | solution.py:247
  24.9 0.3 shard_map.42
  25.3 0.1 collective-permute-start.5
  25.4 4.2 %collective-permute-start.6 = (f32[36,1024]{1,0:T(8,128)S(1)}, f32[36,1024]{1,0:T(8,128)S(1)}, u32[]{:S(2)}, u32[]{:S(2)}) collective-permute-start(f32[36,1024]{1,0:T(8,128)S(1)} %get-tuple-element.22), channel_id=1, source_target_pairs={{0,128},{64,192},{128,0},{192,64},{1,129},{65,193},{129,1},{193,65... | collective-permute-start | bytes 442376 | tf_op jit(solution)/shard_map/ppermute | solution.py:247
  29.6 0.5 %collective-permute-start.7 = (f32[36,1024]{1,0:T(8,128)S(1)}, f32[36,1024]{1,0:T(8,128)S(1)}, u32[]{:S(2)}, u32[]{:S(2)}) collective-permute-start(f32[36,1024]{1,0:T(8,128)S(1)} %get-tuple-element.23), channel_id=1, source_target_pairs={{0,192},{64,128},{128,64},{192,0},{1,193},{65,129},{129,65},{193,1... | collective-permute-start | bytes 442376 | tf_op jit(solution)/shard_map/ppermute | solution.py:247
  30.1 2.3 %collective-permute-done.5.one_ref = f32[36,1024]{1,0:T(8,128)S(1)} collective-permute-done((f32[36,1024]{1,0:T(8,128)S(1)}, f32[36,1024]{1,0:T(8,128)S(1)}, u32[]{:S(2)}, u32[]{:S(2)}) %collective-permute-start.5) | collective-permute-done | bytes 147488 | tf_op jit(solution)/shard_map/ppermute | solution.py:247
  32.4 5.0 %collective-permute-done.6.two_ref = f32[36,1024]{1,0:T(8,128)S(1)} collective-permute-done((f32[36,1024]{1,0:T(8,128)S(1)}, f32[36,1024]{1,0:T(8,128)S(1)}, u32[]{:S(2)}, u32[]{:S(2)}) %collective-permute-start.6) | collective-permute-done | bytes 147488 | tf_op jit(solution)/shard_map/ppermute | solution.py:247
  37.4 2.6 %collective-permute-done.7.three_ref = f32[36,1024]{1,0:T(8,128)S(1)} collective-permute-done((f32[36,1024]{1,0:T(8,128)S(1)}, f32[36,1024]{1,0:T(8,128)S(1)}, u32[]{:S(2)}, u32[]{:S(2)}) %collective-permute-start.7) | collective-permute-done | bytes 147488 | tf_op jit(solution)/shard_map/ppermute | solution.py:247
  40.0 4.1 %shard_map.43 = (f32[128,1024]{1,0:T(8,128)}, f32[128,1024]{1,0:T(8,128)}) custom-call(f32[128,1024]{1,0:T(8,128)S(1)} %bitcast.8, f32[128,1024]{1,0:T(8,128)S(1)} %copy-done.1, f32[48,1024]{1,0:T(8,128)S(1)} %collective-permute-done.intra_ref, f32[48,1024]{1,0:T(8,128)S(1)} %collective-permute-done.1.inter_ref, ...), custom_call_target="tpu_custom_call" | custom-call | tf_op jit(solution)/shard_map/pallas_call | solution.py:286
  (1 shorter events, 0.0 us)
Async XLA Ops:
  1.6 6.3 %copy-start = (f32[1,128,1024]{2,1,0:T(8,128)S(1)}, f32[1,128,1024]{2,1,0:T(8,128)}, u32[]{:S(2)}) copy-start(f32[1,128,1024]{2,1,0:T(8,128)} %param.2) | copy-start | bytes 1572868
  1.6 6.3 %copy-start.1 = (f32[128,1024]{1,0:T(8,128)S(1)}, f32[128,1024]{1,0:T(8,128)}, u32[]{:S(2)}) copy-start(f32[128,1024]{1,0:T(8,128)} %s_ref.3) | copy-start | bytes 1572868
  2.7 5.2 %collective-permute-start.1 = (f32[48,1024]{1,0:T(8,128)S(1)}, f32[48,1024]{1,0:T(8,128)S(1)}, u32[]{:S(2)}, u32[]{:S(2)}) collective-permute-start(f32[48,1024]{1,0:T(8,128)S(1)} %get-tuple-element.30), channel_id=1, source_target_pairs={{1,2},{3,4},{5,6},{7,8},{9,10},{11,12},{13,14},{15,16},{17,18},{19... | collective-permute-start | bytes 589832 | tf_op jit(solution)/shard_map/ppermute | solution.py:269
  3.0 4.9 %collective-permute-start = (f32[48,1024]{1,0:T(8,128)S(1)}, f32[48,1024]{1,0:T(8,128)S(1)}, u32[]{:S(2)}, u32[]{:S(2)}) collective-permute-start(f32[48,1024]{1,0:T(8,128)S(1)} %get-tuple-element.31), channel_id=1, source_target_pairs={{0,1},{1,0},{2,3},{3,2},{4,5},{5,4},{6,7},{7,6},{8,9},{9,8},{10,11... | collective-permute-start | bytes 589832 | tf_op jit(solution)/shard_map/ppermute | solution.py:247
  11.7 6.2 %collective-permute-start.2 = (f32[40,1024]{1,0:T(8,128)S(1)}, f32[40,1024]{1,0:T(8,128)S(1)}, u32[]{:S(2)}, u32[]{:S(2)}) collective-permute-start(f32[40,1024]{1,0:T(8,128)S(1)} %get-tuple-element.16), channel_id=1, source_target_pairs={{0,64},{64,0},{128,192},{192,128},{1,65},{65,1},{129,193},{193,129... | collective-permute-start | bytes 491528 | tf_op jit(solution)/shard_map/ppermute | solution.py:247
  12.6 8.8 %collective-permute-start.3 = (f32[40,1024]{1,0:T(8,128)S(1)}, f32[40,1024]{1,0:T(8,128)S(1)}, u32[]{:S(2)}, u32[]{:S(2)}) collective-permute-start(f32[40,1024]{1,0:T(8,128)S(1)} %get-tuple-element.17), channel_id=1, source_target_pairs={{0,128},{64,192},{128,0},{192,64},{1,129},{65,193},{129,1},{193,65... | collective-permute-start | bytes 491528 | tf_op jit(solution)/shard_map/ppermute | solution.py:247
  13.7 11.2 %collective-permute-start.4 = (f32[40,1024]{1,0:T(8,128)S(1)}, f32[40,1024]{1,0:T(8,128)S(1)}, u32[]{:S(2)}, u32[]{:S(2)}) collective-permute-start(f32[40,1024]{1,0:T(8,128)S(1)} %get-tuple-element.18), channel_id=1, source_target_pairs={{0,192},{64,128},{128,64},{192,0},{1,193},{65,129},{129,65},{193,1... | collective-permute-start | bytes 491528 | tf_op jit(solution)/shard_map/ppermute | solution.py:247
  25.3 7.1 %collective-permute-start.5 = (f32[36,1024]{1,0:T(8,128)S(1)}, f32[36,1024]{1,0:T(8,128)S(1)}, u32[]{:S(2)}, u32[]{:S(2)}) collective-permute-start(f32[36,1024]{1,0:T(8,128)S(1)} %get-tuple-element.21), channel_id=1, source_target_pairs={{0,64},{64,0},{128,192},{192,128},{1,65},{65,1},{129,193},{193,129... | collective-permute-start | bytes 442376 | tf_op jit(solution)/shard_map/ppermute | solution.py:247
  25.4 12.0 %collective-permute-start.6 = (f32[36,1024]{1,0:T(8,128)S(1)}, f32[36,1024]{1,0:T(8,128)S(1)}, u32[]{:S(2)}, u32[]{:S(2)}) collective-permute-start(f32[36,1024]{1,0:T(8,128)S(1)} %get-tuple-element.22), channel_id=1, source_target_pairs={{0,128},{64,192},{128,0},{192,64},{1,129},{65,193},{129,1},{193,65... | collective-permute-start | bytes 442376 | tf_op jit(solution)/shard_map/ppermute | solution.py:247
  29.6 10.4 %collective-permute-start.7 = (f32[36,1024]{1,0:T(8,128)S(1)}, f32[36,1024]{1,0:T(8,128)S(1)}, u32[]{:S(2)}, u32[]{:S(2)}) collective-permute-start(f32[36,1024]{1,0:T(8,128)S(1)} %get-tuple-element.23), channel_id=1, source_target_pairs={{0,192},{64,128},{128,64},{192,0},{1,193},{65,129},{129,65},{193,1... | collective-permute-start | bytes 442376 | tf_op jit(solution)/shard_map/ppermute | solution.py:247

commit v2 on v1

v2 whole, which is shorter than its diff:
```python
import functools

import jax
import jax.numpy as jnp
from jax import lax
from jax.experimental import pallas as pl
from jax.experimental.pallas import tpu as pltpu
from jax.sharding import PartitionSpec as P

ADVECT = 0.02
DIFFUSE = 0.01
FORCE = 0.05
STEPS = 8
SLABS = 4
ROWS = 128
COLS = 1024
LANE = 128
TILES = COLS // LANE
HALO = 24
PAD = 8
REACH = STEPS
PART = (ROWS + 2 * REACH) // SLABS
BLOCK = PART + 4
FAR = REACH + 2
RIM = 2 * HALO
SIDE = RIM + 2 * PAD


ORDERS = ((0, 2, 1, 3), (0, 2, 3, 1))


def increment(now, above, below, left, right, force):
    twice = now + now
    rear = above + left - twice
    ahead = below + right - twice
    gain = jnp.maximum(now, 0.0) + DIFFUSE
    return force + gain * rear + (gain - now) * ahead


def row_tile(state, start, lane_ids):
    now = [state[g, pl.ds(start, 8), :] for g in range(TILES)]
    above = [state[g, pl.ds(start - 1, 8), :] for g in range(TILES)]
    below = [state[g, pl.ds(start + 1, 8), :] for g in range(TILES)]
    for g in range(TILES):
        left = pltpu.roll(jnp.where(lane_ids == LANE - 1, now[g - 1], now[g]), 1, 1)
        right = pltpu.roll(jnp.where(lane_ids == 0, now[(g + 1) % TILES], now[g]), LANE - 1, 1)
        yield g, now[g], above[g], below[g], left, right


def lanes():
    return lax.broadcasted_iota(jnp.int32, (8, LANE), 1)


def parity():
    return lax.axis_index("space") % 2


def place():
    slab = lax.axis_index("tm")
    strip = lax.axis_index("space")
    up_mask = jnp.where(strip == 0, 0.0, 1.0)
    down_mask = jnp.where(strip == lax.axis_size("space") - 1, 0.0, 1.0)
    return slab, strip % 2, up_mask, down_mask


def pack_kernel(c_ref, s_ref, intra_ref, inter_ref, sems):
    odd = parity()
    low = pl.multiple_of((ROWS - HALO) * odd, 8)
    high = pl.multiple_of((ROWS - HALO) * (1 - odd), 8)
    copies = []
    for n, (source, at) in enumerate(((c_ref.at[0], 0), (s_ref, HALO))):
        for m, (target, start) in enumerate(((inter_ref, low), (intra_ref, high))):
            copies.append(
                pltpu.make_async_copy(
                    source.at[pl.ds(start, HALO)], target.at[pl.ds(at, HALO)], sems.at[2 * n + m]
                )
            )
    for copy in copies:
        copy.start()
    for copy in copies:
        copy.wait()


def load(target, at, source, start, count, scale):
    for i in range(count):
        for g in range(TILES):
            target[g, pl.ds(at + 8 * i, 8), :] = source[pl.ds(start + 8 * i, 8), pl.ds(g * LANE, LANE)] * scale


def sweep(source, target, force, tiles, lane_ids, coarse=None, masks=None):
    for at in tiles:
        for g, now, above, below, left, right in row_tile(source, at, lane_ids):
            inc = increment(now, above, below, left, right, force[g, pl.ds(at, 8), :])
            new = now + inc
            if coarse is not None:
                coarse[g, pl.ds(at, 8), :] = now + 8.0 * inc
            if masks and at in masks:
                new = new * masks[at]
            target[g, pl.ds(at, 8), :] = new


def partner(place):
    first, second = ORDERS[0][place], ORDERS[1][place]
    return first if first == second else jnp.where(parity() == 0, first, second)


def inner_kernel(c_ref, s_ref, defect_ref, gift_ref, force_ref, one, two, coarse):
    slab = lax.axis_index("tm")
    lane_ids = lanes()
    count = ROWS // 8
    load(one, PAD, c_ref, 0, count, ADVECT)
    load(force_ref, PAD, s_ref, 0, count, ADVECT * FORCE)
    tiles = [PAD + 8 * i for i in range(count)]
    sweep(one, two, force_ref, tiles, lane_ids, coarse)
    sweep(two, one, force_ref, tiles, lane_ids)

    def pair(_, carry):
        sweep(one, two, force_ref, tiles, lane_ids)
        sweep(two, one, force_ref, tiles, lane_ids)
        return carry

    lax.fori_loop(0, STEPS // 2 - 1, pair, 0)
    first = jnp.where(slab == 0, 0.0, 1.0)
    for i in range(1, count - 1):
        rows = pl.ds(PAD + 8 * i, 8)
        for g in range(TILES):
            fine = one[g, rows, :]
            rough = coarse[g, rows, :]
            gift_ref[g, rows, :] = fine - first * rough
            defect_ref[pl.ds(8 * i, 8), pl.ds(g * LANE, LANE)] = fine - rough


def rim_kernel(c_ref, s_ref, intra_ref, inter_ref, inner_gift_ref, inner_force_ref, defect_ref, mine_ref, one_ref, two_ref, three_ref, block_ref, one, two, force, coarse, gift, wide_force):
    slab, odd, up_mask, down_mask = place()
    lane_ids = lanes()
    low, high = PAD, SIDE + PAD
    third = HALO // 8

    def fill(target, scale, top, main, bottom, offset):
        load(target, low, top, offset, third, scale * up_mask)
        load(target, low + HALO, main, 0, third, scale)
        load(target, high, main, ROWS - HALO, third, scale)
        load(target, high + HALO, bottom, offset, third, scale * down_mask)

    @pl.when(odd == 1)
    def _():
        fill(one, ADVECT, intra_ref, c_ref, inter_ref, 0)
        fill(force, ADVECT * FORCE, intra_ref, s_ref, inter_ref, HALO)

    @pl.when(odd == 0)
    def _():
        fill(one, ADVECT, inter_ref, c_ref, intra_ref, 0)
        fill(force, ADVECT * FORCE, inter_ref, s_ref, intra_ref, HALO)

    def tiles(first, last):
        upper = [low + 8 * i for i in range(first, last)]
        lower = [high + 8 * i for i in range(2 * third - last, 2 * third - first)]
        return upper + lower

    masks = {low + 8 * i: up_mask for i in range(third)}
    masks.update({high + HALO + 8 * i: down_mask for i in range(third)})
    sweep(one, two, force, tiles(0, 6), lane_ids, coarse, masks)
    sweep(two, one, force, tiles(1, 6), lane_ids, None, masks)
    sweep(one, two, force, tiles(1, 6), lane_ids, None, masks)
    sweep(two, one, force, tiles(1, 5), lane_ids, None, masks)

    def pair(_, carry):
        sweep(one, two, force, tiles(1, 5), lane_ids, None, masks)
        sweep(two, one, force, tiles(1, 5), lane_ids, None, masks)
        return carry

    lax.fori_loop(0, STEPS // 2 - 2, pair, 0)
    first = jnp.where(slab == 0, 0.0, 1.0)
    base = 2 * REACH
    for g in range(TILES):
        for i in range(1, ROWS // 8 - 1):
            gift[g, pl.ds(base + 8 * i, 8), :] = inner_gift_ref[g, pl.ds(PAD + 8 * i, 8), :]
        for i in range(ROWS // 8):
            wide_force[g, pl.ds(base + 8 * i, 8), :] = inner_force_ref[g, pl.ds(PAD + 8 * i, 8), :]
        for i in range(2):
            wide_force[g, pl.ds(8 * i, 8), :] = force[g, pl.ds(low + 8 + 8 * i, 8), :]
            wide_force[g, pl.ds(base + ROWS + 8 * i, 8), :] = force[g, pl.ds(high + HALO + 8 * i, 8), :]
    for n, at in enumerate([low + 8, low + 16, low + 24, high + 16, high + 24, high + 32]):
        rows = pl.ds(at, 8)
        place_at = 8 * n if n < 3 else base + ROWS - 8 + 8 * (n - 3)
        for g in range(TILES):
            fine = one[g, rows, :]
            rough = coarse[g, rows, :]
            if at in masks:
                rough = rough * masks[at]
            gift[g, pl.ds(place_at, 8), :] = fine - first * rough
            if at == low + HALO:
                defect_ref[pl.ds(0, 8), pl.ds(g * LANE, LANE)] = fine - rough
            if at == high + HALO - 8:
                defect_ref[pl.ds(8, 8), pl.ds(g * LANE, LANE)] = fine - rough
    for k, out in enumerate((mine_ref, one_ref, two_ref, three_ref)):
        start = base - FAR + PART * (slab ^ partner(k))
        for i in range(BLOCK // 8):
            for g in range(TILES):
                rows = pl.ds(start + 8 * i, 8)
                out[pl.ds(8 * i, 8), pl.ds(g * LANE, LANE)] = gift[g, rows, :]
                if k == 0:
                    block_ref[g, pl.ds(8 * i, 8), :] = wide_force[g, rows, :]


def each_place(slab, odd, body):
    for t in range(SLABS):
        for core in range(2):
            pl.when((slab == t) & (odd == core))(functools.partial(body, t, ORDERS[core]))


def chain_kernel(mine_ref, one_ref, two_ref, three_ref, force_ref, out0_ref, out1_ref, out2_ref, out3_ref, start1, start2, start3):
    slab, odd, up_mask, down_mask = place()
    lane_ids = lanes()
    boxes = (mine_ref, one_ref, two_ref, three_ref)
    outs = (out0_ref, out1_ref, out2_ref, out3_ref)
    row_ids = lax.broadcasted_iota(jnp.int32, (8, LANE), 0)
    origin = PART * slab - FAR

    def leap(source, target, defect):
        for i in range(BLOCK // 8):
            at = PAD + 8 * i
            row = row_ids + (origin + 8 * i)
            mask = jnp.where(row < 0, up_mask, jnp.where(row >= ROWS, down_mask, 1.0))
            for g, now, above, below, left, right in row_tile(source, at, lane_ids):
                inc = increment(now, above, below, left, right, force_ref[g, pl.ds(8 * i, 8), :])
                new = now + 8.0 * inc + defect[pl.ds(8 * i, 8), pl.ds(g * LANE, LANE)]
                target[g, pl.ds(at, 8), :] = new * mask

    def body(t, order):
        load(start1, PAD, boxes[order.index(t)], 0, BLOCK // 8, 1.0)
        leap(start1, start2, boxes[order.index(t ^ 1)])
        leap(start2, start3, boxes[order.index(t ^ 2)])
        starts = (None, start1, start2, start3)
        for k in range(SLABS):
            begin = starts[max(t ^ order[k], 1)]
            for i in range(BLOCK // 8):
                size = min(8, PART - 8 * i)
                for g in range(TILES):
                    outs[k][pl.ds(8 * i, size), pl.ds(g * LANE, LANE)] = begin[g, pl.ds(PAD + 2 + 8 * i, size), :]

    each_place(slab, odd, body)


def fine_kernel(c_ref, intra_ref, inter_ref, defect_ref, rim_defect_ref, inner_force_ref, mine_ref, one_ref, two_ref, three_ref, new_ref, end_ref, one, two, force):
    boxes = (mine_ref, one_ref, two_ref, three_ref)
    slab, odd, up_mask, down_mask = place()
    lane_ids = lanes()
    base = PAD + REACH
    last = base + ROWS

    def ends(target, scale, top, bottom, offset):
        load(target, PAD, top, offset + HALO - 8, 1, scale * up_mask)
        load(target, last, bottom, offset, 1, scale * down_mask)

    for g in range(TILES):
        for i in range(ROWS // 8):
            force[g, pl.ds(base + 8 * i, 8), :] = inner_force_ref[g, pl.ds(PAD + 8 * i, 8), :]

    @pl.when(odd == 1)
    def _():
        ends(force, ADVECT * FORCE, intra_ref, inter_ref, HALO)

    @pl.when(odd == 0)
    def _():
        ends(force, ADVECT * FORCE, inter_ref, intra_ref, HALO)

    @pl.when((slab == 0) & (odd == 1))
    def _():
        ends(one, ADVECT, intra_ref, inter_ref, 0)

    @pl.when((slab == 0) & (odd == 0))
    def _():
        ends(one, ADVECT, inter_ref, intra_ref, 0)

    @pl.when(slab == 0)
    def _():
        load(one, base, c_ref, 0, ROWS // 8, ADVECT)

    def body(t, order):
        for w in range(SLABS):
            source = boxes[order.index(t ^ w)]
            for i in range((PART + 7) // 8):
                size = min(8, PART - 8 * i)
                for g in range(TILES):
                    one[g, pl.ds(PAD + PART * w + 8 * i, size), :] = source[pl.ds(8 * i, size), pl.ds(g * LANE, LANE)]

    @pl.when(slab > 0)
    def _():
        each_place(slab, odd, body)

    tiles = [PAD + 8 * i for i in range((ROWS + 2 * REACH) // 8)]
    masks = {PAD: up_mask, last: down_mask}
    for at in tiles:
        for g, now, above, below, left, right in row_tile(one, at, lane_ids):
            inc = increment(now, above, below, left, right, force[g, pl.ds(at, 8), :])
            new = now + inc
            cut = pl.ds(g * LANE, LANE)
            if at in masks:
                new = new * masks[at]
            else:
                if at == base:
                    defect = rim_defect_ref[pl.ds(0, 8), cut]
                elif at == last - 8:
                    defect = rim_defect_ref[pl.ds(8, 8), cut]
                else:
                    defect = defect_ref[pl.ds(at - base, 8), cut]
                new_ref[pl.ds(at - base, 8), cut] = (now + 8.0 * inc + defect) * (1.0 / ADVECT)
            two[g, pl.ds(at, 8), :] = new

    def pair(_, carry):
        sweep(two, one, force, tiles, lane_ids, None, masks)
        sweep(one, two, force, tiles, lane_ids, None, masks)
        return carry

    lax.fori_loop(0, STEPS // 2 - 1, pair, 0)
    for at in tiles[1:-1]:
        for g, now, above, below, left, right in row_tile(two, at, lane_ids):
            inc = increment(now, above, below, left, right, force[g, pl.ds(at, 8), :])
            end_ref[pl.ds(at - base, 8), pl.ds(g * LANE, LANE)] = (now + inc) * (1.0 / ADVECT)


def swap(array, axis, by):
    size = lax.axis_size(axis)
    return lax.ppermute(array, axis, [(i, i ^ by) for i in range(size)])


def swap_all(boxes):
    count, width = lax.axis_size("tm"), lax.axis_size("space")
    received = [boxes[0]]
    for order in range(1, count):
        pairs = []
        for t in range(count):
            for strip in range(width):
                by = ORDERS[strip % 2][order]
                pairs.append((t * width + strip, (t ^ by) * width + strip))
        received.append(lax.ppermute(boxes[order], ("tm", "space"), pairs))
    return received


def call(kernel, outs, scratch):
    spec = pl.BlockSpec(memory_space=pltpu.VMEM)
    return pl.pallas_call(
        kernel,
        out_shape=[jax.ShapeDtypeStruct(shape, jnp.float32) for shape in outs],
        out_specs=[spec] * len(outs),
        scratch_shapes=[pltpu.VMEM(shape, jnp.float32) for shape in scratch],
        compiler_params=pltpu.CompilerParams(vmem_limit_bytes=24 * 1024 * 1024),
    )


def local(c_points, source):
    field = c_points[0]
    count = lax.axis_size("space")
    edges = jax.ShapeDtypeStruct((2 * HALO, COLS), jnp.float32)
    to_intra, to_inter = pl.pallas_call(
        pack_kernel,
        out_shape=[edges, edges],
        in_specs=[pl.BlockSpec(memory_space=pl.ANY)] * 2,
        out_specs=[pl.BlockSpec(memory_space=pltpu.VMEM)] * 2,
        scratch_shapes=[pltpu.SemaphoreType.DMA((4,))],
    )(c_points, source)
    pairs = []
    for t in range(lax.axis_size("tm")):
        for strip in range(count):
            if strip in (0, count - 1):
                mate = (t ^ 1) * count + strip
            else:
                mate = t * count + strip + (1 if strip % 2 else -1)
            pairs.append((t * count + strip, mate))
    inter = lax.ppermute(to_inter, ("tm", "space"), pairs)
    intra = swap(to_intra, "space", 1)

    wide = (TILES, ROWS + 2 * PAD, LANE)
    defect, gift, force = call(inner_kernel, [(ROWS, COLS), wide, wide], [wide] * 3)(field, source)
    narrow = (TILES, ROWS + 4 * REACH, LANE)
    rim_defect, *boxes, block_force = call(
        rim_kernel,
        [(16, COLS)] + [(BLOCK, COLS)] * 4 + [(TILES, BLOCK, LANE)],
        [(TILES, 2 * SIDE, LANE)] * 4 + [narrow] * 2,
    )(field, source, intra, inter, gift, force)
    starts = call(
        chain_kernel, [(PART, COLS)] * 4, [(TILES, BLOCK + 2 * PAD, LANE)] * 3
    )(*swap_all(boxes), block_force)
    middle = (TILES, ROWS + 2 * REACH + 2 * PAD, LANE)
    corrected, fine = call(fine_kernel, [(ROWS, COLS)] * 2, [middle] * 3)(
        field, intra, inter, defect, rim_defect, force, *swap_all(starts)
    )
    return corrected[None], fine[None]


def solution(mesh):
    return jax.shard_map(
        local,
        mesh=mesh,
        in_specs=(P("tm", "space", None), P("space", None)),
        out_specs=(P("tm", "space", None), P("tm", "space", None)),
        check_vma=False,
    )
```

time: 44.2 us -> 40 us (0.905)
  the two profiles are of different devices: /device:TPU:158 before, /device:TPU:1 now
where the time goes in v2:
time: 40 us; the launch traced here: 39.9 us
  waiting for transfers between devices  19.9 us (50%)
  Pallas kernels  10.5 us (26%)
  starting transfers between devices  8.8 us (22%)
  between operations  0.7 us (2%)
    ppermute x6, waiting for transfers between devices, swap_all(): received.append(lax.ppermute(boxes[order], ('tm', 'space'), pairs))  17 us
    ppermute x6, starting transfers between devices, swap_all(): received.append(lax.ppermute(boxes[order], ('tm', 'space'), pairs))  5.47 us
    pallas_call x1, Pallas kernels, local(): call(fine_kernel, [(ROWS, COLS)] * 2, [middle] * 3)  3.88 us
    ppermute x1, starting transfers between devices, swap(): return lax.ppermute(array, axis, [(i, i ^ by) for i in range(size)])  3.33 us
    ppermute x1, waiting for transfers between devices, local(): inter = lax.ppermute(to_inter, ('tm', 'space'), pairs)  2.93 us
    pallas_call x1, Pallas kernels, local(): call(inner_kernel, [(ROWS, COLS), wide, wide], [wide] * 3)(field, source)  2.62 us
    pallas_call x1, Pallas kernels, local(): pl.pallas_call(pack_kernel, out_shape=[edges, edges], in_specs=[pl.BlockS...  1.91 us
    pallas_call x1, Pallas kernels, local(): call(rim_kernel, [(16, COLS)] + [(BLOCK, COLS)] * 4 + [(TILES, BLOCK, LAN...  1.75 us
  transfers between devices with their start and end apart: 8, of which 5 were waited for; matrix products, arithmetic and copies ran while one was open for 0% of the time, Pallas kernels for 7%

profile of v2, /device:TPU:1, one launch (start us, length us, event | category | flops | bytes accessed | tf_op | source)
XLA Modules:
  0.0 39.9 jit_solution(15425234960039419764)
XLA Ops:
  0.6 0.0 copy-start.1
  0.6 0.0 copy-start
  0.6 1.9 %shard_map.41 = (f32[48,1024]{1,0:T(8,128)}, f32[48,1024]{1,0:T(8,128)}) custom-call(f32[1,128,1024]{2,1,0:T(8,128)} %c_ref.1, f32[128,1024]{1,0:T(8,128)} %s_ref.5), custom_call_target="tpu_custom_call" | custom-call | tf_op jit(solution)/shard_map/pallas_call | solution.py:356
  2.6 3.3 %collective-permute-start = (f32[48,1024]{1,0:T(8,128)}, f32[48,1024]{1,0:T(8,128)S(1)}, u32[]{:S(2)}, u32[]{:S(2)}) collective-permute-start(f32[48,1024]{1,0:T(8,128)} %get-tuple-element.19), channel_id=1, source_target_pairs={{0,1},{1,0},{2,3},{3,2},{4,5},{5,4},{6,7},{7,6},{8,9},{9,8},{10,11... | collective-permute-start | bytes 589832 | tf_op jit(solution)/shard_map/ppermute | solution.py:325
  5.9 0.0 collective-permute-start.1
  5.9 0.0 copy-done.1
  5.9 0.0 copy-done
  5.9 2.6 %shard_map.42 = (f32[128,1024]{1,0:T(8,128)S(1)}, f32[8,144,128]{2,1,0:T(8,128)S(1)}, f32[8,144,128]{2,1,0:T(8,128)S(1)}) custom-call(f32[128,1024]{1,0:T(8,128)S(1)} %bitcast.3, f32[128,1024]{1,0:T(8,128)S(1)} %copy-done.1), custom_call_target="tpu_custom_call" | custom-call | tf_op jit(solution)/shard_map/pallas_call | solution.py:375
  8.5 0.0 collective-permute-done.intra_ref
  8.5 2.9 %collective-permute-done.1.inter_ref = f32[48,1024]{1,0:T(8,128)S(1)} collective-permute-done((f32[48,1024]{1,0:T(8,128)}, f32[48,1024]{1,0:T(8,128)S(1)}, u32[]{:S(2)}, u32[]{:S(2)}) %collective-permute-start.1) | collective-permute-done | bytes 196640 | tf_op jit(solution)/shard_map/ppermute | solution.py:371
  11.5 1.8 %shard_map.43 = (f32[16,1024]{1,0:T(8,128)S(1)}, f32[40,1024]{1,0:T(8,128)S(1)}, f32[40,1024]{1,0:T(8,128)S(1)}, f32[40,1024]{1,0:T(8,128)S(1)}, f32[40,1024]{1,0:T(8,128)S(1)}, /*index=5*/f32[8,40,128]{2,1,0:T(8,128)S(1)}) custom-call(f32[128,1024]{1,0:T(8,128)S(1)} %bitcast.4, f32[128,1024]{1,0:T(8,128)S(1)} %copy-done.1, ...), custom_call_target="tpu_custom_call" | custom-call | tf_op jit(solution)/shard_map/pallas_call | solution.py:377
  13.2 1.1 %collective-permute-start.2 = (f32[40,1024]{1,0:T(8,128)S(1)}, f32[40,1024]{1,0:T(8,128)S(1)}, u32[]{:S(2)}, u32[]{:S(2)}) collective-permute-start(f32[40,1024]{1,0:T(8,128)S(1)} %get-tuple-element.26), channel_id=1, source_target_pairs={{0,128},{1,129},{2,130},{3,131},{4,132},{5,133},{6,134},{7,135},{8... | collective-permute-start | bytes 491528 | tf_op jit(solution)/shard_map/ppermute | solution.py:337
  14.3 0.9 %collective-permute-start.3 = (f32[40,1024]{1,0:T(8,128)S(1)}, f32[40,1024]{1,0:T(8,128)S(1)}, u32[]{:S(2)}, u32[]{:S(2)}) collective-permute-start(f32[40,1024]{1,0:T(8,128)S(1)} %get-tuple-element.27), channel_id=1, source_target_pairs={{0,64},{1,193},{2,66},{3,195},{4,68},{5,197},{6,70},{7,199},{8,72}... | collective-permute-start | bytes 491528 | tf_op jit(solution)/shard_map/ppermute | solution.py:337
  15.2 0.8 %collective-permute-start.4 = (f32[40,1024]{1,0:T(8,128)S(1)}, f32[40,1024]{1,0:T(8,128)S(1)}, u32[]{:S(2)}, u32[]{:S(2)}) collective-permute-start(f32[40,1024]{1,0:T(8,128)S(1)} %get-tuple-element.28), channel_id=1, source_target_pairs={{0,192},{1,65},{2,194},{3,67},{4,196},{5,69},{6,198},{7,71},{8,200... | collective-permute-start | bytes 491528 | tf_op jit(solution)/shard_map/ppermute | solution.py:337
  16.0 4.3 %collective-permute-done.2.one_ref = f32[40,1024]{1,0:T(8,128)S(1)} collective-permute-done((f32[40,1024]{1,0:T(8,128)S(1)}, f32[40,1024]{1,0:T(8,128)S(1)}, u32[]{:S(2)}, u32[]{:S(2)}) %collective-permute-start.2) | collective-permute-done | bytes 163872 | tf_op jit(solution)/shard_map/ppermute | solution.py:337
  20.3 4.2 %collective-permute-done.3.two_ref = f32[40,1024]{1,0:T(8,128)S(1)} collective-permute-done((f32[40,1024]{1,0:T(8,128)S(1)}, f32[40,1024]{1,0:T(8,128)S(1)}, u32[]{:S(2)}, u32[]{:S(2)}) %collective-permute-start.3) | collective-permute-done | bytes 163872 | tf_op jit(solution)/shard_map/ppermute | solution.py:337
  24.5 0.0 collective-permute-done.4.three_ref
  24.5 0.4 shard_map.44
  24.8 1.1 %collective-permute-start.5 = (f32[36,1024]{1,0:T(8,128)S(1)}, f32[36,1024]{1,0:T(8,128)S(1)}, u32[]{:S(2)}, u32[]{:S(2)}) collective-permute-start(f32[36,1024]{1,0:T(8,128)S(1)} %get-tuple-element.31), channel_id=1, source_target_pairs={{0,128},{1,129},{2,130},{3,131},{4,132},{5,133},{6,134},{7,135},{8... | collective-permute-start | bytes 442376 | tf_op jit(solution)/shard_map/ppermute | solution.py:337
  25.9 0.7 %collective-permute-start.6 = (f32[36,1024]{1,0:T(8,128)S(1)}, f32[36,1024]{1,0:T(8,128)S(1)}, u32[]{:S(2)}, u32[]{:S(2)}) collective-permute-start(f32[36,1024]{1,0:T(8,128)S(1)} %get-tuple-element.32), channel_id=1, source_target_pairs={{0,64},{1,193},{2,66},{3,195},{4,68},{5,197},{6,70},{7,199},{8,72}... | collective-permute-start | bytes 442376 | tf_op jit(solution)/shard_map/ppermute | solution.py:337
  26.6 0.9 %collective-permute-start.7 = (f32[36,1024]{1,0:T(8,128)S(1)}, f32[36,1024]{1,0:T(8,128)S(1)}, u32[]{:S(2)}, u32[]{:S(2)}) collective-permute-start(f32[36,1024]{1,0:T(8,128)S(1)} %get-tuple-element.33), channel_id=1, source_target_pairs={{0,192},{1,65},{2,194},{3,67},{4,196},{5,69},{6,198},{7,71},{8,200... | collective-permute-start | bytes 442376 | tf_op jit(solution)/shard_map/ppermute | solution.py:337
  27.6 4.2 %collective-permute-done.5.one_ref = f32[36,1024]{1,0:T(8,128)S(1)} collective-permute-done((f32[36,1024]{1,0:T(8,128)S(1)}, f32[36,1024]{1,0:T(8,128)S(1)}, u32[]{:S(2)}, u32[]{:S(2)}) %collective-permute-start.5) | collective-permute-done | bytes 147488 | tf_op jit(solution)/shard_map/ppermute | solution.py:337
  31.7 4.3 %collective-permute-done.6.two_ref = f32[36,1024]{1,0:T(8,128)S(1)} collective-permute-done((f32[36,1024]{1,0:T(8,128)S(1)}, f32[36,1024]{1,0:T(8,128)S(1)}, u32[]{:S(2)}, u32[]{:S(2)}) %collective-permute-start.6) | collective-permute-done | bytes 147488 | tf_op jit(solution)/shard_map/ppermute | solution.py:337
  36.1 0.0 collective-permute-done.7.three_ref
  36.1 3.9 %shard_map.45 = (f32[128,1024]{1,0:T(8,128)}, f32[128,1024]{1,0:T(8,128)}) custom-call(f32[128,1024]{1,0:T(8,128)S(1)} %bitcast.5, f32[48,1024]{1,0:T(8,128)S(1)} %collective-permute-done.intra_ref, f32[48,1024]{1,0:T(8,128)S(1)} %collective-permute-done.1.inter_ref, f32[128,1024]{1,0:T(8,128)S(1)} %get-tuple-element.21.defect_ref, ...), custom_call_target="tpu_custom_call" | custom-call | tf_op jit(solution)/shard_map/pallas_call | solution.py:386
Async XLA Ops:
  0.6 5.3 %copy-start.1 = (f32[128,1024]{1,0:T(8,128)S(1)}, f32[128,1024]{1,0:T(8,128)}, u32[]{:S(2)}) copy-start(f32[128,1024]{1,0:T(8,128)} %s_ref.5) | copy-start | bytes 1572868
  0.6 5.3 %copy-start = (f32[1,128,1024]{2,1,0:T(8,128)S(1)}, f32[1,128,1024]{2,1,0:T(8,128)}, u32[]{:S(2)}) copy-start(f32[1,128,1024]{2,1,0:T(8,128)} %c_ref.1) | copy-start | bytes 1572868
  2.6 6.0 %collective-permute-start = (f32[48,1024]{1,0:T(8,128)}, f32[48,1024]{1,0:T(8,128)S(1)}, u32[]{:S(2)}, u32[]{:S(2)}) collective-permute-start(f32[48,1024]{1,0:T(8,128)} %get-tuple-element.19), channel_id=1, source_target_pairs={{0,1},{1,0},{2,3},{3,2},{4,5},{5,4},{6,7},{7,6},{8,9},{9,8},{10,11... | collective-permute-start | bytes 589832 | tf_op jit(solution)/shard_map/ppermute | solution.py:325
  5.9 5.6 %collective-permute-start.1 = (f32[48,1024]{1,0:T(8,128)}, f32[48,1024]{1,0:T(8,128)S(1)}, u32[]{:S(2)}, u32[]{:S(2)}) collective-permute-start(f32[48,1024]{1,0:T(8,128)} %get-tuple-element.20), channel_id=1, source_target_pairs={{0,64},{1,2},{2,1},{3,4},{4,3},{5,6},{6,5},{7,8},{8,7},{9,10},{10,... | collective-permute-start | bytes 589832 | tf_op jit(solution)/shard_map/ppermute | solution.py:371
  13.2 7.0 %collective-permute-start.2 = (f32[40,1024]{1,0:T(8,128)S(1)}, f32[40,1024]{1,0:T(8,128)S(1)}, u32[]{:S(2)}, u32[]{:S(2)}) collective-permute-start(f32[40,1024]{1,0:T(8,128)S(1)} %get-tuple-element.26), channel_id=1, source_target_pairs={{0,128},{1,129},{2,130},{3,131},{4,132},{5,133},{6,134},{7,135},{8... | collective-permute-start | bytes 491528 | tf_op jit(solution)/shard_map/ppermute | solution.py:337
  14.3 10.1 %collective-permute-start.3 = (f32[40,1024]{1,0:T(8,128)S(1)}, f32[40,1024]{1,0:T(8,128)S(1)}, u32[]{:S(2)}, u32[]{:S(2)}) collective-permute-start(f32[40,1024]{1,0:T(8,128)S(1)} %get-tuple-element.27), channel_id=1, source_target_pairs={{0,64},{1,193},{2,66},{3,195},{4,68},{5,197},{6,70},{7,199},{8,72}... | collective-permute-start | bytes 491528 | tf_op jit(solution)/shard_map/ppermute | solution.py:337
  15.2 9.3 %collective-permute-start.4 = (f32[40,1024]{1,0:T(8,128)S(1)}, f32[40,1024]{1,0:T(8,128)S(1)}, u32[]{:S(2)}, u32[]{:S(2)}) collective-permute-start(f32[40,1024]{1,0:T(8,128)S(1)} %get-tuple-element.28), channel_id=1, source_target_pairs={{0,192},{1,65},{2,194},{3,67},{4,196},{5,69},{6,198},{7,71},{8,200... | collective-permute-start | bytes 491528 | tf_op jit(solution)/shard_map/ppermute | solution.py:337
  24.8 6.9 %collective-permute-start.5 = (f32[36,1024]{1,0:T(8,128)S(1)}, f32[36,1024]{1,0:T(8,128)S(1)}, u32[]{:S(2)}, u32[]{:S(2)}) collective-permute-start(f32[36,1024]{1,0:T(8,128)S(1)} %get-tuple-element.31), channel_id=1, source_target_pairs={{0,128},{1,129},{2,130},{3,131},{4,132},{5,133},{6,134},{7,135},{8... | collective-permute-start | bytes 442376 | tf_op jit(solution)/shard_map/ppermute | solution.py:337
  25.9 10.1 %collective-permute-start.6 = (f32[36,1024]{1,0:T(8,128)S(1)}, f32[36,1024]{1,0:T(8,128)S(1)}, u32[]{:S(2)}, u32[]{:S(2)}) collective-permute-start(f32[36,1024]{1,0:T(8,128)S(1)} %get-tuple-element.32), channel_id=1, source_target_pairs={{0,64},{1,193},{2,66},{3,195},{4,68},{5,197},{6,70},{7,199},{8,72}... | collective-permute-start | bytes 442376 | tf_op jit(solution)/shard_map/ppermute | solution.py:337
  26.6 9.4 %collective-permute-start.7 = (f32[36,1024]{1,0:T(8,128)S(1)}, f32[36,1024]{1,0:T(8,128)S(1)}, u32[]{:S(2)}, u32[]{:S(2)}) collective-permute-start(f32[36,1024]{1,0:T(8,128)S(1)} %get-tuple-element.33), channel_id=1, source_target_pairs={{0,192},{1,65},{2,194},{3,67},{4,196},{5,69},{6,198},{7,71},{8,200... | collective-permute-start | bytes 442376 | tf_op jit(solution)/shard_map/ppermute | solution.py:337

commit v3 on v2

--- a/solution.py
+++ b/solution.py
@@ -21,7 +21,12 @@
 REACH = STEPS
 PART = (ROWS + 2 * REACH) // SLABS
 BLOCK = PART + 4
+BOX = 48
+FAR_BOX = 48
+PIECE = BOX // 2
+EDGE = PART // 2
 FAR = REACH + 2
+RIM_SLAB = 1
 RIM = 2 * HALO
 SIDE = RIM + 2 * PAD
 
@@ -104,7 +109,11 @@
     return first if first == second else jnp.where(parity() == 0, first, second)
 
 
-def inner_kernel(c_ref, s_ref, defect_ref, gift_ref, force_ref, one, two, coarse):
+def inner_start(worker):
+    return REACH + PART * jnp.where(worker > RIM_SLAB, worker - 1, jnp.where(worker == RIM_SLAB, 0, worker))
+
+
+def inner_kernel(c_ref, s_ref, defect_ref, gift_ref, force_ref, far_ref, one, two, coarse):
     slab = lax.axis_index("tm")
     lane_ids = lanes()
     count = ROWS // 8
@@ -128,9 +137,13 @@
             rough = coarse[g, rows, :]
             gift_ref[g, rows, :] = fine - first * rough
             defect_ref[pl.ds(8 * i, 8), pl.ds(g * LANE, LANE)] = fine - rough
-
-
-def rim_kernel(c_ref, s_ref, intra_ref, inter_ref, inner_gift_ref, inner_force_ref, defect_ref, mine_ref, one_ref, two_ref, three_ref, block_ref, one, two, force, coarse, gift, wide_force):
+    start = PAD + inner_start(slab ^ 2)
+    for i in range(FAR_BOX // 8):
+        for g in range(TILES):
+            far_ref[pl.ds(8 * i, 8), pl.ds(g * LANE, LANE)] = gift_ref[g, pl.ds(start + 8 * i, 8), :]
+
+
+def rim_kernel(c_ref, s_ref, intra_ref, inter_ref, inner_gift_ref, inner_force_ref, defect_ref, mine_ref, one_ref, two_ref, block_ref, one, two, force, coarse, gift, wide_force):
     slab, odd, up_mask, down_mask = place()
     lane_ids = lanes()
     low, high = PAD, SIDE + PAD
@@ -193,14 +206,32 @@
                 defect_ref[pl.ds(0, 8), pl.ds(g * LANE, LANE)] = fine - rough
             if at == high + HALO - 8:
                 defect_ref[pl.ds(8, 8), pl.ds(g * LANE, LANE)] = fine - rough
-    for k, out in enumerate((mine_ref, one_ref, two_ref, three_ref)):
-        start = base - FAR + PART * (slab ^ partner(k))
-        for i in range(BLOCK // 8):
-            for g in range(TILES):
-                rows = pl.ds(start + 8 * i, 8)
-                out[pl.ds(8 * i, 8), pl.ds(g * LANE, LANE)] = gift[g, rows, :]
-                if k == 0:
-                    block_ref[g, pl.ds(8 * i, 8), :] = wide_force[g, rows, :]
+    for order, out in ((0, mine_ref), (2, one_ref), (3, two_ref)):
+        worker = slab ^ partner(order)
+
+        def cut(out, source, starts):
+            for i in range(BOX // 8):
+                at = starts[0] + 8 * i if i < PIECE // 8 else starts[1] + 8 * i - PIECE
+                for g in range(TILES):
+                    piece = source[g, pl.ds(at, 8), :]
+                    if len(out.shape) == 3:
+                        out[g, pl.ds(8 * i, 8), :] = piece
+                    else:
+                        out[pl.ds(8 * i, 8), pl.ds(g * LANE, LANE)] = piece
+
+        def cut_all(starts, order=order, out=out):
+            cut(out, gift, starts)
+            if order == 0:
+                cut(block_ref, wide_force, starts)
+
+        @pl.when(worker == RIM_SLAB)
+        def _(cut_all=cut_all):
+            cut_all((base - FAR, base + ROWS + FAR - PIECE))
+
+        @pl.when(worker != RIM_SLAB)
+        def _(cut_all=cut_all, worker=worker):
+            start = base + inner_start(worker)
+            cut_all((start, start + PIECE))
 
 
 def each_place(slab, odd, body):
@@ -215,29 +246,35 @@
     boxes = (mine_ref, one_ref, two_ref, three_ref)
     outs = (out0_ref, out1_ref, out2_ref, out3_ref)
     row_ids = lax.broadcasted_iota(jnp.int32, (8, LANE), 0)
-    origin = PART * slab - FAR
-
-    def leap(source, target, defect):
-        for i in range(BLOCK // 8):
+    masks = {
+        0: up_mask,
+        1: jnp.where(row_ids < FAR - 8, up_mask, 1.0),
+        4: jnp.where(row_ids >= 8 - (FAR - 8), down_mask, 1.0),
+        5: down_mask,
+    }
+
+    def leap(source, target, defect, rim):
+        for i in range((BOX if rim else BLOCK) // 8):
             at = PAD + 8 * i
-            row = row_ids + (origin + 8 * i)
-            mask = jnp.where(row < 0, up_mask, jnp.where(row >= ROWS, down_mask, 1.0))
             for g, now, above, below, left, right in row_tile(source, at, lane_ids):
                 inc = increment(now, above, below, left, right, force_ref[g, pl.ds(8 * i, 8), :])
                 new = now + 8.0 * inc + defect[pl.ds(8 * i, 8), pl.ds(g * LANE, LANE)]
-                target[g, pl.ds(at, 8), :] = new * mask
+                target[g, pl.ds(at, 8), :] = new * masks[i] if rim and i in masks else new
 
     def body(t, order):
-        load(start1, PAD, boxes[order.index(t)], 0, BLOCK // 8, 1.0)
-        leap(start1, start2, boxes[order.index(t ^ 1)])
-        leap(start2, start3, boxes[order.index(t ^ 2)])
+        rim = t == RIM_SLAB
+        load(start1, PAD, boxes[order.index(t)], 0, (BOX if rim else BLOCK) // 8, 1.0)
+        leap(start1, start2, boxes[order.index(t ^ 1)], rim)
+        leap(start2, start3, boxes[order.index(t ^ 2)], rim)
         starts = (None, start1, start2, start3)
+        pieces = ((0, 2, EDGE), (EDGE, BOX - 2 - EDGE, EDGE)) if rim else ((0, 2, PART),)
         for k in range(SLABS):
             begin = starts[max(t ^ order[k], 1)]
-            for i in range(BLOCK // 8):
-                size = min(8, PART - 8 * i)
-                for g in range(TILES):
-                    outs[k][pl.ds(8 * i, size), pl.ds(g * LANE, LANE)] = begin[g, pl.ds(PAD + 2 + 8 * i, size), :]
+            for to, at, rows in pieces:
+                for i in range((rows + 7) // 8):
+                    size = min(8, rows - 8 * i)
+                    for g in range(TILES):
+                        outs[k][pl.ds(to + 8 * i, size), pl.ds(g * LANE, LANE)] = begin[g, pl.ds(PAD + at + 8 * i, size), :]
 
     each_place(slab, odd, body)
 
@@ -280,10 +317,15 @@
     def body(t, order):
         for w in range(SLABS):
             source = boxes[order.index(t ^ w)]
-            for i in range((PART + 7) // 8):
-                size = min(8, PART - 8 * i)
-                for g in range(TILES):
-                    one[g, pl.ds(PAD + PART * w + 8 * i, size), :] = source[pl.ds(8 * i, size), pl.ds(g * LANE, LANE)]
+            if w == RIM_SLAB:
+                pieces = ((0, -REACH, EDGE), (EDGE, ROWS + REACH - EDGE, EDGE))
+            else:
+                pieces = ((0, EDGE - REACH + PART * (w - (w > RIM_SLAB)), PART),)
+            for begin, row, rows in pieces:
+                for i in range((rows + 7) // 8):
+                    size = min(8, rows - 8 * i)
+                    for g in range(TILES):
+                        one[g, pl.ds(base + row + 8 * i, size), :] = source[pl.ds(begin + 8 * i, size), pl.ds(g * LANE, LANE)]
 
     @pl.when(slab > 0)
     def _():
@@ -325,17 +367,14 @@
     return lax.ppermute(array, axis, [(i, i ^ by) for i in range(size)])
 
 
-def swap_all(boxes):
+def swap_one(box, order):
     count, width = lax.axis_size("tm"), lax.axis_size("space")
-    received = [boxes[0]]
-    for order in range(1, count):
-        pairs = []
-        for t in range(count):
-            for strip in range(width):
-                by = ORDERS[strip % 2][order]
-                pairs.append((t * width + strip, (t ^ by) * width + strip))
-        received.append(lax.ppermute(boxes[order], ("tm", "space"), pairs))
-    return received
+    pairs = []
+    for t in range(count):
+        for strip in range(width):
+            by = ORDERS[strip % 2][order]
+            pairs.append((t * width + strip, (t ^ by) * width + strip))
+    return lax.ppermute(box, ("tm", "space"), pairs)
 
 
 def call(kernel, outs, scratch):
@@ -372,19 +411,24 @@
     intra = swap(to_intra, "space", 1)
 
     wide = (TILES, ROWS + 2 * PAD, LANE)
-    defect, gift, force = call(inner_kernel, [(ROWS, COLS), wide, wide], [wide] * 3)(field, source)
+    defect, gift, force, far = call(
+        inner_kernel, [(ROWS, COLS), wide, wide, (FAR_BOX, COLS)], [wide] * 3
+    )(field, source)
+    far = swap_one(far, 1)
     narrow = (TILES, ROWS + 4 * REACH, LANE)
-    rim_defect, *boxes, block_force = call(
+    rim_defect, mine, one, two, block_force = call(
         rim_kernel,
-        [(16, COLS)] + [(BLOCK, COLS)] * 4 + [(TILES, BLOCK, LANE)],
+        [(16, COLS)] + [(BOX, COLS)] * 3 + [(TILES, BOX, LANE)],
         [(TILES, 2 * SIDE, LANE)] * 4 + [narrow] * 2,
     )(field, source, intra, inter, gift, force)
+    one, two = swap_one(one, 2), swap_one(two, 3)
     starts = call(
-        chain_kernel, [(PART, COLS)] * 4, [(TILES, BLOCK + 2 * PAD, LANE)] * 3
-    )(*swap_all(boxes), block_force)
+        chain_kernel, [(PART, COLS)] * 4, [(TILES, BOX + 2 * PAD, LANE)] * 3
+    )(mine, far, one, two, block_force)
+    starts = [starts[0]] + [swap_one(starts[order], order) for order in range(1, SLABS)]
     middle = (TILES, ROWS + 2 * REACH + 2 * PAD, LANE)
     corrected, fine = call(fine_kernel, [(ROWS, COLS)] * 2, [middle] * 3)(
-        field, intra, inter, defect, rim_defect, force, *swap_all(starts)
+        field, intra, inter, defect, rim_defect, force, *starts
     )
     return corrected[None], fine[None]
 

time: 40 us -> 36.4 us (0.910)
  the two profiles are of different devices: /device:TPU:1 before, /device:TPU:121 now
where the time goes in v3:
time: 36.4 us; the launch traced here: 36.3 us
  waiting for transfers between devices  13.4 us (37%)
  starting transfers between devices  11.7 us (32%)
  Pallas kernels  10.5 us (29%)
  between operations  0.69 us (2%)
    ppermute x6, waiting for transfers between devices, swap_one(): return lax.ppermute(box, ('tm', 'space'), pairs)  12.7 us
    ppermute x6, starting transfers between devices, swap_one(): return lax.ppermute(box, ('tm', 'space'), pairs)  8.43 us
    pallas_call x1, Pallas kernels, local(): call(fine_kernel, [(ROWS, COLS)] * 2, [middle] * 3)  3.88 us
    pallas_call x1, Pallas kernels, local(): call(inner_kernel, [(ROWS, COLS), wide, wide, (FAR_BOX, COLS)], [wide] * 3)  2.63 us
    ppermute x1, starting transfers between devices, local(): inter = lax.ppermute(to_inter, ('tm', 'space'), pairs)  2.49 us
    pallas_call x1, Pallas kernels, local(): pl.pallas_call(pack_kernel, out_shape=[edges, edges], in_specs=[pl.BlockS...  1.91 us
    pallas_call x1, Pallas kernels, local(): call(rim_kernel, [(16, COLS)] + [(BOX, COLS)] * 3 + [(TILES, BOX, LANE)],...  1.76 us
    ppermute x1, starting transfers between devices, swap(): return lax.ppermute(array, axis, [(i, i ^ by) for i in range(size)])  0.76 us
  transfers between devices with their start and end apart: 8, of which 5 were waited for; matrix products, arithmetic and copies ran while one was open for 0% of the time, Pallas kernels for 12%

profile of v3, /device:TPU:121, one launch (start us, length us, event | category | flops | bytes accessed | tf_op | source)
XLA Modules:
  0.0 36.3 jit_solution(4921988176566729200)
XLA Ops:
  0.6 0.0 copy-start.1
  0.6 0.0 copy-start
  0.6 1.9 %shard_map.41 = (f32[48,1024]{1,0:T(8,128)}, f32[48,1024]{1,0:T(8,128)}) custom-call(f32[1,128,1024]{2,1,0:T(8,128)} %c_ref.1, f32[128,1024]{1,0:T(8,128)} %s_ref.5), custom_call_target="tpu_custom_call" | custom-call | tf_op jit(solution)/shard_map/pallas_call | solution.py:395
  2.6 0.8 %collective-permute-start = (f32[48,1024]{1,0:T(8,128)}, f32[48,1024]{1,0:T(8,128)S(1)}, u32[]{:S(2)}, u32[]{:S(2)}) collective-permute-start(f32[48,1024]{1,0:T(8,128)} %get-tuple-element.19), channel_id=1, source_target_pairs={{0,1},{1,0},{2,3},{3,2},{4,5},{5,4},{6,7},{7,6},{8,9},{9,8},{10,11... | collective-permute-start | bytes 589832 | tf_op jit(solution)/shard_map/ppermute | solution.py:367
  3.3 2.5 %collective-permute-start.1 = (f32[48,1024]{1,0:T(8,128)}, f32[48,1024]{1,0:T(8,128)S(1)}, u32[]{:S(2)}, u32[]{:S(2)}) collective-permute-start(f32[48,1024]{1,0:T(8,128)} %get-tuple-element.20), channel_id=1, source_target_pairs={{0,64},{1,2},{2,1},{3,4},{4,3},{5,6},{6,5},{7,8},{8,7},{9,10},{10,... | collective-permute-start | bytes 589832 | tf_op jit(solution)/shard_map/ppermute | solution.py:410
  5.8 0.0 copy-done.1
  5.8 0.0 copy-done
  5.8 2.6 %shard_map.42 = (f32[128,1024]{1,0:T(8,128)S(1)}, f32[8,144,128]{2,1,0:T(8,128)S(1)}, f32[8,144,128]{2,1,0:T(8,128)S(1)}, f32[48,1024]{1,0:T(8,128)S(1)}) custom-call(f32[128,1024]{1,0:T(8,128)S(1)} %bitcast.3, f32[128,1024]{1,0:T(8,128)S(1)} %copy-done.1), custom_call_target="tpu_custom_call" | custom-call | tf_op jit(solution)/shard_map/pallas_call | solution.py:414
  8.5 2.8 %collective-permute-start.2 = (f32[48,1024]{1,0:T(8,128)S(1)}, f32[48,1024]{1,0:T(8,128)S(1)}, u32[]{:S(2)}, u32[]{:S(2)}) collective-permute-start(f32[48,1024]{1,0:T(8,128)S(1)} %get-tuple-element.26), channel_id=1, source_target_pairs={{0,128},{1,129},{2,130},{3,131},{4,132},{5,133},{6,134},{7,135},{8... | collective-permute-start | bytes 589832 | tf_op jit(solution)/shard_map/ppermute | solution.py:377
  11.3 0.0 collective-permute-done.intra_ref
  11.3 0.7 %collective-permute-done.1.inter_ref = f32[48,1024]{1,0:T(8,128)S(1)} collective-permute-done((f32[48,1024]{1,0:T(8,128)}, f32[48,1024]{1,0:T(8,128)S(1)}, u32[]{:S(2)}, u32[]{:S(2)}) %collective-permute-start.1) | collective-permute-done | bytes 196640 | tf_op jit(solution)/shard_map/ppermute | solution.py:410
  12.0 1.8 %shard_map.43 = (f32[16,1024]{1,0:T(8,128)S(1)}, f32[48,1024]{1,0:T(8,128)S(1)}, f32[48,1024]{1,0:T(8,128)S(1)}, f32[48,1024]{1,0:T(8,128)S(1)}, f32[8,48,128]{2,1,0:T(8,128)S(1)}) custom-call(f32[128,1024]{1,0:T(8,128)S(1)} %bitcast.4, f32[128,1024]{1,0:T(8,128)S(1)} %copy-done.1, f32[48,1024]{1,0:T(8,128)S(1)} %collective-permute-done.intra_ref, ...), custom_call_target="tpu_custom_call" | custom-call | tf_op jit(solution)/shard_map/pallas_call | solution.py:419
  13.7 2.6 %collective-permute-start.3 = (f32[48,1024]{1,0:T(8,128)S(1)}, f32[48,1024]{1,0:T(8,128)S(1)}, u32[]{:S(2)}, u32[]{:S(2)}) collective-permute-start(f32[48,1024]{1,0:T(8,128)S(1)} %get-tuple-element.27), channel_id=1, source_target_pairs={{0,64},{1,193},{2,66},{3,195},{4,68},{5,197},{6,70},{7,199},{8,72}... | collective-permute-start | bytes 589832 | tf_op jit(solution)/shard_map/ppermute | solution.py:377
  16.3 0.0 collective-permute-start.4
  16.3 0.0 collective-permute-done.2.one_ref
  16.3 4.4 %collective-permute-done.3.two_ref = f32[48,1024]{1,0:T(8,128)S(1)} collective-permute-done((f32[48,1024]{1,0:T(8,128)S(1)}, f32[48,1024]{1,0:T(8,128)S(1)}, u32[]{:S(2)}, u32[]{:S(2)}) %collective-permute-start.3) | collective-permute-done | bytes 196640 | tf_op jit(solution)/shard_map/ppermute | solution.py:377
  20.7 0.1 collective-permute-done.4.three_ref
  20.8 0.4 shard_map.44
  21.2 1.9 %collective-permute-start.5 = (f32[36,1024]{1,0:T(8,128)S(1)}, f32[36,1024]{1,0:T(8,128)S(1)}, u32[]{:S(2)}, u32[]{:S(2)}) collective-permute-start(f32[36,1024]{1,0:T(8,128)S(1)} %get-tuple-element.31), channel_id=1, source_target_pairs={{0,128},{1,129},{2,130},{3,131},{4,132},{5,133},{6,134},{7,135},{8... | collective-permute-start | bytes 442376 | tf_op jit(solution)/shard_map/ppermute | solution.py:377
  23.1 1.1 %collective-permute-start.6 = (f32[36,1024]{1,0:T(8,128)S(1)}, f32[36,1024]{1,0:T(8,128)S(1)}, u32[]{:S(2)}, u32[]{:S(2)}) collective-permute-start(f32[36,1024]{1,0:T(8,128)S(1)} %get-tuple-element.32), channel_id=1, source_target_pairs={{0,64},{1,193},{2,66},{3,195},{4,68},{5,197},{6,70},{7,199},{8,72}... | collective-permute-start | bytes 442376 | tf_op jit(solution)/shard_map/ppermute | solution.py:377
  24.2 0.0 collective-permute-start.7
  24.2 4.7 %collective-permute-done.5.one_ref = f32[36,1024]{1,0:T(8,128)S(1)} collective-permute-done((f32[36,1024]{1,0:T(8,128)S(1)}, f32[36,1024]{1,0:T(8,128)S(1)}, u32[]{:S(2)}, u32[]{:S(2)}) %collective-permute-start.5) | collective-permute-done | bytes 147488 | tf_op jit(solution)/shard_map/ppermute | solution.py:377
  28.9 3.5 %collective-permute-done.6.two_ref = f32[36,1024]{1,0:T(8,128)S(1)} collective-permute-done((f32[36,1024]{1,0:T(8,128)S(1)}, f32[36,1024]{1,0:T(8,128)S(1)}, u32[]{:S(2)}, u32[]{:S(2)}) %collective-permute-start.6) | collective-permute-done | bytes 147488 | tf_op jit(solution)/shard_map/ppermute | solution.py:377
  32.4 0.0 collective-permute-done.7.three_ref
  32.4 3.9 %shard_map.45 = (f32[128,1024]{1,0:T(8,128)}, f32[128,1024]{1,0:T(8,128)}) custom-call(f32[128,1024]{1,0:T(8,128)S(1)} %bitcast.5, f32[48,1024]{1,0:T(8,128)S(1)} %collective-permute-done.intra_ref, f32[48,1024]{1,0:T(8,128)S(1)} %collective-permute-done.1.inter_ref, f32[128,1024]{1,0:T(8,128)S(1)} %get-tuple-element.21.defect_ref, ...), custom_call_target="tpu_custom_call" | custom-call | tf_op jit(solution)/shard_map/pallas_call | solution.py:430
Async XLA Ops:
  0.6 5.2 %copy-start.1 = (f32[128,1024]{1,0:T(8,128)S(1)}, f32[128,1024]{1,0:T(8,128)}, u32[]{:S(2)}) copy-start(f32[128,1024]{1,0:T(8,128)} %s_ref.5) | copy-start | bytes 1572868
  0.6 5.2 %copy-start = (f32[1,128,1024]{2,1,0:T(8,128)S(1)}, f32[1,128,1024]{2,1,0:T(8,128)}, u32[]{:S(2)}) copy-start(f32[1,128,1024]{2,1,0:T(8,128)} %c_ref.1) | copy-start | bytes 1572868
  2.6 8.7 %collective-permute-start = (f32[48,1024]{1,0:T(8,128)}, f32[48,1024]{1,0:T(8,128)S(1)}, u32[]{:S(2)}, u32[]{:S(2)}) collective-permute-start(f32[48,1024]{1,0:T(8,128)} %get-tuple-element.19), channel_id=1, source_target_pairs={{0,1},{1,0},{2,3},{3,2},{4,5},{5,4},{6,7},{7,6},{8,9},{9,8},{10,11... | collective-permute-start | bytes 589832 | tf_op jit(solution)/shard_map/ppermute | solution.py:367
  3.3 8.6 %collective-permute-start.1 = (f32[48,1024]{1,0:T(8,128)}, f32[48,1024]{1,0:T(8,128)S(1)}, u32[]{:S(2)}, u32[]{:S(2)}) collective-permute-start(f32[48,1024]{1,0:T(8,128)} %get-tuple-element.20), channel_id=1, source_target_pairs={{0,64},{1,2},{2,1},{3,4},{4,3},{5,6},{6,5},{7,8},{8,7},{9,10},{10,... | collective-permute-start | bytes 589832 | tf_op jit(solution)/shard_map/ppermute | solution.py:410
  8.5 7.8 %collective-permute-start.2 = (f32[48,1024]{1,0:T(8,128)S(1)}, f32[48,1024]{1,0:T(8,128)S(1)}, u32[]{:S(2)}, u32[]{:S(2)}) collective-permute-start(f32[48,1024]{1,0:T(8,128)S(1)} %get-tuple-element.26), channel_id=1, source_target_pairs={{0,128},{1,129},{2,130},{3,131},{4,132},{5,133},{6,134},{7,135},{8... | collective-permute-start | bytes 589832 | tf_op jit(solution)/shard_map/ppermute | solution.py:377
  13.7 7.0 %collective-permute-start.3 = (f32[48,1024]{1,0:T(8,128)S(1)}, f32[48,1024]{1,0:T(8,128)S(1)}, u32[]{:S(2)}, u32[]{:S(2)}) collective-permute-start(f32[48,1024]{1,0:T(8,128)S(1)} %get-tuple-element.27), channel_id=1, source_target_pairs={{0,64},{1,193},{2,66},{3,195},{4,68},{5,197},{6,70},{7,199},{8,72}... | collective-permute-start | bytes 589832 | tf_op jit(solution)/shard_map/ppermute | solution.py:377
  16.3 4.5 %collective-permute-start.4 = (f32[48,1024]{1,0:T(8,128)S(1)}, f32[48,1024]{1,0:T(8,128)S(1)}, u32[]{:S(2)}, u32[]{:S(2)}) collective-permute-start(f32[48,1024]{1,0:T(8,128)S(1)} %get-tuple-element.28), channel_id=1, source_target_pairs={{0,192},{1,65},{2,194},{3,67},{4,196},{5,69},{6,198},{7,71},{8,200... | collective-permute-start | bytes 589832 | tf_op jit(solution)/shard_map/ppermute | solution.py:377
  21.2 7.7 %collective-permute-start.5 = (f32[36,1024]{1,0:T(8,128)S(1)}, f32[36,1024]{1,0:T(8,128)S(1)}, u32[]{:S(2)}, u32[]{:S(2)}) collective-permute-start(f32[36,1024]{1,0:T(8,128)S(1)} %get-tuple-element.31), channel_id=1, source_target_pairs={{0,128},{1,129},{2,130},{3,131},{4,132},{5,133},{6,134},{7,135},{8... | collective-permute-start | bytes 442376 | tf_op jit(solution)/shard_map/ppermute | solution.py:377
  23.1 9.4 %collective-permute-start.6 = (f32[36,1024]{1,0:T(8,128)S(1)}, f32[36,1024]{1,0:T(8,128)S(1)}, u32[]{:S(2)}, u32[]{:S(2)}) collective-permute-start(f32[36,1024]{1,0:T(8,128)S(1)} %get-tuple-element.32), channel_id=1, source_target_pairs={{0,64},{1,193},{2,66},{3,195},{4,68},{5,197},{6,70},{7,199},{8,72}... | collective-permute-start | bytes 442376 | tf_op jit(solution)/shard_map/ppermute | solution.py:377
  24.2 8.2 %collective-permute-start.7 = (f32[36,1024]{1,0:T(8,128)S(1)}, f32[36,1024]{1,0:T(8,128)S(1)}, u32[]{:S(2)}, u32[]{:S(2)}) collective-permute-start(f32[36,1024]{1,0:T(8,128)S(1)} %get-tuple-element.33), channel_id=1, source_target_pairs={{0,192},{1,65},{2,194},{3,67},{4,196},{5,69},{6,198},{7,71},{8,200... | collective-permute-start | bytes 442376 | tf_op jit(solution)/shard_map/ppermute | solution.py:377

commit v4 on v3

--- a/solution.py
+++ b/solution.py
@@ -22,7 +22,8 @@
 PART = (ROWS + 2 * REACH) // SLABS
 BLOCK = PART + 4
 BOX = 48
-FAR_BOX = 48
+FAR_BOX = 64
+CHUNK = 32
 PIECE = BOX // 2
 EDGE = PART // 2
 FAR = REACH + 2
@@ -68,10 +69,11 @@
     return slab, strip % 2, up_mask, down_mask
 
 
-def pack_kernel(c_ref, s_ref, intra_ref, inter_ref, sems):
+def pack_kernel(c_ref, s_ref, intra_ref, inter_ref, far_ref, sems):
     odd = parity()
     low = pl.multiple_of((ROWS - HALO) * odd, 8)
     high = pl.multiple_of((ROWS - HALO) * (1 - odd), 8)
+    middle = pl.multiple_of(FAR_BOX // 2 * inner_place(lax.axis_index("tm") ^ 2), 8)
     copies = []
     for n, (source, at) in enumerate(((c_ref.at[0], 0), (s_ref, HALO))):
         for m, (target, start) in enumerate(((inter_ref, low), (intra_ref, high))):
@@ -80,6 +82,7 @@
                     source.at[pl.ds(start, HALO)], target.at[pl.ds(at, HALO)], sems.at[2 * n + m]
                 )
             )
+    copies.append(pltpu.make_async_copy(c_ref.at[0, pl.ds(middle, FAR_BOX)], far_ref, sems.at[4]))
     for copy in copies:
         copy.start()
     for copy in copies:
@@ -109,11 +112,15 @@
     return first if first == second else jnp.where(parity() == 0, first, second)
 
 
+def inner_place(worker):
+    return jnp.where(worker > RIM_SLAB, worker - 1, 0)
+
+
 def inner_start(worker):
-    return REACH + PART * jnp.where(worker > RIM_SLAB, worker - 1, jnp.where(worker == RIM_SLAB, 0, worker))
-
-
-def inner_kernel(c_ref, s_ref, defect_ref, gift_ref, force_ref, far_ref, one, two, coarse):
+    return REACH + PART * inner_place(worker)
+
+
+def inner_kernel(c_ref, s_ref, defect_ref, gift_ref, force_ref, one, two, coarse):
     slab = lax.axis_index("tm")
     lane_ids = lanes()
     count = ROWS // 8
@@ -137,13 +144,36 @@
             rough = coarse[g, rows, :]
             gift_ref[g, rows, :] = fine - first * rough
             defect_ref[pl.ds(8 * i, 8), pl.ds(g * LANE, LANE)] = fine - rough
-    start = PAD + inner_start(slab ^ 2)
-    for i in range(FAR_BOX // 8):
+
+
+def far_kernel(raw_ref, force_ref, far_ref, one, two, force, coarse):
+    slab = lax.axis_index("tm")
+    lane_ids = lanes()
+    count = FAR_BOX // 8
+    tiles = [PAD + 8 * i for i in range(count)]
+    load(one, PAD, raw_ref, 0, count, ADVECT)
+    low = pl.multiple_of(PAD + FAR_BOX // 2 * inner_place(slab), 8)
+    for g in range(TILES):
+        for i in range(count):
+            force[g, pl.ds(PAD + 8 * i, 8), :] = force_ref[g, pl.ds(low + 8 * i, 8), :]
+    sweep(one, two, force, tiles, lane_ids, coarse)
+    sweep(two, one, force, tiles, lane_ids)
+
+    def pair(_, carry):
+        sweep(one, two, force, tiles, lane_ids)
+        sweep(two, one, force, tiles, lane_ids)
+        return carry
+
+    lax.fori_loop(0, STEPS // 2 - 1, pair, 0)
+    first = jnp.where(slab ^ 2 == 0, 0.0, 1.0)
+    start = PAD + REACH + (PART - FAR_BOX // 2) * inner_place(slab)
+    for i in range(BLOCK // 8):
+        rows = pl.ds(start + 8 * i, 8)
         for g in range(TILES):
-            far_ref[pl.ds(8 * i, 8), pl.ds(g * LANE, LANE)] = gift_ref[g, pl.ds(start + 8 * i, 8), :]
-
-
-def rim_kernel(c_ref, s_ref, intra_ref, inter_ref, inner_gift_ref, inner_force_ref, defect_ref, mine_ref, one_ref, two_ref, block_ref, one, two, force, coarse, gift, wide_force):
+            far_ref[pl.ds(8 * i, 8), pl.ds(g * LANE, LANE)] = one[g, rows, :] - first * coarse[g, rows, :]
+
+
+def rim_kernel(c_ref, s_ref, intra_ref, inter_ref, inner_gift_ref, inner_force_ref, defect_ref, mine_ref, one_ref, two_ref, block_ref, rim_gift_ref, wide_force, one, two, force, coarse, gift):
     slab, odd, up_mask, down_mask = place()
     lane_ids = lanes()
     low, high = PAD, SIDE + PAD
@@ -201,11 +231,12 @@
             rough = coarse[g, rows, :]
             if at in masks:
                 rough = rough * masks[at]
-            gift[g, pl.ds(place_at, 8), :] = fine - first * rough
-            if at == low + HALO:
-                defect_ref[pl.ds(0, 8), pl.ds(g * LANE, LANE)] = fine - rough
-            if at == high + HALO - 8:
-                defect_ref[pl.ds(8, 8), pl.ds(g * LANE, LANE)] = fine - rough
+            given = fine - first * rough
+            gift[g, pl.ds(place_at, 8), :] = given
+            if at in (low + HALO, high + HALO - 8):
+                cut = (pl.ds(0 if at == low + HALO else 8, 8), pl.ds(g * LANE, LANE))
+                defect_ref[cut] = fine - rough
+                rim_gift_ref[cut] = given
     for order, out in ((0, mine_ref), (2, one_ref), (3, two_ref)):
         worker = slab ^ partner(order)
 
@@ -279,40 +310,35 @@
     each_place(slab, odd, body)
 
 
-def fine_kernel(c_ref, intra_ref, inter_ref, defect_ref, rim_defect_ref, inner_force_ref, mine_ref, one_ref, two_ref, three_ref, new_ref, end_ref, one, two, force):
+def first_kernel(inner_gift_ref, rim_gift_ref, new_out, end_out, stage, sems):
+    @pl.when(lax.axis_index("tm") == 0)
+    def _():
+        last = ROWS // 8 - 1
+        for g in range(TILES):
+            cut = pl.ds(g * LANE, LANE)
+            for i in range(last + 1):
+                if i in (0, last):
+                    value = rim_gift_ref[pl.ds(8 * (i > 0), 8), cut]
+                else:
+                    value = inner_gift_ref[g, pl.ds(PAD + 8 * i, 8), :]
+                stage[pl.ds(8 * i, 8), cut] = value * (1.0 / ADVECT)
+        copies = [pltpu.make_async_copy(stage, out, sems.at[n]) for n, out in enumerate((new_out, end_out))]
+        for copy in copies:
+            copy.start()
+        for copy in copies:
+            copy.wait()
+
+
+def fine_kernel(*refs):
+    pl.when(lax.axis_index("tm") > 0)(functools.partial(later_slabs, *refs))
+
+
+def later_slabs(defect_ref, rim_defect_ref, force, mine_ref, one_ref, two_ref, three_ref, new_in, end_in, new_out, end_out, one, two, new_ref, end_ref, sems):
     boxes = (mine_ref, one_ref, two_ref, three_ref)
     slab, odd, up_mask, down_mask = place()
     lane_ids = lanes()
     base = PAD + REACH
     last = base + ROWS
-
-    def ends(target, scale, top, bottom, offset):
-        load(target, PAD, top, offset + HALO - 8, 1, scale * up_mask)
-        load(target, last, bottom, offset, 1, scale * down_mask)
-
-    for g in range(TILES):
-        for i in range(ROWS // 8):
-            force[g, pl.ds(base + 8 * i, 8), :] = inner_force_ref[g, pl.ds(PAD + 8 * i, 8), :]
-
-    @pl.when(odd == 1)
-    def _():
-        ends(force, ADVECT * FORCE, intra_ref, inter_ref, HALO)
-
-    @pl.when(odd == 0)
-    def _():
-        ends(force, ADVECT * FORCE, inter_ref, intra_ref, HALO)
-
-    @pl.when((slab == 0) & (odd == 1))
-    def _():
-        ends(one, ADVECT, intra_ref, inter_ref, 0)
-
-    @pl.when((slab == 0) & (odd == 0))
-    def _():
-        ends(one, ADVECT, inter_ref, intra_ref, 0)
-
-    @pl.when(slab == 0)
-    def _():
-        load(one, base, c_ref, 0, ROWS // 8, ADVECT)
 
     def body(t, order):
         for w in range(SLABS):
@@ -327,9 +353,7 @@
                     for g in range(TILES):
                         one[g, pl.ds(base + row + 8 * i, size), :] = source[pl.ds(begin + 8 * i, size), pl.ds(g * LANE, LANE)]
 
-    @pl.when(slab > 0)
-    def _():
-        each_place(slab, odd, body)
+    each_place(slab, odd, body)
 
     tiles = [PAD + 8 * i for i in range((ROWS + 2 * REACH) // 8)]
     masks = {PAD: up_mask, last: down_mask}
@@ -350,6 +374,9 @@
                 new_ref[pl.ds(at - base, 8), cut] = (now + 8.0 * inc + defect) * (1.0 / ADVECT)
             two[g, pl.ds(at, 8), :] = new
 
+    copies = [pltpu.make_async_copy(new_ref, new_out, sems.at[0])]
+    copies[0].start()
+
     def pair(_, carry):
         sweep(two, one, force, tiles, lane_ids, None, masks)
         sweep(one, two, force, tiles, lane_ids, None, masks)
@@ -360,6 +387,13 @@
         for g, now, above, below, left, right in row_tile(two, at, lane_ids):
             inc = increment(now, above, below, left, right, force[g, pl.ds(at, 8), :])
             end_ref[pl.ds(at - base, 8), pl.ds(g * LANE, LANE)] = (now + inc) * (1.0 / ADVECT)
+        done = at + 8 - base
+        if done % CHUNK == 0:
+            rows = pl.ds(done - CHUNK, CHUNK)
+            copies.append(pltpu.make_async_copy(end_ref.at[rows], end_out.at[rows], sems.at[len(copies)]))
+            copies[-1].start()
+    for copy in copies:
+        copy.wait()
 
 
 def swap(array, axis, by):
@@ -377,14 +411,16 @@
     return lax.ppermute(box, ("tm", "space"), pairs)
 
 
-def call(kernel, outs, scratch):
-    spec = pl.BlockSpec(memory_space=pltpu.VMEM)
+def call(kernel, outs, scratch, place=pltpu.VMEM, copies=0, **more):
+    spec = pl.BlockSpec(memory_space=place)
     return pl.pallas_call(
         kernel,
         out_shape=[jax.ShapeDtypeStruct(shape, jnp.float32) for shape in outs],
         out_specs=[spec] * len(outs),
-        scratch_shapes=[pltpu.VMEM(shape, jnp.float32) for shape in scratch],
+        scratch_shapes=[pltpu.VMEM(shape, jnp.float32) for shape in scratch]
+        + [pltpu.SemaphoreType.DMA((copies,))] * (copies > 0),
         compiler_params=pltpu.CompilerParams(vmem_limit_bytes=24 * 1024 * 1024),
+        **more,
     )
 
 
@@ -392,12 +428,12 @@
     field = c_points[0]
     count = lax.axis_size("space")
     edges = jax.ShapeDtypeStruct((2 * HALO, COLS), jnp.float32)
-    to_intra, to_inter = pl.pallas_call(
+    to_intra, to_inter, to_far = pl.pallas_call(
         pack_kernel,
-        out_shape=[edges, edges],
+        out_shape=[edges, edges, jax.ShapeDtypeStruct((FAR_BOX, COLS), jnp.float32)],
         in_specs=[pl.BlockSpec(memory_space=pl.ANY)] * 2,
-        out_specs=[pl.BlockSpec(memory_space=pltpu.VMEM)] * 2,
-        scratch_shapes=[pltpu.SemaphoreType.DMA((4,))],
+        out_specs=[pl.BlockSpec(memory_space=pltpu.VMEM)] * 3,
+        scratch_shapes=[pltpu.SemaphoreType.DMA((5,))],
     )(c_points, source)
     pairs = []
     for t in range(lax.axis_size("tm")):
@@ -411,25 +447,32 @@
     intra = swap(to_intra, "space", 1)
 
     wide = (TILES, ROWS + 2 * PAD, LANE)
-    defect, gift, force, far = call(
-        inner_kernel, [(ROWS, COLS), wide, wide, (FAR_BOX, COLS)], [wide] * 3
-    )(field, source)
-    far = swap_one(far, 1)
+    raw = swap_one(to_far, 1)
+    defect, gift, force = call(inner_kernel, [(ROWS, COLS), wide, wide], [wide] * 3)(field, source)
     narrow = (TILES, ROWS + 4 * REACH, LANE)
-    rim_defect, mine, one, two, block_force = call(
+    rim_defect, mine, one, two, block_force, rim_gift, wide_force = call(
         rim_kernel,
-        [(16, COLS)] + [(BOX, COLS)] * 3 + [(TILES, BOX, LANE)],
-        [(TILES, 2 * SIDE, LANE)] * 4 + [narrow] * 2,
+        [(16, COLS)] + [(BOX, COLS)] * 3 + [(TILES, BOX, LANE), (16, COLS), narrow],
+        [(TILES, 2 * SIDE, LANE)] * 4 + [narrow],
     )(field, source, intra, inter, gift, force)
     one, two = swap_one(one, 2), swap_one(two, 3)
+    far = call(far_kernel, [(BLOCK, COLS)], [(TILES, FAR_BOX + 2 * PAD, LANE)] * 4)(raw, force)[0]
     starts = call(
         chain_kernel, [(PART, COLS)] * 4, [(TILES, BOX + 2 * PAD, LANE)] * 3
     )(mine, far, one, two, block_force)
     starts = [starts[0]] + [swap_one(starts[order], order) for order in range(1, SLABS)]
+    new, end = call(first_kernel, [(ROWS, COLS)] * 2, [(ROWS, COLS)], pl.ANY, 2)(gift, rim_gift)
     middle = (TILES, ROWS + 2 * REACH + 2 * PAD, LANE)
-    corrected, fine = call(fine_kernel, [(ROWS, COLS)] * 2, [middle] * 3)(
-        field, intra, inter, defect, rim_defect, force, *starts
-    )
+    inside, outside = pl.BlockSpec(memory_space=pltpu.VMEM), pl.BlockSpec(memory_space=pl.ANY)
+    corrected, fine = call(
+        fine_kernel,
+        [(ROWS, COLS)] * 2,
+        [middle] * 2 + [(ROWS, COLS)] * 2,
+        pl.ANY,
+        1 + ROWS // CHUNK,
+        in_specs=[inside] * 7 + [outside] * 2,
+        input_output_aliases={7: 0, 8: 1},
+    )(defect, rim_defect, wide_force, *starts, new, end)
     return corrected[None], fine[None]
 
 

time: 36.4 us -> 35.2 us (0.967)
  the two profiles are of different devices: /device:TPU:121 before, /device:TPU:123 now
where the time goes in v4:
time: 35.2 us; the launch traced here: 35 us
  Pallas kernels  12 us (34%)
  starting transfers between devices  11.9 us (34%)
  waiting for transfers between devices  10.4 us (30%)
  between operations  0.71 us (2%)
    ppermute x6, waiting for transfers between devices, swap_one(): return lax.ppermute(box, ('tm', 'space'), pairs)  8.73 us
    ppermute x6, starting transfers between devices, swap_one(): return lax.ppermute(box, ('tm', 'space'), pairs)  8.61 us
    pallas_call x1, Pallas kernels, local(): call(fine_kernel, [(ROWS, COLS)] * 2, [middle] * 2 + [(ROWS, COLS)] * 2,...  3.66 us
    pallas_call x1, Pallas kernels, local(): call(inner_kernel, [(ROWS, COLS), wide, wide], [wide] * 3)(field, source)  2.62 us
    ppermute x1, starting transfers between devices, local(): inter = lax.ppermute(to_inter, ('tm', 'space'), pairs)  2.49 us
    pallas_call x1, Pallas kernels, local(): pl.pallas_call(pack_kernel, out_shape=[edges, edges, jax.ShapeDtypeStruct...  2.11 us
    pallas_call x1, Pallas kernels, local(): call(rim_kernel, [(16, COLS)] + [(BOX, COLS)] * 3 + [(TILES, BOX, LANE),...  1.77 us
    ppermute x1, waiting for transfers between devices, local(): inter = lax.ppermute(to_inter, ('tm', 'space'), pairs)  1.64 us
  transfers between devices with their start and end apart: 8, of which 5 were waited for; matrix products, arithmetic and copies ran while one was open for 0% of the time, Pallas kernels for 17%

profile of v4, /device:TPU:123, one launch (start us, length us, event | category | flops | bytes accessed | tf_op | source)
XLA Modules:
  0.0 35.0 jit_solution(1101437239291834413)
XLA Ops:
  0.6 0.0 copy-start.1
  0.6 0.0 copy-start
  0.6 2.1 %shard_map.42 = (f32[48,1024]{1,0:T(8,128)}, f32[48,1024]{1,0:T(8,128)}, f32[64,1024]{1,0:T(8,128)}) custom-call(f32[1,128,1024]{2,1,0:T(8,128)} %c_ref.1, f32[128,1024]{1,0:T(8,128)} %s_ref.5), custom_call_target="tpu_custom_call" | custom-call | tf_op jit(solution)/shard_map/pallas_call | solution.py:431
  2.8 0.8 %collective-permute-start = (f32[48,1024]{1,0:T(8,128)}, f32[48,1024]{1,0:T(8,128)S(1)}, u32[]{:S(2)}, u32[]{:S(2)}) collective-permute-start(f32[48,1024]{1,0:T(8,128)} %get-tuple-element.24), channel_id=1, source_target_pairs={{0,1},{1,0},{2,3},{3,2},{4,5},{5,4},{6,7},{7,6},{8,9},{9,8},{10,11... | collective-permute-start | bytes 589832 | tf_op jit(solution)/shard_map/ppermute | solution.py:401
  3.5 2.5 %collective-permute-start.1 = (f32[48,1024]{1,0:T(8,128)}, f32[48,1024]{1,0:T(8,128)S(1)}, u32[]{:S(2)}, u32[]{:S(2)}) collective-permute-start(f32[48,1024]{1,0:T(8,128)} %get-tuple-element.25), channel_id=1, source_target_pairs={{0,64},{1,2},{2,1},{3,4},{4,3},{5,6},{6,5},{7,8},{8,7},{9,10},{10,... | collective-permute-start | bytes 589832 | tf_op jit(solution)/shard_map/ppermute | solution.py:446
  6.0 1.8 %collective-permute-start.2 = (f32[64,1024]{1,0:T(8,128)}, f32[64,1024]{1,0:T(8,128)S(1)}, u32[]{:S(2)}, u32[]{:S(2)}) collective-permute-start(f32[64,1024]{1,0:T(8,128)} %get-tuple-element.31), channel_id=1, source_target_pairs={{0,128},{1,129},{2,130},{3,131},{4,132},{5,133},{6,134},{7,135},{8... | collective-permute-start | bytes 786440 | tf_op jit(solution)/shard_map/ppermute | solution.py:411
  7.9 0.0 copy-done.1
  7.9 0.0 copy-done
  7.9 2.6 %shard_map.41 = (f32[128,1024]{1,0:T(8,128)S(1)}, f32[8,144,128]{2,1,0:T(8,128)S(1)}, f32[8,144,128]{2,1,0:T(8,128)S(1)}) custom-call(f32[128,1024]{1,0:T(8,128)S(1)} %bitcast.3, f32[128,1024]{1,0:T(8,128)S(1)} %copy-done.1), custom_call_target="tpu_custom_call" | custom-call | tf_op jit(solution)/shard_map/pallas_call | solution.py:451
  10.5 0.0 collective-permute-done.intra_ref
  10.5 1.6 %collective-permute-done.1.inter_ref = f32[48,1024]{1,0:T(8,128)S(1)} collective-permute-done((f32[48,1024]{1,0:T(8,128)}, f32[48,1024]{1,0:T(8,128)S(1)}, u32[]{:S(2)}, u32[]{:S(2)}) %collective-permute-start.1) | collective-permute-done | bytes 196640 | tf_op jit(solution)/shard_map/ppermute | solution.py:446
  12.2 1.8 %shard_map.43 = (f32[16,1024]{1,0:T(8,128)S(1)}, f32[48,1024]{1,0:T(8,128)S(1)}, f32[48,1024]{1,0:T(8,128)S(1)}, f32[48,1024]{1,0:T(8,128)S(1)}, f32[8,48,128]{2...) custom-call(f32[128,1024]{1,0:T(8,128)S(1)} %bitcast.4, f32[128,1024]{1,0:T(8,128)S(1)} %copy-done.1, ...), custom_call_target="tpu_custom_call" | custom-call | tf_op jit(solution)/shard_map/pallas_call | solution.py:453
  13.9 1.3 %collective-permute-start.3 = (f32[48,1024]{1,0:T(8,128)S(1)}, f32[48,1024]{1,0:T(8,128)S(1)}, u32[]{:S(2)}, u32[]{:S(2)}) collective-permute-start(f32[48,1024]{1,0:T(8,128)S(1)} %get-tuple-element.32), channel_id=1, source_target_pairs={{0,64},{1,193},{2,66},{3,195},{4,68},{5,197},{6,70},{7,199},{8,72}... | collective-permute-start | bytes 589832 | tf_op jit(solution)/shard_map/ppermute | solution.py:411
  15.2 1.5 %collective-permute-start.4 = (f32[48,1024]{1,0:T(8,128)S(1)}, f32[48,1024]{1,0:T(8,128)S(1)}, u32[]{:S(2)}, u32[]{:S(2)}) collective-permute-start(f32[48,1024]{1,0:T(8,128)S(1)} %get-tuple-element.33), channel_id=1, source_target_pairs={{0,192},{1,65},{2,194},{3,67},{4,196},{5,69},{6,198},{7,71},{8,200... | collective-permute-start | bytes 589832 | tf_op jit(solution)/shard_map/ppermute | solution.py:411
  16.8 0.0 collective-permute-done.2.raw_ref
  16.8 1.4 %shard_map.44.one_ref = f32[40,1024]{1,0:T(8,128)S(1)} custom-call(f32[64,1024]{1,0:T(8,128)S(1)} %collective-permute-done.2.raw_ref, f32[8,144,128]{2,1,0:T(8,128)S(1)} %get-tuple-element.27.inner_force_ref.force_ref), custom_call_target="tpu_custom_call" | custom-call | tf_op jit(solution)/shard_map/pallas_call | solution.py:459
  18.2 1.4 %collective-permute-done.3.two_ref = f32[48,1024]{1,0:T(8,128)S(1)} collective-permute-done((f32[48,1024]{1,0:T(8,128)S(1)}, f32[48,1024]{1,0:T(8,128)S(1)}, u32[]{:S(2)}, u32[]{:S(2)}) %collective-permute-start.3) | collective-permute-done | bytes 196640 | tf_op jit(solution)/shard_map/ppermute | solution.py:411
  19.6 0.2 collective-permute-done.4.three_ref
  19.8 0.4 %shard_map.45 = (f32[36,1024]{1,0:T(8,128)S(1)}, f32[36,1024]{1,0:T(8,128)S(1)}, f32[36,1024]{1,0:T(8,128)S(1)}, f32[36,1024]{1,0:T(8,128)S(1)}) custom-call(f32[48,1024]{1,0:T(8,128)S(1)} %get-tuple-element.30.mine_ref, f32[40,1024]{1,0:T(8,128)S(1)} %shard_map.44.one_ref, f32[48,1024]{1,0:T(8,128)S(1)} %collective-permute-done.3.two_ref, ...), custom_call_target="tpu_custom_call" | custom-call | tf_op jit(solution)/shard_map/pallas_call | solution.py:460
  20.2 2.0 %collective-permute-start.5 = (f32[36,1024]{1,0:T(8,128)S(1)}, f32[36,1024]{1,0:T(8,128)S(1)}, u32[]{:S(2)}, u32[]{:S(2)}) collective-permute-start(f32[36,1024]{1,0:T(8,128)S(1)} %get-tuple-element.36), channel_id=1, source_target_pairs={{0,128},{1,129},{2,130},{3,131},{4,132},{5,133},{6,134},{7,135},{8... | collective-permute-start | bytes 442376 | tf_op jit(solution)/shard_map/ppermute | solution.py:411
  22.2 0.7 %collective-permute-start.6 = (f32[36,1024]{1,0:T(8,128)S(1)}, f32[36,1024]{1,0:T(8,128)S(1)}, u32[]{:S(2)}, u32[]{:S(2)}) collective-permute-start(f32[36,1024]{1,0:T(8,128)S(1)} %get-tuple-element.37), channel_id=1, source_target_pairs={{0,64},{1,193},{2,66},{3,195},{4,68},{5,197},{6,70},{7,199},{8,72}... | collective-permute-start | bytes 442376 | tf_op jit(solution)/shard_map/ppermute | solution.py:411
  22.9 1.3 %collective-permute-start.7 = (f32[36,1024]{1,0:T(8,128)S(1)}, f32[36,1024]{1,0:T(8,128)S(1)}, u32[]{:S(2)}, u32[]{:S(2)}) collective-permute-start(f32[36,1024]{1,0:T(8,128)S(1)} %get-tuple-element.38), channel_id=1, source_target_pairs={{0,192},{1,65},{2,194},{3,67},{4,196},{5,69},{6,198},{7,71},{8,200... | collective-permute-start | bytes 442376 | tf_op jit(solution)/shard_map/ppermute | solution.py:411
  24.2 3.6 %collective-permute-done.5.refs_4_ = f32[36,1024]{1,0:T(8,128)S(1)} collective-permute-done((f32[36,1024]{1,0:T(8,128)S(1)}, f32[36,1024]{1,0:T(8,128)S(1)}, u32[]{:S(2)}, u32[]{:S(2)}) %collective-permute-start.5) | collective-permute-done | bytes 147488 | tf_op jit(solution)/shard_map/ppermute | solution.py:411
  27.8 3.5 %collective-permute-done.6.refs_5_ = f32[36,1024]{1,0:T(8,128)S(1)} collective-permute-done((f32[36,1024]{1,0:T(8,128)S(1)}, f32[36,1024]{1,0:T(8,128)S(1)}, u32[]{:S(2)}, u32[]{:S(2)}) %collective-permute-start.6) | collective-permute-done | bytes 147488 | tf_op jit(solution)/shard_map/ppermute | solution.py:411
  31.3 0.0 collective-permute-done.7.refs_6_
  31.3 3.7 %shard_map.47 = (f32[128,1024]{1,0:T(8,128)}, f32[128,1024]{1,0:T(8,128)}) custom-call(f32[128,1024]{1,0:T(8,128)S(1)} %get-tuple-element.23.refs_0_, f32[16,1024]{1,0:T(8,128)S(1)} %get-tuple-element.28.refs_1_, f32[8,160,128]{2,1,0:T(8,128)S(1)} %get-tuple-element.29.refs_2_, ...), custom_call_target="tpu_custom_call", output_to_operand_aliasing={{0}: (7, {}), {1}: (8, {})} | custom-call | tf_op jit(solution)/shard_map/pallas_call | solution.py:467
  (1 shorter events, 0.0 us)
Async XLA Ops:
  0.6 7.2 %copy-start.1 = (f32[128,1024]{1,0:T(8,128)S(1)}, f32[128,1024]{1,0:T(8,128)}, u32[]{:S(2)}) copy-start(f32[128,1024]{1,0:T(8,128)} %s_ref.5) | copy-start | bytes 1572868
  0.6 7.2 %copy-start = (f32[1,128,1024]{2,1,0:T(8,128)S(1)}, f32[1,128,1024]{2,1,0:T(8,128)}, u32[]{:S(2)}) copy-start(f32[1,128,1024]{2,1,0:T(8,128)} %c_ref.1) | copy-start | bytes 1572868
  2.8 7.7 %collective-permute-start = (f32[48,1024]{1,0:T(8,128)}, f32[48,1024]{1,0:T(8,128)S(1)}, u32[]{:S(2)}, u32[]{:S(2)}) collective-permute-start(f32[48,1024]{1,0:T(8,128)} %get-tuple-element.24), channel_id=1, source_target_pairs={{0,1},{1,0},{2,3},{3,2},{4,5},{5,4},{6,7},{7,6},{8,9},{9,8},{10,11... | collective-permute-start | bytes 589832 | tf_op jit(solution)/shard_map/ppermute | solution.py:401
  3.5 8.6 %collective-permute-start.1 = (f32[48,1024]{1,0:T(8,128)}, f32[48,1024]{1,0:T(8,128)S(1)}, u32[]{:S(2)}, u32[]{:S(2)}) collective-permute-start(f32[48,1024]{1,0:T(8,128)} %get-tuple-element.25), channel_id=1, source_target_pairs={{0,64},{1,2},{2,1},{3,4},{4,3},{5,6},{6,5},{7,8},{8,7},{9,10},{10,... | collective-permute-start | bytes 589832 | tf_op jit(solution)/shard_map/ppermute | solution.py:446
  6.0 10.7 %collective-permute-start.2 = (f32[64,1024]{1,0:T(8,128)}, f32[64,1024]{1,0:T(8,128)S(1)}, u32[]{:S(2)}, u32[]{:S(2)}) collective-permute-start(f32[64,1024]{1,0:T(8,128)} %get-tuple-element.31), channel_id=1, source_target_pairs={{0,128},{1,129},{2,130},{3,131},{4,132},{5,133},{6,134},{7,135},{8... | collective-permute-start | bytes 786440 | tf_op jit(solution)/shard_map/ppermute | solution.py:411
  13.9 5.6 %collective-permute-start.3 = (f32[48,1024]{1,0:T(8,128)S(1)}, f32[48,1024]{1,0:T(8,128)S(1)}, u32[]{:S(2)}, u32[]{:S(2)}) collective-permute-start(f32[48,1024]{1,0:T(8,128)S(1)} %get-tuple-element.32), channel_id=1, source_target_pairs={{0,64},{1,193},{2,66},{3,195},{4,68},{5,197},{6,70},{7,199},{8,72}... | collective-permute-start | bytes 589832 | tf_op jit(solution)/shard_map/ppermute | solution.py:411
  15.2 4.6 %collective-permute-start.4 = (f32[48,1024]{1,0:T(8,128)S(1)}, f32[48,1024]{1,0:T(8,128)S(1)}, u32[]{:S(2)}, u32[]{:S(2)}) collective-permute-start(f32[48,1024]{1,0:T(8,128)S(1)} %get-tuple-element.33), channel_id=1, source_target_pairs={{0,192},{1,65},{2,194},{3,67},{4,196},{5,69},{6,198},{7,71},{8,200... | collective-permute-start | bytes 589832 | tf_op jit(solution)/shard_map/ppermute | solution.py:411
  20.2 7.6 %collective-permute-start.5 = (f32[36,1024]{1,0:T(8,128)S(1)}, f32[36,1024]{1,0:T(8,128)S(1)}, u32[]{:S(2)}, u32[]{:S(2)}) collective-permute-start(f32[36,1024]{1,0:T(8,128)S(1)} %get-tuple-element.36), channel_id=1, source_target_pairs={{0,128},{1,129},{2,130},{3,131},{4,132},{5,133},{6,134},{7,135},{8... | collective-permute-start | bytes 442376 | tf_op jit(solution)/shard_map/ppermute | solution.py:411
  22.2 9.1 %collective-permute-start.6 = (f32[36,1024]{1,0:T(8,128)S(1)}, f32[36,1024]{1,0:T(8,128)S(1)}, u32[]{:S(2)}, u32[]{:S(2)}) collective-permute-start(f32[36,1024]{1,0:T(8,128)S(1)} %get-tuple-element.37), channel_id=1, source_target_pairs={{0,64},{1,193},{2,66},{3,195},{4,68},{5,197},{6,70},{7,199},{8,72}... | collective-permute-start | bytes 442376 | tf_op jit(solution)/shard_map/ppermute | solution.py:411
  22.9 8.4 %collective-permute-start.7 = (f32[36,1024]{1,0:T(8,128)S(1)}, f32[36,1024]{1,0:T(8,128)S(1)}, u32[]{:S(2)}, u32[]{:S(2)}) collective-permute-start(f32[36,1024]{1,0:T(8,128)S(1)} %get-tuple-element.38), channel_id=1, source_target_pairs={{0,192},{1,65},{2,194},{3,67},{4,196},{5,69},{6,198},{7,71},{8,200... | collective-permute-start | bytes 442376 | tf_op jit(solution)/shard_map/ppermute | solution.py:411

commit v5 on v4

--- a/solution.py
+++ b/solution.py
@@ -17,14 +17,16 @@
 LANE = 128
 TILES = COLS // LANE
 HALO = 24
+DEEP = 18
 PAD = 8
 REACH = STEPS
 PART = (ROWS + 2 * REACH) // SLABS
 BLOCK = PART + 4
-BOX = 48
-FAR_BOX = 64
+BOX = 44
+FAR_BOX = BLOCK + 2 * REACH
 CHUNK = 32
 PIECE = BOX // 2
+BOX_TILES = (0, 8, 16, 24, 32, BOX - 8)
 EDGE = PART // 2
 FAR = REACH + 2
 RIM_SLAB = 1
@@ -69,24 +71,35 @@
     return slab, strip % 2, up_mask, down_mask
 
 
-def pack_kernel(c_ref, s_ref, intra_ref, inter_ref, far_ref, sems):
+def pack_kernel(c_ref, s_ref, inter_ref, far_ref, intra_ref):
     odd = parity()
-    low = pl.multiple_of((ROWS - HALO) * odd, 8)
-    high = pl.multiple_of((ROWS - HALO) * (1 - odd), 8)
-    middle = pl.multiple_of(FAR_BOX // 2 * inner_place(lax.axis_index("tm") ^ 2), 8)
-    copies = []
-    for n, (source, at) in enumerate(((c_ref.at[0], 0), (s_ref, HALO))):
-        for m, (target, start) in enumerate(((inter_ref, low), (intra_ref, high))):
-            copies.append(
-                pltpu.make_async_copy(
-                    source.at[pl.ds(start, HALO)], target.at[pl.ds(at, HALO)], sems.at[2 * n + m]
-                )
-            )
-    copies.append(pltpu.make_async_copy(c_ref.at[0, pl.ds(middle, FAR_BOX)], far_ref, sems.at[4]))
-    for copy in copies:
-        copy.start()
-    for copy in copies:
-        copy.wait()
+
+    def edges(core):
+        top, bottom = 0, ROWS - DEEP
+        for out, start in ((inter_ref, bottom if core else top), (intra_ref, top if core else bottom)):
+            for n, source in enumerate((c_ref, s_ref)):
+                for i in range(0, DEEP, 8):
+                    size = min(8, DEEP - i)
+                    for g in range(TILES):
+                        piece = source[pl.ds(start + i, size), pl.ds(g * LANE, LANE)]
+                        out[pl.ds(2 * DEEP * g + DEEP * n + i, size), :] = piece
+
+    def inner(place):
+        for i in range(0, FAR_BOX, 8):
+            far_ref[pl.ds(i, 8), :] = c_ref[pl.ds(PART * place + i, 8), :]
+
+    for core in range(2):
+        pl.when(odd == core)(functools.partial(edges, core))
+    wanted = inner_place(lax.axis_index("tm") ^ 2)
+    for place in range(SLABS - 1):
+        pl.when(wanted == place)(functools.partial(inner, place))
+
+
+def load_deep(target, at, source, begin, scale):
+    for i in range(0, DEEP, 8):
+        size = min(8, DEEP - i)
+        for g in range(TILES):
+            target[g, pl.ds(at + i, size), :] = source[pl.ds(2 * DEEP * g + begin + i, size), :] * scale
 
 
 def load(target, at, source, start, count, scale):
@@ -152,7 +165,7 @@
     count = FAR_BOX // 8
     tiles = [PAD + 8 * i for i in range(count)]
     load(one, PAD, raw_ref, 0, count, ADVECT)
-    low = pl.multiple_of(PAD + FAR_BOX // 2 * inner_place(slab), 8)
+    low = PAD + PART * inner_place(slab)
     for g in range(TILES):
         for i in range(count):
             force[g, pl.ds(PAD + 8 * i, 8), :] = force_ref[g, pl.ds(low + 8 * i, 8), :]
@@ -166,34 +179,34 @@
 
     lax.fori_loop(0, STEPS // 2 - 1, pair, 0)
     first = jnp.where(slab ^ 2 == 0, 0.0, 1.0)
-    start = PAD + REACH + (PART - FAR_BOX // 2) * inner_place(slab)
+    start = PAD + REACH
     for i in range(BLOCK // 8):
         rows = pl.ds(start + 8 * i, 8)
         for g in range(TILES):
             far_ref[pl.ds(8 * i, 8), pl.ds(g * LANE, LANE)] = one[g, rows, :] - first * coarse[g, rows, :]
 
 
-def rim_kernel(c_ref, s_ref, intra_ref, inter_ref, inner_gift_ref, inner_force_ref, defect_ref, mine_ref, one_ref, two_ref, block_ref, rim_gift_ref, wide_force, one, two, force, coarse, gift):
+def rim_kernel(c_ref, s_ref, intra_ref, inter_ref, inner_gift_ref, inner_force_ref, defect_ref, mine_ref, one_ref, two_ref, block_ref, rim_gift_ref, rim_force_ref, one, two, force, coarse):
     slab, odd, up_mask, down_mask = place()
     lane_ids = lanes()
     low, high = PAD, SIDE + PAD
     third = HALO // 8
 
     def fill(target, scale, top, main, bottom, offset):
-        load(target, low, top, offset, third, scale * up_mask)
+        load_deep(target, low + HALO - DEEP, top, offset, scale * up_mask)
         load(target, low + HALO, main, 0, third, scale)
         load(target, high, main, ROWS - HALO, third, scale)
-        load(target, high + HALO, bottom, offset, third, scale * down_mask)
+        load_deep(target, high + HALO, bottom, offset, scale * down_mask)
 
     @pl.when(odd == 1)
     def _():
         fill(one, ADVECT, intra_ref, c_ref, inter_ref, 0)
-        fill(force, ADVECT * FORCE, intra_ref, s_ref, inter_ref, HALO)
+        fill(force, ADVECT * FORCE, intra_ref, s_ref, inter_ref, DEEP)
 
     @pl.when(odd == 0)
     def _():
         fill(one, ADVECT, inter_ref, c_ref, intra_ref, 0)
-        fill(force, ADVECT * FORCE, inter_ref, s_ref, intra_ref, HALO)
+        fill(force, ADVECT * FORCE, inter_ref, s_ref, intra_ref, DEEP)
 
     def tiles(first, last):
         upper = [low + 8 * i for i in range(first, last)]
@@ -214,55 +227,48 @@
 
     lax.fori_loop(0, STEPS // 2 - 2, pair, 0)
     first = jnp.where(slab == 0, 0.0, 1.0)
-    base = 2 * REACH
-    for g in range(TILES):
-        for i in range(1, ROWS // 8 - 1):
-            gift[g, pl.ds(base + 8 * i, 8), :] = inner_gift_ref[g, pl.ds(PAD + 8 * i, 8), :]
-        for i in range(ROWS // 8):
-            wide_force[g, pl.ds(base + 8 * i, 8), :] = inner_force_ref[g, pl.ds(PAD + 8 * i, 8), :]
-        for i in range(2):
-            wide_force[g, pl.ds(8 * i, 8), :] = force[g, pl.ds(low + 8 + 8 * i, 8), :]
-            wide_force[g, pl.ds(base + ROWS + 8 * i, 8), :] = force[g, pl.ds(high + HALO + 8 * i, 8), :]
-    for n, at in enumerate([low + 8, low + 16, low + 24, high + 16, high + 24, high + 32]):
+    for at in tiles(1, 5):
         rows = pl.ds(at, 8)
-        place_at = 8 * n if n < 3 else base + ROWS - 8 + 8 * (n - 3)
         for g in range(TILES):
             fine = one[g, rows, :]
             rough = coarse[g, rows, :]
             if at in masks:
                 rough = rough * masks[at]
             given = fine - first * rough
-            gift[g, pl.ds(place_at, 8), :] = given
+            two[g, rows, :] = given
             if at in (low + HALO, high + HALO - 8):
                 cut = (pl.ds(0 if at == low + HALO else 8, 8), pl.ds(g * LANE, LANE))
                 defect_ref[cut] = fine - rough
                 rim_gift_ref[cut] = given
+    for g in range(TILES):
+        for i in range(2):
+            rim_force_ref[g, pl.ds(8 * i, 8), :] = force[g, pl.ds(low + 8 + 8 * i, 8), :]
+            rim_force_ref[g, pl.ds(16 + 8 * i, 8), :] = force[g, pl.ds(high + HALO + 8 * i, 8), :]
+    ends = (low + HALO - FAR, high + HALO + FAR - PIECE)
     for order, out in ((0, mine_ref), (2, one_ref), (3, two_ref)):
         worker = slab ^ partner(order)
 
-        def cut(out, source, starts):
-            for i in range(BOX // 8):
-                at = starts[0] + 8 * i if i < PIECE // 8 else starts[1] + 8 * i - PIECE
+        def cut_rim(order=order, out=out):
+            for n, start in enumerate(ends):
+                for i in range(0, PIECE, 8):
+                    size = min(8, PIECE - i)
+                    for g in range(TILES):
+                        rows = pl.ds(start + i, size)
+                        out[pl.ds(BOX * g + PIECE * n + i, size), :] = two[g, rows, :]
+                        if order == 0:
+                            block_ref[g, pl.ds(PIECE * n + i, size), :] = force[g, rows, :]
+
+        def cut_inner(order=order, out=out, worker=worker):
+            start = PAD + inner_start(worker)
+            for i in range(0, BLOCK, 8):
                 for g in range(TILES):
-                    piece = source[g, pl.ds(at, 8), :]
-                    if len(out.shape) == 3:
-                        out[g, pl.ds(8 * i, 8), :] = piece
-                    else:
-                        out[pl.ds(8 * i, 8), pl.ds(g * LANE, LANE)] = piece
-
-        def cut_all(starts, order=order, out=out):
-            cut(out, gift, starts)
-            if order == 0:
-                cut(block_ref, wide_force, starts)
-
-        @pl.when(worker == RIM_SLAB)
-        def _(cut_all=cut_all):
-            cut_all((base - FAR, base + ROWS + FAR - PIECE))
-
-        @pl.when(worker != RIM_SLAB)
-        def _(cut_all=cut_all, worker=worker):
-            start = base + inner_start(worker)
-            cut_all((start, start + PIECE))
+                    rows = pl.ds(start + i, 8)
+                    out[pl.ds(BOX * g + i, 8), :] = inner_gift_ref[g, rows, :]
+                    if order == 0:
+                        block_ref[g, pl.ds(i, 8), :] = inner_force_ref[g, rows, :]
+
+        pl.when(worker == RIM_SLAB)(cut_rim)
+        pl.when(worker != RIM_SLAB)(cut_inner)
 
 
 def each_place(slab, odd, body):
@@ -277,40 +283,54 @@
     boxes = (mine_ref, one_ref, two_ref, three_ref)
     outs = (out0_ref, out1_ref, out2_ref, out3_ref)
     row_ids = lax.broadcasted_iota(jnp.int32, (8, LANE), 0)
-    masks = {
-        0: up_mask,
-        1: jnp.where(row_ids < FAR - 8, up_mask, 1.0),
-        4: jnp.where(row_ids >= 8 - (FAR - 8), down_mask, 1.0),
-        5: down_mask,
-    }
-
-    def leap(source, target, defect, rim):
-        for i in range((BOX if rim else BLOCK) // 8):
-            at = PAD + 8 * i
-            for g, now, above, below, left, right in row_tile(source, at, lane_ids):
-                inc = increment(now, above, below, left, right, force_ref[g, pl.ds(8 * i, 8), :])
-                new = now + 8.0 * inc + defect[pl.ds(8 * i, 8), pl.ds(g * LANE, LANE)]
-                target[g, pl.ds(at, 8), :] = new * masks[i] if rim and i in masks else new
+    def mask_at(at):
+        row = row_ids + at
+        row = jnp.where(row < PIECE, row - FAR, row + (ROWS + FAR - BOX))
+        return jnp.where(row < 0, up_mask, jnp.where(row >= ROWS, down_mask, 1.0))
+
+    masks = {at: mask_at(at) for at in (0, 8, 32, BOX - 8)}
+
+    def read(box, at, g):
+        if box.shape[1] == COLS:
+            return box[pl.ds(at, 8), pl.ds(g * LANE, LANE)]
+        return box[pl.ds(BOX * g + at, 8), :]
+
+    def leap(source, target, defect, tiles, rim):
+        for at in tiles:
+            for g, now, above, below, left, right in row_tile(source, PAD + at, lane_ids):
+                inc = increment(now, above, below, left, right, force_ref[g, pl.ds(at, 8), :])
+                new = now + 8.0 * inc + read(defect, at, g)
+                target[g, pl.ds(PAD + at, 8), :] = new * masks[at] if rim and at in masks else new
 
     def body(t, order):
         rim = t == RIM_SLAB
-        load(start1, PAD, boxes[order.index(t)], 0, (BOX if rim else BLOCK) // 8, 1.0)
-        leap(start1, start2, boxes[order.index(t ^ 1)], rim)
-        leap(start2, start3, boxes[order.index(t ^ 2)], rim)
+        tiles = BOX_TILES if rim else BOX_TILES[: BLOCK // 8]
+        for at in tiles:
+            for g in range(TILES):
+                start1[g, pl.ds(PAD + at, 8), :] = read(boxes[order.index(t)], at, g)
+        leap(start1, start2, boxes[order.index(t ^ 1)], tiles, rim)
+        leap(start2, start3, boxes[order.index(t ^ 2)], tiles, rim)
         starts = (None, start1, start2, start3)
-        pieces = ((0, 2, EDGE), (EDGE, BOX - 2 - EDGE, EDGE)) if rim else ((0, 2, PART),)
+        pieces = ((0, 2, EDGE), (EDGE, PIECE + 2, EDGE)) if rim else ((0, 2, PART),)
         for k in range(SLABS):
             begin = starts[max(t ^ order[k], 1)]
             for to, at, rows in pieces:
-                for i in range((rows + 7) // 8):
-                    size = min(8, rows - 8 * i)
+                for i in range(0, rows, 8):
+                    size = min(8, rows - i)
                     for g in range(TILES):
-                        outs[k][pl.ds(to + 8 * i, size), pl.ds(g * LANE, LANE)] = begin[g, pl.ds(PAD + at + 8 * i, size), :]
+                        outs[k][pl.ds(PART * g + to + i, size), :] = begin[g, pl.ds(PAD + at + i, size), :]
 
     each_place(slab, odd, body)
 
 
-def first_kernel(inner_gift_ref, rim_gift_ref, new_out, end_out, stage, sems):
+def first_kernel(inner_gift_ref, rim_gift_ref, inner_force_ref, rim_force_ref, new_out, end_out, wide_force, stage, sems):
+    for g in range(TILES):
+        for i in range(2):
+            wide_force[g, pl.ds(8 * i, 8), :] = rim_force_ref[g, pl.ds(8 * i, 8), :]
+            wide_force[g, pl.ds(16 + ROWS + 8 * i, 8), :] = rim_force_ref[g, pl.ds(16 + 8 * i, 8), :]
+        for i in range(ROWS // 8):
+            wide_force[g, pl.ds(16 + 8 * i, 8), :] = inner_force_ref[g, pl.ds(PAD + 8 * i, 8), :]
+
     @pl.when(lax.axis_index("tm") == 0)
     def _():
         last = ROWS // 8 - 1
@@ -348,10 +368,10 @@
             else:
                 pieces = ((0, EDGE - REACH + PART * (w - (w > RIM_SLAB)), PART),)
             for begin, row, rows in pieces:
-                for i in range((rows + 7) // 8):
-                    size = min(8, rows - 8 * i)
+                for i in range(0, rows, 8):
+                    size = min(8, rows - i)
                     for g in range(TILES):
-                        one[g, pl.ds(base + row + 8 * i, size), :] = source[pl.ds(begin + 8 * i, size), pl.ds(g * LANE, LANE)]
+                        one[g, pl.ds(base + row + i, size), :] = source[pl.ds(PART * g + begin + i, size), :]
 
     each_place(slab, odd, body)
 
@@ -412,11 +432,11 @@
 
 
 def call(kernel, outs, scratch, place=pltpu.VMEM, copies=0, **more):
-    spec = pl.BlockSpec(memory_space=place)
+    places = place if isinstance(place, list) else [place] * len(outs)
     return pl.pallas_call(
         kernel,
         out_shape=[jax.ShapeDtypeStruct(shape, jnp.float32) for shape in outs],
-        out_specs=[spec] * len(outs),
+        out_specs=[pl.BlockSpec(memory_space=space) for space in places],
         scratch_shapes=[pltpu.VMEM(shape, jnp.float32) for shape in scratch]
         + [pltpu.SemaphoreType.DMA((copies,))] * (copies > 0),
         compiler_params=pltpu.CompilerParams(vmem_limit_bytes=24 * 1024 * 1024),
@@ -425,16 +445,10 @@
 
 
 def local(c_points, source):
+    count = lax.axis_size("space")
+    edges = (TILES * 2 * DEEP, LANE)
     field = c_points[0]
-    count = lax.axis_size("space")
-    edges = jax.ShapeDtypeStruct((2 * HALO, COLS), jnp.float32)
-    to_intra, to_inter, to_far = pl.pallas_call(
-        pack_kernel,
-        out_shape=[edges, edges, jax.ShapeDtypeStruct((FAR_BOX, COLS), jnp.float32)],
-        in_specs=[pl.BlockSpec(memory_space=pl.ANY)] * 2,
-        out_specs=[pl.BlockSpec(memory_space=pltpu.VMEM)] * 3,
-        scratch_shapes=[pltpu.SemaphoreType.DMA((5,))],
-    )(c_points, source)
+    to_inter, to_far, to_intra = call(pack_kernel, [edges, (FAR_BOX, COLS), edges], [])(field, source)
     pairs = []
     for t in range(lax.axis_size("tm")):
         for strip in range(count):
@@ -450,18 +464,25 @@
     raw = swap_one(to_far, 1)
     defect, gift, force = call(inner_kernel, [(ROWS, COLS), wide, wide], [wide] * 3)(field, source)
     narrow = (TILES, ROWS + 4 * REACH, LANE)
-    rim_defect, mine, one, two, block_force, rim_gift, wide_force = call(
+    box = (TILES * BOX, LANE)
+    rim_defect, mine, one, two, block_force, rim_gift, rim_force = call(
         rim_kernel,
-        [(16, COLS)] + [(BOX, COLS)] * 3 + [(TILES, BOX, LANE), (16, COLS), narrow],
-        [(TILES, 2 * SIDE, LANE)] * 4 + [narrow],
+        [(16, COLS), box, box, box, (TILES, 48, LANE), (16, COLS), (TILES, 32, LANE)],
+        [(TILES, 2 * SIDE, LANE)] * 4,
     )(field, source, intra, inter, gift, force)
     one, two = swap_one(one, 2), swap_one(two, 3)
     far = call(far_kernel, [(BLOCK, COLS)], [(TILES, FAR_BOX + 2 * PAD, LANE)] * 4)(raw, force)[0]
     starts = call(
-        chain_kernel, [(PART, COLS)] * 4, [(TILES, BOX + 2 * PAD, LANE)] * 3
+        chain_kernel, [(TILES * PART, LANE)] * 4, [(TILES, 48 + 2 * PAD, LANE)] * 3
     )(mine, far, one, two, block_force)
     starts = [starts[0]] + [swap_one(starts[order], order) for order in range(1, SLABS)]
-    new, end = call(first_kernel, [(ROWS, COLS)] * 2, [(ROWS, COLS)], pl.ANY, 2)(gift, rim_gift)
+    new, end, wide_force = call(
+        first_kernel,
+        [(ROWS, COLS), (ROWS, COLS), narrow],
+        [(ROWS, COLS)],
+        [pl.ANY, pl.ANY, pltpu.VMEM],
+        2,
+    )(gift, rim_gift, force, rim_force)
     middle = (TILES, ROWS + 2 * REACH + 2 * PAD, LANE)
     inside, outside = pl.BlockSpec(memory_space=pltpu.VMEM), pl.BlockSpec(memory_space=pl.ANY)
     corrected, fine = call(

time: 35.2 us -> 33.7 us (0.957)
  Pallas kernels: 12 us -> 9.81 us
  local copies, waits for them, and re-layouts: 0.01 us -> 2.08 us
  waiting for transfers between devices: 10.4 us -> 9.12 us
    unnamed x4, local copies, waits for them, and re-layouts: 0.01 us -> 2.08 us
    pallas_call x4, Pallas kernels: 4.31 us -> 2.26 us  [the longest x1 1.72 us: local(): call(rim_kernel, [(16, COLS), box, box, box, (TILES, 48, LANE), (16, COLS...]
    ppermute x1, waiting for transfers between devices: 1.64 us -> 0.91 us  [local(): inter = lax.ppermute(to_inter, ('tm', 'space'), pairs)]
    ppermute x6, waiting for transfers between devices: 8.73 us -> 8.21 us  [swap_one(): return lax.ppermute(box, ('tm', 'space'), pairs)]
  transfers between devices with their start and end apart: 8 -> 8, of which waited for: 5 -> 4; matrix products, arithmetic and copies ran while one was open for 0% -> 0% of each run, Pallas kernels for 17% -> 17%
where the time goes in v5:
time: 33.7 us; the launch traced here: 33.6 us
  starting transfers between devices  11.9 us (35%)
  Pallas kernels  9.81 us (29%)
  waiting for transfers between devices  9.12 us (27%)
  local copies, waits for them, and re-layouts  2.08 us (6%)
  between operations  0.7 us (2%)
    ppermute x6, starting transfers between devices, swap_one(): return lax.ppermute(box, ('tm', 'space'), pairs)  8.6 us
    ppermute x6, waiting for transfers between devices, swap_one(): return lax.ppermute(box, ('tm', 'space'), pairs)  8.21 us
    pallas_call x1, Pallas kernels, local(): call(fine_kernel, [(ROWS, COLS)] * 2, [middle] * 2 + [(ROWS, COLS)] * 2,...  3.65 us
    pallas_call x1, Pallas kernels, local(): call(inner_kernel, [(ROWS, COLS), wide, wide], [wide] * 3)(field, source)  2.62 us
    ppermute x1, starting transfers between devices, local(): inter = lax.ppermute(to_inter, ('tm', 'space'), pairs)  2.49 us
    unnamed x4, local copies, waits for them, and re-layouts  2.08 us
    pallas_call x1, Pallas kernels, local(): call(rim_kernel, [(16, COLS), box, box, box, (TILES, 48, LANE), (16, COLS...  1.72 us
    pallas_call x1, Pallas kernels, local(): call(far_kernel, [(BLOCK, COLS)], [(TILES, FAR_BOX + 2 * PAD, LANE)] * 4)  1.28 us
  transfers between devices with their start and end apart: 8, of which 4 were waited for; matrix products, arithmetic and copies ran while one was open for 0% of the time, Pallas kernels for 17%

profile of v5, /device:TPU:123, one launch (start us, length us, event | category | flops | bytes accessed | tf_op | source)
XLA Modules:
  0.0 33.6 jit_solution(6042630575902796044)
XLA Ops:
  0.6 0.0 copy-start
  0.6 1.0 %copy-done = f32[1,128,1024]{2,1,0:T(8,128)S(1)} copy-done((f32[1,128,1024]{2,1,0:T(8,128)S(1)}, f32[1,128,1024]{2,1,0:T(8,128)}, u32[]{:S(2)}) %copy-start) | copy-done | bytes 524312
  1.7 0.0 copy-start.1
  1.7 1.0 %copy-done.1 = f32[128,1024]{1,0:T(8,128)S(1)} copy-done((f32[128,1024]{1,0:T(8,128)S(1)}, f32[128,1024]{1,0:T(8,128)}, u32[]{:S(2)}) %copy-start.1) | copy-done | bytes 524312
  2.7 0.1 shard_map.42
  2.8 0.8 %collective-permute-start = (f32[288,128]{1,0:T(8,128)S(1)}, f32[288,128]{1,0:T(8,128)S(1)}, u32[]{:S(2)}, u32[]{:S(2)}) collective-permute-start(f32[288,128]{1,0:T(8,128)S(1)} %get-tuple-element.25), channel_id=1, source_target_pairs={{0,1},{1,0},{2,3},{3,2},{4,5},{5,4},{6,7},{7,6},{8,9},{9,8},{10,11... | collective-permute-start | bytes 442376 | tf_op jit(solution)/shard_map/ppermute | solution.py:421
  3.6 2.5 %collective-permute-start.1 = (f32[288,128]{1,0:T(8,128)S(1)}, f32[288,128]{1,0:T(8,128)S(1)}, u32[]{:S(2)}, u32[]{:S(2)}) collective-permute-start(f32[288,128]{1,0:T(8,128)S(1)} %get-tuple-element.26), channel_id=1, source_target_pairs={{0,64},{1,2},{2,1},{3,4},{4,3},{5,6},{6,5},{7,8},{8,7},{9,10},{10,... | collective-permute-start | bytes 442376 | tf_op jit(solution)/shard_map/ppermute | solution.py:460
  6.1 1.8 %collective-permute-start.2 = (f32[56,1024]{1,0:T(8,128)S(1)}, f32[56,1024]{1,0:T(8,128)S(1)}, u32[]{:S(2)}, u32[]{:S(2)}) collective-permute-start(f32[56,1024]{1,0:T(8,128)S(1)} %get-tuple-element.34), channel_id=1, source_target_pairs={{0,128},{1,129},{2,130},{3,131},{4,132},{5,133},{6,134},{7,135},{8... | collective-permute-start | bytes 688136 | tf_op jit(solution)/shard_map/ppermute | solution.py:431
  7.9 2.6 %shard_map.41 = (f32[128,1024]{1,0:T(8,128)S(1)}, f32[8,144,128]{2,1,0:T(8,128)S(1)}, f32[8,144,128]{2,1,0:T(8,128)S(1)}) custom-call(f32[128,1024]{1,0:T(8,128)S(1)} %bitcast.4, f32[128,1024]{1,0:T(8,128)S(1)} %copy-done.1), custom_call_target="tpu_custom_call" | custom-call | tf_op jit(solution)/shard_map/pallas_call | solution.py:465
  10.5 0.0 collective-permute-done.intra_ref
  10.5 0.9 %collective-permute-done.1.inter_ref = f32[288,128]{1,0:T(8,128)S(1)} collective-permute-done((f32[288,128]{1,0:T(8,128)S(1)}, f32[288,128]{1,0:T(8,128)S(1)}, u32[]{:S(2)}, u32[]{:S(2)}) %collective-permute-start.1) | collective-permute-done | bytes 147488 | tf_op jit(solution)/shard_map/ppermute | solution.py:460
  11.4 1.7 %shard_map.43 = (f32[16,1024]{1,0:T(8,128)S(1)}, f32[352,128]{1,0:T(8,128)S(1)}, f32[352,128]{1,0:T(8,128)S(1)}, f32[352,128]{1,0:T(8,128)S(1)}, f32[8,48,128]{2...) custom-call(f32[128,1024]{1,0:T(8,128)S(1)} %bitcast.5, f32[128,1024]{1,0:T(8,128)S(1)} %copy-done.1, ...), custom_call_target="tpu_custom_call" | custom-call | tf_op jit(solution)/shard_map/pallas_call | solution.py:468
  13.2 1.3 %collective-permute-start.3 = (f32[352,128]{1,0:T(8,128)S(1)}, f32[352,128]{1,0:T(8,128)S(1)}, u32[]{:S(2)}, u32[]{:S(2)}) collective-permute-start(f32[352,128]{1,0:T(8,128)S(1)} %get-tuple-element.35), channel_id=1, source_target_pairs={{0,64},{1,193},{2,66},{3,195},{4,68},{5,197},{6,70},{7,199},{8,72}... | collective-permute-start | bytes 540680 | tf_op jit(solution)/shard_map/ppermute | solution.py:431
  14.5 1.5 %collective-permute-start.4 = (f32[352,128]{1,0:T(8,128)S(1)}, f32[352,128]{1,0:T(8,128)S(1)}, u32[]{:S(2)}, u32[]{:S(2)}) collective-permute-start(f32[352,128]{1,0:T(8,128)S(1)} %get-tuple-element.36), channel_id=1, source_target_pairs={{0,192},{1,65},{2,194},{3,67},{4,196},{5,69},{6,198},{7,71},{8,200... | collective-permute-start | bytes 540680 | tf_op jit(solution)/shard_map/ppermute | solution.py:431
  16.0 0.0 collective-permute-done.2.raw_ref
  16.0 1.3 %shard_map.45.one_ref = f32[40,1024]{1,0:T(8,128)S(1)} custom-call(f32[56,1024]{1,0:T(8,128)S(1)} %collective-permute-done.2.raw_ref, f32[8,144,128]{2,1,0:T(8,128)S(1)} %get-tuple-element.28.inner_force_ref.force_ref), custom_call_target="tpu_custom_call" | custom-call | tf_op jit(solution)/shard_map/pallas_call | solution.py:474
  17.3 1.9 %collective-permute-done.3.two_ref = f32[352,128]{1,0:T(8,128)S(1)} collective-permute-done((f32[352,128]{1,0:T(8,128)S(1)}, f32[352,128]{1,0:T(8,128)S(1)}, u32[]{:S(2)}, u32[]{:S(2)}) %collective-permute-start.3) | collective-permute-done | bytes 180256 | tf_op jit(solution)/shard_map/ppermute | solution.py:431
  19.2 0.0 collective-permute-done.4.three_ref
  19.2 0.4 %shard_map.46 = (f32[288,128]{1,0:T(8,128)S(1)}, f32[288,128]{1,0:T(8,128)S(1)}, f32[288,128]{1,0:T(8,128)S(1)}, f32[288,128]{1,0:T(8,128)S(1)}) custom-call(f32[352,128]{1,0:T(8,128)S(1)} %get-tuple-element.33.mine_ref, f32[40,1024]{1,0:T(8,128)S(1)} %shard_map.45.one_ref, f32[352,128]{1,0:T(8,128)S(1)} %collective-permute-done.3.two_ref, ...), custom_call_target="tpu_custom_call" | custom-call | tf_op jit(solution)/shard_map/pallas_call | solution.py:475
  19.7 1.5 %collective-permute-start.5 = (f32[288,128]{1,0:T(8,128)S(1)}, f32[288,128]{1,0:T(8,128)S(1)}, u32[]{:S(2)}, u32[]{:S(2)}) collective-permute-start(f32[288,128]{1,0:T(8,128)S(1)} %get-tuple-element.39), channel_id=1, source_target_pairs={{0,128},{1,129},{2,130},{3,131},{4,132},{5,133},{6,134},{7,135},{8... | collective-permute-start | bytes 442376 | tf_op jit(solution)/shard_map/ppermute | solution.py:431
  21.1 1.2 %collective-permute-start.6 = (f32[288,128]{1,0:T(8,128)S(1)}, f32[288,128]{1,0:T(8,128)S(1)}, u32[]{:S(2)}, u32[]{:S(2)}) collective-permute-start(f32[288,128]{1,0:T(8,128)S(1)} %get-tuple-element.40), channel_id=1, source_target_pairs={{0,64},{1,193},{2,66},{3,195},{4,68},{5,197},{6,70},{7,199},{8,72}... | collective-permute-start | bytes 442376 | tf_op jit(solution)/shard_map/ppermute | solution.py:431
  22.4 1.2 %collective-permute-start.7 = (f32[288,128]{1,0:T(8,128)S(1)}, f32[288,128]{1,0:T(8,128)S(1)}, u32[]{:S(2)}, u32[]{:S(2)}) collective-permute-start(f32[288,128]{1,0:T(8,128)S(1)} %get-tuple-element.41), channel_id=1, source_target_pairs={{0,192},{1,65},{2,194},{3,67},{4,196},{5,69},{6,198},{7,71},{8,200... | collective-permute-start | bytes 442376 | tf_op jit(solution)/shard_map/ppermute | solution.py:431
  23.6 0.1 shard_map.44
  23.7 2.7 %collective-permute-done.5.refs_4_ = f32[288,128]{1,0:T(8,128)S(1)} collective-permute-done((f32[288,128]{1,0:T(8,128)S(1)}, f32[288,128]{1,0:T(8,128)S(1)}, u32[]{:S(2)}, u32[]{:S(2)}) %collective-permute-start.5) | collective-permute-done | bytes 147488 | tf_op jit(solution)/shard_map/ppermute | solution.py:431
  26.3 3.6 %collective-permute-done.6.refs_5_ = f32[288,128]{1,0:T(8,128)S(1)} collective-permute-done((f32[288,128]{1,0:T(8,128)S(1)}, f32[288,128]{1,0:T(8,128)S(1)}, u32[]{:S(2)}, u32[]{:S(2)}) %collective-permute-start.6) | collective-permute-done | bytes 147488 | tf_op jit(solution)/shard_map/ppermute | solution.py:431
  29.9 0.0 collective-permute-done.7.refs_6_
  29.9 3.6 %shard_map.47 = (f32[128,1024]{1,0:T(8,128)}, f32[128,1024]{1,0:T(8,128)}) custom-call(f32[128,1024]{1,0:T(8,128)S(1)} %get-tuple-element.24.refs_0_, f32[16,1024]{1,0:T(8,128)S(1)} %get-tuple-element.29.refs_1_, f32[8,160,128]{2,1,0:T(8,128)S(1)} %get-tuple-element.32.refs_2_, ...), custom_call_target="tpu_custom_call", output_to_operand_aliasing={{0}: (7, {}), {1}: (8, {})} | custom-call | tf_op jit(solution)/shard_map/pallas_call | solution.py:488
Async XLA Ops:
  0.6 1.0 %copy-start = (f32[1,128,1024]{2,1,0:T(8,128)S(1)}, f32[1,128,1024]{2,1,0:T(8,128)}, u32[]{:S(2)}) copy-start(f32[1,128,1024]{2,1,0:T(8,128)} %param.2) | copy-start | bytes 1572868
  1.7 1.0 %copy-start.1 = (f32[128,1024]{1,0:T(8,128)S(1)}, f32[128,1024]{1,0:T(8,128)}, u32[]{:S(2)}) copy-start(f32[128,1024]{1,0:T(8,128)} %s_ref.5) | copy-start | bytes 1572868
  2.8 7.7 %collective-permute-start = (f32[288,128]{1,0:T(8,128)S(1)}, f32[288,128]{1,0:T(8,128)S(1)}, u32[]{:S(2)}, u32[]{:S(2)}) collective-permute-start(f32[288,128]{1,0:T(8,128)S(1)} %get-tuple-element.25), channel_id=1, source_target_pairs={{0,1},{1,0},{2,3},{3,2},{4,5},{5,4},{6,7},{7,6},{8,9},{9,8},{10,11... | collective-permute-start | bytes 442376 | tf_op jit(solution)/shard_map/ppermute | solution.py:421
  3.6 7.9 %collective-permute-start.1 = (f32[288,128]{1,0:T(8,128)S(1)}, f32[288,128]{1,0:T(8,128)S(1)}, u32[]{:S(2)}, u32[]{:S(2)}) collective-permute-start(f32[288,128]{1,0:T(8,128)S(1)} %get-tuple-element.26), channel_id=1, source_target_pairs={{0,64},{1,2},{2,1},{3,4},{4,3},{5,6},{6,5},{7,8},{8,7},{9,10},{10,... | collective-permute-start | bytes 442376 | tf_op jit(solution)/shard_map/ppermute | solution.py:460
  6.1 9.9 %collective-permute-start.2 = (f32[56,1024]{1,0:T(8,128)S(1)}, f32[56,1024]{1,0:T(8,128)S(1)}, u32[]{:S(2)}, u32[]{:S(2)}) collective-permute-start(f32[56,1024]{1,0:T(8,128)S(1)} %get-tuple-element.34), channel_id=1, source_target_pairs={{0,128},{1,129},{2,130},{3,131},{4,132},{5,133},{6,134},{7,135},{8... | collective-permute-start | bytes 688136 | tf_op jit(solution)/shard_map/ppermute | solution.py:431
  13.2 6.1 %collective-permute-start.3 = (f32[352,128]{1,0:T(8,128)S(1)}, f32[352,128]{1,0:T(8,128)S(1)}, u32[]{:S(2)}, u32[]{:S(2)}) collective-permute-start(f32[352,128]{1,0:T(8,128)S(1)} %get-tuple-element.35), channel_id=1, source_target_pairs={{0,64},{1,193},{2,66},{3,195},{4,68},{5,197},{6,70},{7,199},{8,72}... | collective-permute-start | bytes 540680 | tf_op jit(solution)/shard_map/ppermute | solution.py:431
  14.5 4.8 %collective-permute-start.4 = (f32[352,128]{1,0:T(8,128)S(1)}, f32[352,128]{1,0:T(8,128)S(1)}, u32[]{:S(2)}, u32[]{:S(2)}) collective-permute-start(f32[352,128]{1,0:T(8,128)S(1)} %get-tuple-element.36), channel_id=1, source_target_pairs={{0,192},{1,65},{2,194},{3,67},{4,196},{5,69},{6,198},{7,71},{8,200... | collective-permute-start | bytes 540680 | tf_op jit(solution)/shard_map/ppermute | solution.py:431
  19.7 6.7 %collective-permute-start.5 = (f32[288,128]{1,0:T(8,128)S(1)}, f32[288,128]{1,0:T(8,128)S(1)}, u32[]{:S(2)}, u32[]{:S(2)}) collective-permute-start(f32[288,128]{1,0:T(8,128)S(1)} %get-tuple-element.39), channel_id=1, source_target_pairs={{0,128},{1,129},{2,130},{3,131},{4,132},{5,133},{6,134},{7,135},{8... | collective-permute-start | bytes 442376 | tf_op jit(solution)/shard_map/ppermute | solution.py:431
  21.1 8.8 %collective-permute-start.6 = (f32[288,128]{1,0:T(8,128)S(1)}, f32[288,128]{1,0:T(8,128)S(1)}, u32[]{:S(2)}, u32[]{:S(2)}) collective-permute-start(f32[288,128]{1,0:T(8,128)S(1)} %get-tuple-element.40), channel_id=1, source_target_pairs={{0,64},{1,193},{2,66},{3,195},{4,68},{5,197},{6,70},{7,199},{8,72}... | collective-permute-start | bytes 442376 | tf_op jit(solution)/shard_map/ppermute | solution.py:431
  22.4 7.6 %collective-permute-start.7 = (f32[288,128]{1,0:T(8,128)S(1)}, f32[288,128]{1,0:T(8,128)S(1)}, u32[]{:S(2)}, u32[]{:S(2)}) collective-permute-start(f32[288,128]{1,0:T(8,128)S(1)} %get-tuple-element.41), channel_id=1, source_target_pairs={{0,192},{1,65},{2,194},{3,67},{4,196},{5,69},{6,198},{7,71},{8,200... | collective-permute-start | bytes 442376 | tf_op jit(solution)/shard_map/ppermute | solution.py:431

commit v6 on v5

--- a/solution.py
+++ b/solution.py
@@ -133,19 +133,29 @@
     return REACH + PART * inner_place(worker)
 
 
-def inner_kernel(c_ref, s_ref, defect_ref, gift_ref, force_ref, one, two, coarse):
+def inner_kernel(c_ref, s_ref, defect_ref, gift_ref, force_ref, trace_ref, one, two, coarse):
     slab = lax.axis_index("tm")
     lane_ids = lanes()
     count = ROWS // 8
     load(one, PAD, c_ref, 0, count, ADVECT)
     load(force_ref, PAD, s_ref, 0, count, ADVECT * FORCE)
     tiles = [PAD + 8 * i for i in range(count)]
+
+    def note(step, state):
+        for n, row in enumerate((REACH, ROWS - 2 * REACH)):
+            for g in range(TILES):
+                trace_ref[step, n, g] = state[g, pl.ds(PAD + row, 8), :]
+
     sweep(one, two, force_ref, tiles, lane_ids, coarse)
+    note(1, two)
     sweep(two, one, force_ref, tiles, lane_ids)
-
-    def pair(_, carry):
+    note(2, one)
+
+    def pair(i, carry):
         sweep(one, two, force_ref, tiles, lane_ids)
+        note(3 + 2 * i, two)
         sweep(two, one, force_ref, tiles, lane_ids)
+        note(4 + 2 * i, one)
         return carry
 
     lax.fori_loop(0, STEPS // 2 - 1, pair, 0)
@@ -186,7 +196,7 @@
             far_ref[pl.ds(8 * i, 8), pl.ds(g * LANE, LANE)] = one[g, rows, :] - first * coarse[g, rows, :]
 
 
-def rim_kernel(c_ref, s_ref, intra_ref, inter_ref, inner_gift_ref, inner_force_ref, defect_ref, mine_ref, one_ref, two_ref, block_ref, rim_gift_ref, rim_force_ref, one, two, force, coarse):
+def rim_kernel(c_ref, s_ref, intra_ref, inter_ref, inner_gift_ref, inner_force_ref, trace_ref, defect_ref, mine_ref, one_ref, two_ref, block_ref, rim_gift_ref, rim_force_ref, one, two, force, coarse):
     slab, odd, up_mask, down_mask = place()
     lane_ids = lanes()
     low, high = PAD, SIDE + PAD
@@ -215,19 +225,28 @@
 
     masks = {low + 8 * i: up_mask for i in range(third)}
     masks.update({high + HALO + 8 * i: down_mask for i in range(third)})
-    sweep(one, two, force, tiles(0, 6), lane_ids, coarse, masks)
-    sweep(two, one, force, tiles(1, 6), lane_ids, None, masks)
-    sweep(one, two, force, tiles(1, 6), lane_ids, None, masks)
-    sweep(two, one, force, tiles(1, 5), lane_ids, None, masks)
-
-    def pair(_, carry):
-        sweep(one, two, force, tiles(1, 5), lane_ids, None, masks)
-        sweep(two, one, force, tiles(1, 5), lane_ids, None, masks)
+
+    def beside(target, piece):
+        for n, at in enumerate((low + HALO + REACH, high + REACH)):
+            for g in range(TILES):
+                target[g, pl.ds(at, 8), :] = piece(n, g)
+
+    def step(source, target, number):
+        beside(source, lambda n, g: trace_ref[number - 1, n, g])
+        sweep(source, target, force, tiles(1, 4), lane_ids, None, masks)
+
+    sweep(one, two, force, tiles(0, 4), lane_ids, coarse, masks)
+    step(two, one, 2)
+
+    def pair(i, carry):
+        step(one, two, 3 + 2 * i)
+        step(two, one, 4 + 2 * i)
         return carry
 
-    lax.fori_loop(0, STEPS // 2 - 2, pair, 0)
+    lax.fori_loop(0, STEPS // 2 - 1, pair, 0)
+    beside(two, lambda n, g: inner_gift_ref[g, pl.ds(PAD + (REACH, ROWS - 2 * REACH)[n], 8), :])
     first = jnp.where(slab == 0, 0.0, 1.0)
-    for at in tiles(1, 5):
+    for at in tiles(1, 4):
         rows = pl.ds(at, 8)
         for g in range(TILES):
             fine = one[g, rows, :]
@@ -462,14 +481,16 @@
 
     wide = (TILES, ROWS + 2 * PAD, LANE)
     raw = swap_one(to_far, 1)
-    defect, gift, force = call(inner_kernel, [(ROWS, COLS), wide, wide], [wide] * 3)(field, source)
+    defect, gift, force, trace = call(
+        inner_kernel, [(ROWS, COLS), wide, wide, (STEPS + 1, 2, TILES, 8, LANE)], [wide] * 3
+    )(field, source)
     narrow = (TILES, ROWS + 4 * REACH, LANE)
     box = (TILES * BOX, LANE)
     rim_defect, mine, one, two, block_force, rim_gift, rim_force = call(
         rim_kernel,
         [(16, COLS), box, box, box, (TILES, 48, LANE), (16, COLS), (TILES, 32, LANE)],
         [(TILES, 2 * SIDE, LANE)] * 4,
-    )(field, source, intra, inter, gift, force)
+    )(field, source, intra, inter, gift, force, trace)
     one, two = swap_one(one, 2), swap_one(two, 3)
     far = call(far_kernel, [(BLOCK, COLS)], [(TILES, FAR_BOX + 2 * PAD, LANE)] * 4)(raw, force)[0]
     starts = call(

time: 33.7 us -> 33.4 us (level)
  transfers between devices with their start and end apart: 8 -> 8, of which waited for: 4 -> 4; matrix products, arithmetic and copies ran while one was open for 0% -> 0% of each run, Pallas kernels for 17% -> 16%
where the time goes in v6:
time: 33.4 us; the launch traced here: 33.3 us
  starting transfers between devices  11.9 us (36%)
  Pallas kernels  9.48 us (28%)
  waiting for transfers between devices  9.14 us (27%)
  local copies, waits for them, and re-layouts  2.08 us (6%)
  between operations  0.7 us (2%)
    ppermute x6, starting transfers between devices, swap_one(): return lax.ppermute(box, ('tm', 'space'), pairs)  8.6 us
    ppermute x6, waiting for transfers between devices, swap_one(): return lax.ppermute(box, ('tm', 'space'), pairs)  8.22 us
    pallas_call x1, Pallas kernels, local(): call(fine_kernel, [(ROWS, COLS)] * 2, [middle] * 2 + [(ROWS, COLS)] * 2,...  3.65 us
    pallas_call x1, Pallas kernels, local(): call(inner_kernel, [(ROWS, COLS), wide, wide, (STEPS + 1, 2, TILES, 8, LA...  2.61 us
    ppermute x1, starting transfers between devices, local(): inter = lax.ppermute(to_inter, ('tm', 'space'), pairs)  2.49 us
    unnamed x4, local copies, waits for them, and re-layouts  2.08 us
    pallas_call x1, Pallas kernels, local(): call(rim_kernel, [(16, COLS), box, box, box, (TILES, 48, LANE), (16, COLS...  1.39 us
    pallas_call x1, Pallas kernels, local(): call(far_kernel, [(BLOCK, COLS)], [(TILES, FAR_BOX + 2 * PAD, LANE)] * 4)  1.28 us
  transfers between devices with their start and end apart: 8, of which 4 were waited for; matrix products, arithmetic and copies ran while one was open for 0% of the time, Pallas kernels for 16%

profile of v6, /device:TPU:123, one launch (start us, length us, event | category | flops | bytes accessed | tf_op | source)
XLA Modules:
  0.0 33.3 jit_solution(988780091915130411)
XLA Ops:
  0.6 0.0 copy-start
  0.6 1.0 %copy-done = f32[1,128,1024]{2,1,0:T(8,128)S(1)} copy-done((f32[1,128,1024]{2,1,0:T(8,128)S(1)}, f32[1,128,1024]{2,1,0:T(8,128)}, u32[]{:S(2)}) %copy-start) | copy-done | bytes 524312
  1.7 0.0 copy-start.1
  1.7 1.0 %copy-done.1 = f32[128,1024]{1,0:T(8,128)S(1)} copy-done((f32[128,1024]{1,0:T(8,128)S(1)}, f32[128,1024]{1,0:T(8,128)}, u32[]{:S(2)}) %copy-start.1) | copy-done | bytes 524312
  2.7 0.1 shard_map.42
  2.8 0.8 %collective-permute-start = (f32[288,128]{1,0:T(8,128)S(1)}, f32[288,128]{1,0:T(8,128)S(1)}, u32[]{:S(2)}, u32[]{:S(2)}) collective-permute-start(f32[288,128]{1,0:T(8,128)S(1)} %get-tuple-element.26), channel_id=1, source_target_pairs={{0,1},{1,0},{2,3},{3,2},{4,5},{5,4},{6,7},{7,6},{8,9},{9,8},{10,11... | collective-permute-start | bytes 442376 | tf_op jit(solution)/shard_map/ppermute | solution.py:440
  3.6 2.5 %collective-permute-start.1 = (f32[288,128]{1,0:T(8,128)S(1)}, f32[288,128]{1,0:T(8,128)S(1)}, u32[]{:S(2)}, u32[]{:S(2)}) collective-permute-start(f32[288,128]{1,0:T(8,128)S(1)} %get-tuple-element.27), channel_id=1, source_target_pairs={{0,64},{1,2},{2,1},{3,4},{4,3},{5,6},{6,5},{7,8},{8,7},{9,10},{10,... | collective-permute-start | bytes 442376 | tf_op jit(solution)/shard_map/ppermute | solution.py:479
  6.1 1.8 %collective-permute-start.2 = (f32[56,1024]{1,0:T(8,128)S(1)}, f32[56,1024]{1,0:T(8,128)S(1)}, u32[]{:S(2)}, u32[]{:S(2)}) collective-permute-start(f32[56,1024]{1,0:T(8,128)S(1)} %get-tuple-element.36), channel_id=1, source_target_pairs={{0,128},{1,129},{2,130},{3,131},{4,132},{5,133},{6,134},{7,135},{8... | collective-permute-start | bytes 688136 | tf_op jit(solution)/shard_map/ppermute | solution.py:450
  7.9 2.6 %shard_map.41 = (f32[128,1024]{1,0:T(8,128)S(1)}, f32[8,144,128]{2,1,0:T(8,128)S(1)}, f32[8,144,128]{2,1,0:T(8,128)S(1)}, f32[9,2,8,8,128]{4,3,2,1,0:T(8,128)S(1)}) custom-call(f32[128,1024]{1,0:T(8,128)S(1)} %bitcast.4, f32[128,1024]{1,0:T(8,128)S(1)} %copy-done.1), custom_call_target="tpu_custom_call" | custom-call | tf_op jit(solution)/shard_map/pallas_call | solution.py:484
  10.5 0.0 collective-permute-done.intra_ref
  10.5 0.9 %collective-permute-done.1.inter_ref = f32[288,128]{1,0:T(8,128)S(1)} collective-permute-done((f32[288,128]{1,0:T(8,128)S(1)}, f32[288,128]{1,0:T(8,128)S(1)}, u32[]{:S(2)}, u32[]{:S(2)}) %collective-permute-start.1) | collective-permute-done | bytes 147488 | tf_op jit(solution)/shard_map/ppermute | solution.py:479
  11.4 1.4 %shard_map.43 = (f32[16,1024]{1,0:T(8,128)S(1)}, f32[352,128]{1,0:T(8,128)S(1)}, f32[352,128]{1,0:T(8,128)S(1)}, f32[352,128]{1,0:T(8,128)S(1)}, f32[8,48,128]{2...) custom-call(f32[128,1024]{1,0:T(8,128)S(1)} %bitcast.5, f32[128,1024]{1,0:T(8,128)S(1)} %copy-done.1, ...), custom_call_target="tpu_custom_call" | custom-call | tf_op jit(solution)/shard_map/pallas_call | solution.py:489
  12.8 1.3 %collective-permute-start.3 = (f32[352,128]{1,0:T(8,128)S(1)}, f32[352,128]{1,0:T(8,128)S(1)}, u32[]{:S(2)}, u32[]{:S(2)}) collective-permute-start(f32[352,128]{1,0:T(8,128)S(1)} %get-tuple-element.37), channel_id=1, source_target_pairs={{0,64},{1,193},{2,66},{3,195},{4,68},{5,197},{6,70},{7,199},{8,72}... | collective-permute-start | bytes 540680 | tf_op jit(solution)/shard_map/ppermute | solution.py:450
  14.1 1.5 %collective-permute-start.4 = (f32[352,128]{1,0:T(8,128)S(1)}, f32[352,128]{1,0:T(8,128)S(1)}, u32[]{:S(2)}, u32[]{:S(2)}) collective-permute-start(f32[352,128]{1,0:T(8,128)S(1)} %get-tuple-element.38), channel_id=1, source_target_pairs={{0,192},{1,65},{2,194},{3,67},{4,196},{5,69},{6,198},{7,71},{8,200... | collective-permute-start | bytes 540680 | tf_op jit(solution)/shard_map/ppermute | solution.py:450
  15.7 0.0 collective-permute-done.2.raw_ref
  15.7 1.3 %shard_map.45.one_ref = f32[40,1024]{1,0:T(8,128)S(1)} custom-call(f32[56,1024]{1,0:T(8,128)S(1)} %collective-permute-done.2.raw_ref, f32[8,144,128]{2,1,0:T(8,128)S(1)} %get-tuple-element.29.inner_force_ref.force_ref), custom_call_target="tpu_custom_call" | custom-call | tf_op jit(solution)/shard_map/pallas_call | solution.py:495
  17.0 1.9 %collective-permute-done.3.two_ref = f32[352,128]{1,0:T(8,128)S(1)} collective-permute-done((f32[352,128]{1,0:T(8,128)S(1)}, f32[352,128]{1,0:T(8,128)S(1)}, u32[]{:S(2)}, u32[]{:S(2)}) %collective-permute-start.3) | collective-permute-done | bytes 180256 | tf_op jit(solution)/shard_map/ppermute | solution.py:450
  18.9 0.0 collective-permute-done.4.three_ref
  18.9 0.4 %shard_map.46 = (f32[288,128]{1,0:T(8,128)S(1)}, f32[288,128]{1,0:T(8,128)S(1)}, f32[288,128]{1,0:T(8,128)S(1)}, f32[288,128]{1,0:T(8,128)S(1)}) custom-call(f32[352,128]{1,0:T(8,128)S(1)} %get-tuple-element.35.mine_ref, f32[40,1024]{1,0:T(8,128)S(1)} %shard_map.45.one_ref, f32[352,128]{1,0:T(8,128)S(1)} %collective-permute-done.3.two_ref, ...), custom_call_target="tpu_custom_call" | custom-call | tf_op jit(solution)/shard_map/pallas_call | solution.py:496
  19.3 1.5 %collective-permute-start.5 = (f32[288,128]{1,0:T(8,128)S(1)}, f32[288,128]{1,0:T(8,128)S(1)}, u32[]{:S(2)}, u32[]{:S(2)}) collective-permute-start(f32[288,128]{1,0:T(8,128)S(1)} %get-tuple-element.41), channel_id=1, source_target_pairs={{0,128},{1,129},{2,130},{3,131},{4,132},{5,133},{6,134},{7,135},{8... | collective-permute-start | bytes 442376 | tf_op jit(solution)/shard_map/ppermute | solution.py:450
  20.8 1.2 %collective-permute-start.6 = (f32[288,128]{1,0:T(8,128)S(1)}, f32[288,128]{1,0:T(8,128)S(1)}, u32[]{:S(2)}, u32[]{:S(2)}) collective-permute-start(f32[288,128]{1,0:T(8,128)S(1)} %get-tuple-element.42), channel_id=1, source_target_pairs={{0,64},{1,193},{2,66},{3,195},{4,68},{5,197},{6,70},{7,199},{8,72}... | collective-permute-start | bytes 442376 | tf_op jit(solution)/shard_map/ppermute | solution.py:450
  22.0 1.2 %collective-permute-start.7 = (f32[288,128]{1,0:T(8,128)S(1)}, f32[288,128]{1,0:T(8,128)S(1)}, u32[]{:S(2)}, u32[]{:S(2)}) collective-permute-start(f32[288,128]{1,0:T(8,128)S(1)} %get-tuple-element.43), channel_id=1, source_target_pairs={{0,192},{1,65},{2,194},{3,67},{4,196},{5,69},{6,198},{7,71},{8,200... | collective-permute-start | bytes 442376 | tf_op jit(solution)/shard_map/ppermute | solution.py:450
  23.3 0.1 shard_map.44
  23.3 2.7 %collective-permute-done.5.refs_4_ = f32[288,128]{1,0:T(8,128)S(1)} collective-permute-done((f32[288,128]{1,0:T(8,128)S(1)}, f32[288,128]{1,0:T(8,128)S(1)}, u32[]{:S(2)}, u32[]{:S(2)}) %collective-permute-start.5) | collective-permute-done | bytes 147488 | tf_op jit(solution)/shard_map/ppermute | solution.py:450
  26.0 3.6 %collective-permute-done.6.refs_5_ = f32[288,128]{1,0:T(8,128)S(1)} collective-permute-done((f32[288,128]{1,0:T(8,128)S(1)}, f32[288,128]{1,0:T(8,128)S(1)}, u32[]{:S(2)}, u32[]{:S(2)}) %collective-permute-start.6) | collective-permute-done | bytes 147488 | tf_op jit(solution)/shard_map/ppermute | solution.py:450
  29.6 0.0 collective-permute-done.7.refs_6_
  29.6 3.6 %shard_map.47 = (f32[128,1024]{1,0:T(8,128)}, f32[128,1024]{1,0:T(8,128)}) custom-call(f32[128,1024]{1,0:T(8,128)S(1)} %get-tuple-element.25.refs_0_, f32[16,1024]{1,0:T(8,128)S(1)} %get-tuple-element.31.refs_1_, f32[8,160,128]{2,1,0:T(8,128)S(1)} %get-tuple-element.34.refs_2_, ...), custom_call_target="tpu_custom_call", output_to_operand_aliasing={{0}: (7, {}), {1}: (8, {})} | custom-call | tf_op jit(solution)/shard_map/pallas_call | solution.py:509
Async XLA Ops:
  0.6 1.0 %copy-start = (f32[1,128,1024]{2,1,0:T(8,128)S(1)}, f32[1,128,1024]{2,1,0:T(8,128)}, u32[]{:S(2)}) copy-start(f32[1,128,1024]{2,1,0:T(8,128)} %param.2) | copy-start | bytes 1572868
  1.7 1.0 %copy-start.1 = (f32[128,1024]{1,0:T(8,128)S(1)}, f32[128,1024]{1,0:T(8,128)}, u32[]{:S(2)}) copy-start(f32[128,1024]{1,0:T(8,128)} %s_ref.5) | copy-start | bytes 1572868
  2.8 7.7 %collective-permute-start = (f32[288,128]{1,0:T(8,128)S(1)}, f32[288,128]{1,0:T(8,128)S(1)}, u32[]{:S(2)}, u32[]{:S(2)}) collective-permute-start(f32[288,128]{1,0:T(8,128)S(1)} %get-tuple-element.26), channel_id=1, source_target_pairs={{0,1},{1,0},{2,3},{3,2},{4,5},{5,4},{6,7},{7,6},{8,9},{9,8},{10,11... | collective-permute-start | bytes 442376 | tf_op jit(solution)/shard_map/ppermute | solution.py:440
  3.6 7.9 %collective-permute-start.1 = (f32[288,128]{1,0:T(8,128)S(1)}, f32[288,128]{1,0:T(8,128)S(1)}, u32[]{:S(2)}, u32[]{:S(2)}) collective-permute-start(f32[288,128]{1,0:T(8,128)S(1)} %get-tuple-element.27), channel_id=1, source_target_pairs={{0,64},{1,2},{2,1},{3,4},{4,3},{5,6},{6,5},{7,8},{8,7},{9,10},{10,... | collective-permute-start | bytes 442376 | tf_op jit(solution)/shard_map/ppermute | solution.py:479
  6.1 9.6 %collective-permute-start.2 = (f32[56,1024]{1,0:T(8,128)S(1)}, f32[56,1024]{1,0:T(8,128)S(1)}, u32[]{:S(2)}, u32[]{:S(2)}) collective-permute-start(f32[56,1024]{1,0:T(8,128)S(1)} %get-tuple-element.36), channel_id=1, source_target_pairs={{0,128},{1,129},{2,130},{3,131},{4,132},{5,133},{6,134},{7,135},{8... | collective-permute-start | bytes 688136 | tf_op jit(solution)/shard_map/ppermute | solution.py:450
  12.8 6.0 %collective-permute-start.3 = (f32[352,128]{1,0:T(8,128)S(1)}, f32[352,128]{1,0:T(8,128)S(1)}, u32[]{:S(2)}, u32[]{:S(2)}) collective-permute-start(f32[352,128]{1,0:T(8,128)S(1)} %get-tuple-element.37), channel_id=1, source_target_pairs={{0,64},{1,193},{2,66},{3,195},{4,68},{5,197},{6,70},{7,199},{8,72}... | collective-permute-start | bytes 540680 | tf_op jit(solution)/shard_map/ppermute | solution.py:450
  14.1 4.7 %collective-permute-start.4 = (f32[352,128]{1,0:T(8,128)S(1)}, f32[352,128]{1,0:T(8,128)S(1)}, u32[]{:S(2)}, u32[]{:S(2)}) collective-permute-start(f32[352,128]{1,0:T(8,128)S(1)} %get-tuple-element.38), channel_id=1, source_target_pairs={{0,192},{1,65},{2,194},{3,67},{4,196},{5,69},{6,198},{7,71},{8,200... | collective-permute-start | bytes 540680 | tf_op jit(solution)/shard_map/ppermute | solution.py:450
  19.3 6.7 %collective-permute-start.5 = (f32[288,128]{1,0:T(8,128)S(1)}, f32[288,128]{1,0:T(8,128)S(1)}, u32[]{:S(2)}, u32[]{:S(2)}) collective-permute-start(f32[288,128]{1,0:T(8,128)S(1)} %get-tuple-element.41), channel_id=1, source_target_pairs={{0,128},{1,129},{2,130},{3,131},{4,132},{5,133},{6,134},{7,135},{8... | collective-permute-start | bytes 442376 | tf_op jit(solution)/shard_map/ppermute | solution.py:450
  20.8 8.8 %collective-permute-start.6 = (f32[288,128]{1,0:T(8,128)S(1)}, f32[288,128]{1,0:T(8,128)S(1)}, u32[]{:S(2)}, u32[]{:S(2)}) collective-permute-start(f32[288,128]{1,0:T(8,128)S(1)} %get-tuple-element.42), channel_id=1, source_target_pairs={{0,64},{1,193},{2,66},{3,195},{4,68},{5,197},{6,70},{7,199},{8,72}... | collective-permute-start | bytes 442376 | tf_op jit(solution)/shard_map/ppermute | solution.py:450
  22.0 7.6 %collective-permute-start.7 = (f32[288,128]{1,0:T(8,128)S(1)}, f32[288,128]{1,0:T(8,128)S(1)}, u32[]{:S(2)}, u32[]{:S(2)}) collective-permute-start(f32[288,128]{1,0:T(8,128)S(1)} %get-tuple-element.43), channel_id=1, source_target_pairs={{0,192},{1,65},{2,194},{3,67},{4,196},{5,69},{6,198},{7,71},{8,200... | collective-permute-start | bytes 442376 | tf_op jit(solution)/shard_map/ppermute | solution.py:450

commit v7 on v6

--- a/solution.py
+++ b/solution.py
@@ -421,8 +421,14 @@
         sweep(one, two, force, tiles, lane_ids, None, masks)
         return carry
 
-    lax.fori_loop(0, STEPS // 2 - 1, pair, 0)
-    for at in tiles[1:-1]:
+    lax.fori_loop(0, STEPS // 2 - 2, pair, 0)
+    sweep(two, one, force, tiles, lane_ids, None, masks)
+    sweep(one, two, force, tiles[:1], lane_ids, None, masks)
+    for n, at in enumerate(tiles[1:]):
+        sweep(one, two, force, [at], lane_ids, None, masks)
+        at = tiles[n]
+        if n == 0:
+            continue
         for g, now, above, below, left, right in row_tile(two, at, lane_ids):
             inc = increment(now, above, below, left, right, force[g, pl.ds(at, 8), :])
             end_ref[pl.ds(at - base, 8), pl.ds(g * LANE, LANE)] = (now + inc) * (1.0 / ADVECT)

time: 33.4 us -> 33.7 us (level)
  no operation moved by 1% of the time
where the time goes in v7:
time: 33.7 us; the launch traced here: 33.5 us
  starting transfers between devices  11.9 us (35%)
  Pallas kernels  9.74 us (29%)
  waiting for transfers between devices  9.14 us (27%)
  local copies, waits for them, and re-layouts  2.08 us (6%)
  between operations  0.7 us (2%)
    ppermute x6, starting transfers between devices, swap_one(): return lax.ppermute(box, ('tm', 'space'), pairs)  8.6 us
    ppermute x6, waiting for transfers between devices, swap_one(): return lax.ppermute(box, ('tm', 'space'), pairs)  8.22 us
    pallas_call x1, Pallas kernels, local(): call(fine_kernel, [(ROWS, COLS)] * 2, [middle] * 2 + [(ROWS, COLS)] * 2,...  3.9 us
    pallas_call x1, Pallas kernels, local(): call(inner_kernel, [(ROWS, COLS), wide, wide, (STEPS + 1, 2, TILES, 8, LA...  2.61 us
    ppermute x1, starting transfers between devices, local(): inter = lax.ppermute(to_inter, ('tm', 'space'), pairs)  2.49 us
    unnamed x4, local copies, waits for them, and re-layouts  2.08 us
    pallas_call x1, Pallas kernels, local(): call(rim_kernel, [(16, COLS), box, box, box, (TILES, 48, LANE), (16, COLS...  1.39 us
    pallas_call x1, Pallas kernels, local(): call(far_kernel, [(BLOCK, COLS)], [(TILES, FAR_BOX + 2 * PAD, LANE)] * 4)  1.28 us
  transfers between devices with their start and end apart: 8, of which 4 were waited for; matrix products, arithmetic and copies ran while one was open for 0% of the time, Pallas kernels for 16%

profile of v7, /device:TPU:123, one launch (start us, length us, event | category | flops | bytes accessed | tf_op | source)
XLA Modules:
  0.0 33.5 jit_solution(17198944581149587215)
XLA Ops:
  0.6 0.0 copy-start
  0.6 1.0 %copy-done = f32[1,128,1024]{2,1,0:T(8,128)S(1)} copy-done((f32[1,128,1024]{2,1,0:T(8,128)S(1)}, f32[1,128,1024]{2,1,0:T(8,128)}, u32[]{:S(2)}) %copy-start) | copy-done | bytes 524312
  1.7 0.0 copy-start.1
  1.7 1.0 %copy-done.1 = f32[128,1024]{1,0:T(8,128)S(1)} copy-done((f32[128,1024]{1,0:T(8,128)S(1)}, f32[128,1024]{1,0:T(8,128)}, u32[]{:S(2)}) %copy-start.1) | copy-done | bytes 524312
  2.7 0.1 shard_map.42
  2.8 0.8 %collective-permute-start = (f32[288,128]{1,0:T(8,128)S(1)}, f32[288,128]{1,0:T(8,128)S(1)}, u32[]{:S(2)}, u32[]{:S(2)}) collective-permute-start(f32[288,128]{1,0:T(8,128)S(1)} %get-tuple-element.26), channel_id=1, source_target_pairs={{0,1},{1,0},{2,3},{3,2},{4,5},{5,4},{6,7},{7,6},{8,9},{9,8},{10,11... | collective-permute-start | bytes 442376 | tf_op jit(solution)/shard_map/ppermute | solution.py:446
  3.6 2.5 %collective-permute-start.1 = (f32[288,128]{1,0:T(8,128)S(1)}, f32[288,128]{1,0:T(8,128)S(1)}, u32[]{:S(2)}, u32[]{:S(2)}) collective-permute-start(f32[288,128]{1,0:T(8,128)S(1)} %get-tuple-element.27), channel_id=1, source_target_pairs={{0,64},{1,2},{2,1},{3,4},{4,3},{5,6},{6,5},{7,8},{8,7},{9,10},{10,... | collective-permute-start | bytes 442376 | tf_op jit(solution)/shard_map/ppermute | solution.py:485
  6.1 1.8 %collective-permute-start.2 = (f32[56,1024]{1,0:T(8,128)S(1)}, f32[56,1024]{1,0:T(8,128)S(1)}, u32[]{:S(2)}, u32[]{:S(2)}) collective-permute-start(f32[56,1024]{1,0:T(8,128)S(1)} %get-tuple-element.36), channel_id=1, source_target_pairs={{0,128},{1,129},{2,130},{3,131},{4,132},{5,133},{6,134},{7,135},{8... | collective-permute-start | bytes 688136 | tf_op jit(solution)/shard_map/ppermute | solution.py:456
  7.9 2.6 %shard_map.41 = (f32[128,1024]{1,0:T(8,128)S(1)}, f32[8,144,128]{2,1,0:T(8,128)S(1)}, f32[8,144,128]{2,1,0:T(8,128)S(1)}, f32[9,2,8,8,128]{4,3,2,1,0:T(8,128)S(1)}) custom-call(f32[128,1024]{1,0:T(8,128)S(1)} %bitcast.4, f32[128,1024]{1,0:T(8,128)S(1)} %copy-done.1), custom_call_target="tpu_custom_call" | custom-call | tf_op jit(solution)/shard_map/pallas_call | solution.py:490
  10.5 0.0 collective-permute-done.intra_ref
  10.5 0.9 %collective-permute-done.1.inter_ref = f32[288,128]{1,0:T(8,128)S(1)} collective-permute-done((f32[288,128]{1,0:T(8,128)S(1)}, f32[288,128]{1,0:T(8,128)S(1)}, u32[]{:S(2)}, u32[]{:S(2)}) %collective-permute-start.1) | collective-permute-done | bytes 147488 | tf_op jit(solution)/shard_map/ppermute | solution.py:485
  11.4 1.4 %shard_map.43 = (f32[16,1024]{1,0:T(8,128)S(1)}, f32[352,128]{1,0:T(8,128)S(1)}, f32[352,128]{1,0:T(8,128)S(1)}, f32[352,128]{1,0:T(8,128)S(1)}, f32[8,48,128]{2...) custom-call(f32[128,1024]{1,0:T(8,128)S(1)} %bitcast.5, f32[128,1024]{1,0:T(8,128)S(1)} %copy-done.1, ...), custom_call_target="tpu_custom_call" | custom-call | tf_op jit(solution)/shard_map/pallas_call | solution.py:495
  12.8 1.3 %collective-permute-start.3 = (f32[352,128]{1,0:T(8,128)S(1)}, f32[352,128]{1,0:T(8,128)S(1)}, u32[]{:S(2)}, u32[]{:S(2)}) collective-permute-start(f32[352,128]{1,0:T(8,128)S(1)} %get-tuple-element.37), channel_id=1, source_target_pairs={{0,64},{1,193},{2,66},{3,195},{4,68},{5,197},{6,70},{7,199},{8,72}... | collective-permute-start | bytes 540680 | tf_op jit(solution)/shard_map/ppermute | solution.py:456
  14.1 1.5 %collective-permute-start.4 = (f32[352,128]{1,0:T(8,128)S(1)}, f32[352,128]{1,0:T(8,128)S(1)}, u32[]{:S(2)}, u32[]{:S(2)}) collective-permute-start(f32[352,128]{1,0:T(8,128)S(1)} %get-tuple-element.38), channel_id=1, source_target_pairs={{0,192},{1,65},{2,194},{3,67},{4,196},{5,69},{6,198},{7,71},{8,200... | collective-permute-start | bytes 540680 | tf_op jit(solution)/shard_map/ppermute | solution.py:456
  15.7 0.0 collective-permute-done.2.raw_ref
  15.7 1.3 %shard_map.45.one_ref = f32[40,1024]{1,0:T(8,128)S(1)} custom-call(f32[56,1024]{1,0:T(8,128)S(1)} %collective-permute-done.2.raw_ref, f32[8,144,128]{2,1,0:T(8,128)S(1)} %get-tuple-element.29.inner_force_ref.force_ref), custom_call_target="tpu_custom_call" | custom-call | tf_op jit(solution)/shard_map/pallas_call | solution.py:501
  17.0 1.9 %collective-permute-done.3.two_ref = f32[352,128]{1,0:T(8,128)S(1)} collective-permute-done((f32[352,128]{1,0:T(8,128)S(1)}, f32[352,128]{1,0:T(8,128)S(1)}, u32[]{:S(2)}, u32[]{:S(2)}) %collective-permute-start.3) | collective-permute-done | bytes 180256 | tf_op jit(solution)/shard_map/ppermute | solution.py:456
  18.9 0.0 collective-permute-done.4.three_ref
  18.9 0.4 %shard_map.46 = (f32[288,128]{1,0:T(8,128)S(1)}, f32[288,128]{1,0:T(8,128)S(1)}, f32[288,128]{1,0:T(8,128)S(1)}, f32[288,128]{1,0:T(8,128)S(1)}) custom-call(f32[352,128]{1,0:T(8,128)S(1)} %get-tuple-element.35.mine_ref, f32[40,1024]{1,0:T(8,128)S(1)} %shard_map.45.one_ref, f32[352,128]{1,0:T(8,128)S(1)} %collective-permute-done.3.two_ref, ...), custom_call_target="tpu_custom_call" | custom-call | tf_op jit(solution)/shard_map/pallas_call | solution.py:502
  19.3 1.5 %collective-permute-start.5 = (f32[288,128]{1,0:T(8,128)S(1)}, f32[288,128]{1,0:T(8,128)S(1)}, u32[]{:S(2)}, u32[]{:S(2)}) collective-permute-start(f32[288,128]{1,0:T(8,128)S(1)} %get-tuple-element.41), channel_id=1, source_target_pairs={{0,128},{1,129},{2,130},{3,131},{4,132},{5,133},{6,134},{7,135},{8... | collective-permute-start | bytes 442376 | tf_op jit(solution)/shard_map/ppermute | solution.py:456
  20.8 1.2 %collective-permute-start.6 = (f32[288,128]{1,0:T(8,128)S(1)}, f32[288,128]{1,0:T(8,128)S(1)}, u32[]{:S(2)}, u32[]{:S(2)}) collective-permute-start(f32[288,128]{1,0:T(8,128)S(1)} %get-tuple-element.42), channel_id=1, source_target_pairs={{0,64},{1,193},{2,66},{3,195},{4,68},{5,197},{6,70},{7,199},{8,72}... | collective-permute-start | bytes 442376 | tf_op jit(solution)/shard_map/ppermute | solution.py:456
  22.0 1.2 %collective-permute-start.7 = (f32[288,128]{1,0:T(8,128)S(1)}, f32[288,128]{1,0:T(8,128)S(1)}, u32[]{:S(2)}, u32[]{:S(2)}) collective-permute-start(f32[288,128]{1,0:T(8,128)S(1)} %get-tuple-element.43), channel_id=1, source_target_pairs={{0,192},{1,65},{2,194},{3,67},{4,196},{5,69},{6,198},{7,71},{8,200... | collective-permute-start | bytes 442376 | tf_op jit(solution)/shard_map/ppermute | solution.py:456
  23.3 0.1 shard_map.44
  23.3 2.7 %collective-permute-done.5.refs_4_ = f32[288,128]{1,0:T(8,128)S(1)} collective-permute-done((f32[288,128]{1,0:T(8,128)S(1)}, f32[288,128]{1,0:T(8,128)S(1)}, u32[]{:S(2)}, u32[]{:S(2)}) %collective-permute-start.5) | collective-permute-done | bytes 147488 | tf_op jit(solution)/shard_map/ppermute | solution.py:456
  26.0 3.6 %collective-permute-done.6.refs_5_ = f32[288,128]{1,0:T(8,128)S(1)} collective-permute-done((f32[288,128]{1,0:T(8,128)S(1)}, f32[288,128]{1,0:T(8,128)S(1)}, u32[]{:S(2)}, u32[]{:S(2)}) %collective-permute-start.6) | collective-permute-done | bytes 147488 | tf_op jit(solution)/shard_map/ppermute | solution.py:456
  29.6 0.0 collective-permute-done.7.refs_6_
  29.6 3.9 %shard_map.47 = (f32[128,1024]{1,0:T(8,128)}, f32[128,1024]{1,0:T(8,128)}) custom-call(f32[128,1024]{1,0:T(8,128)S(1)} %get-tuple-element.25.refs_0_, f32[16,1024]{1,0:T(8,128)S(1)} %get-tuple-element.31.refs_1_, f32[8,160,128]{2,1,0:T(8,128)S(1)} %get-tuple-element.34.refs_2_, ...), custom_call_target="tpu_custom_call", output_to_operand_aliasing={{0}: (7, {}), {1}: (8, {})} | custom-call | tf_op jit(solution)/shard_map/pallas_call | solution.py:515
Async XLA Ops:
  0.6 1.0 %copy-start = (f32[1,128,1024]{2,1,0:T(8,128)S(1)}, f32[1,128,1024]{2,1,0:T(8,128)}, u32[]{:S(2)}) copy-start(f32[1,128,1024]{2,1,0:T(8,128)} %param.2) | copy-start | bytes 1572868
  1.7 1.0 %copy-start.1 = (f32[128,1024]{1,0:T(8,128)S(1)}, f32[128,1024]{1,0:T(8,128)}, u32[]{:S(2)}) copy-start(f32[128,1024]{1,0:T(8,128)} %s_ref.5) | copy-start | bytes 1572868
  2.8 7.7 %collective-permute-start = (f32[288,128]{1,0:T(8,128)S(1)}, f32[288,128]{1,0:T(8,128)S(1)}, u32[]{:S(2)}, u32[]{:S(2)}) collective-permute-start(f32[288,128]{1,0:T(8,128)S(1)} %get-tuple-element.26), channel_id=1, source_target_pairs={{0,1},{1,0},{2,3},{3,2},{4,5},{5,4},{6,7},{7,6},{8,9},{9,8},{10,11... | collective-permute-start | bytes 442376 | tf_op jit(solution)/shard_map/ppermute | solution.py:446
  3.6 7.9 %collective-permute-start.1 = (f32[288,128]{1,0:T(8,128)S(1)}, f32[288,128]{1,0:T(8,128)S(1)}, u32[]{:S(2)}, u32[]{:S(2)}) collective-permute-start(f32[288,128]{1,0:T(8,128)S(1)} %get-tuple-element.27), channel_id=1, source_target_pairs={{0,64},{1,2},{2,1},{3,4},{4,3},{5,6},{6,5},{7,8},{8,7},{9,10},{10,... | collective-permute-start | bytes 442376 | tf_op jit(solution)/shard_map/ppermute | solution.py:485
  6.1 9.6 %collective-permute-start.2 = (f32[56,1024]{1,0:T(8,128)S(1)}, f32[56,1024]{1,0:T(8,128)S(1)}, u32[]{:S(2)}, u32[]{:S(2)}) collective-permute-start(f32[56,1024]{1,0:T(8,128)S(1)} %get-tuple-element.36), channel_id=1, source_target_pairs={{0,128},{1,129},{2,130},{3,131},{4,132},{5,133},{6,134},{7,135},{8... | collective-permute-start | bytes 688136 | tf_op jit(solution)/shard_map/ppermute | solution.py:456
  12.8 6.0 %collective-permute-start.3 = (f32[352,128]{1,0:T(8,128)S(1)}, f32[352,128]{1,0:T(8,128)S(1)}, u32[]{:S(2)}, u32[]{:S(2)}) collective-permute-start(f32[352,128]{1,0:T(8,128)S(1)} %get-tuple-element.37), channel_id=1, source_target_pairs={{0,64},{1,193},{2,66},{3,195},{4,68},{5,197},{6,70},{7,199},{8,72}... | collective-permute-start | bytes 540680 | tf_op jit(solution)/shard_map/ppermute | solution.py:456
  14.1 4.7 %collective-permute-start.4 = (f32[352,128]{1,0:T(8,128)S(1)}, f32[352,128]{1,0:T(8,128)S(1)}, u32[]{:S(2)}, u32[]{:S(2)}) collective-permute-start(f32[352,128]{1,0:T(8,128)S(1)} %get-tuple-element.38), channel_id=1, source_target_pairs={{0,192},{1,65},{2,194},{3,67},{4,196},{5,69},{6,198},{7,71},{8,200... | collective-permute-start | bytes 540680 | tf_op jit(solution)/shard_map/ppermute | solution.py:456
  19.3 6.7 %collective-permute-start.5 = (f32[288,128]{1,0:T(8,128)S(1)}, f32[288,128]{1,0:T(8,128)S(1)}, u32[]{:S(2)}, u32[]{:S(2)}) collective-permute-start(f32[288,128]{1,0:T(8,128)S(1)} %get-tuple-element.41), channel_id=1, source_target_pairs={{0,128},{1,129},{2,130},{3,131},{4,132},{5,133},{6,134},{7,135},{8... | collective-permute-start | bytes 442376 | tf_op jit(solution)/shard_map/ppermute | solution.py:456
  20.8 8.8 %collective-permute-start.6 = (f32[288,128]{1,0:T(8,128)S(1)}, f32[288,128]{1,0:T(8,128)S(1)}, u32[]{:S(2)}, u32[]{:S(2)}) collective-permute-start(f32[288,128]{1,0:T(8,128)S(1)} %get-tuple-element.42), channel_id=1, source_target_pairs={{0,64},{1,193},{2,66},{3,195},{4,68},{5,197},{6,70},{7,199},{8,72}... | collective-permute-start | bytes 442376 | tf_op jit(solution)/shard_map/ppermute | solution.py:456
  22.0 7.6 %collective-permute-start.7 = (f32[288,128]{1,0:T(8,128)S(1)}, f32[288,128]{1,0:T(8,128)S(1)}, u32[]{:S(2)}, u32[]{:S(2)}) collective-permute-start(f32[288,128]{1,0:T(8,128)S(1)} %get-tuple-element.43), channel_id=1, source_target_pairs={{0,192},{1,65},{2,194},{3,67},{4,196},{5,69},{6,198},{7,71},{8,200... | collective-permute-start | bytes 442376 | tf_op jit(solution)/shard_map/ppermute | solution.py:456
